TPU v7x, 32 devices: a whole 2x2x4 slice. The times are simulated.
32 devices in a mesh: mod: 2 (over x), dp: 16 (over z, y, core).
Axes of the slice: x: 2, y: 2, z: 4, core: 2. Of those that a mesh axis runs over, the one named last changes fastest.
Arguments:
- layer_rows: bfloat16 [2, 16384, 768], P('mod', 'dp'), may hold values from -6 to 6
- cotangent: bfloat16 [2, 16384, 768], P('mod', 'dp'), may hold values from -6 to 6
- row_live: int32 [2, 16384], P(None, 'dp'), may hold values from 0 to 1, as said below
- partner: int32 [16, 16], P('dp'), may hold values from 0 to 15, as said below
- w_qkv: bfloat16 [768, 2304], replicated, may hold values from -0.21875 to 0.21875
- b_qv: float32 [2, 768], replicated, may hold values from -1.8 to 1.8
- w_out: bfloat16 [768, 768], replicated, may hold values from -0.875 to 0.875
- norm_gains: float32 [2, 768], replicated, may hold values from 0.5 to 1.5
- bias_rows: float32 [4, 768], replicated, may hold values from -1.8 to 1.8
- w_in: bfloat16 [768, 3072], replicated, may hold values from -0.21875 to 0.21875
- b_in: float32 [3072], replicated, may hold values from -1.8 to 1.8
- w_back: bfloat16 [3072, 768], replicated, may hold values from -0.15625 to 0.15625
Outputs:
- output: bfloat16 [2, 16384, 768], P('mod', 'dp')
- grad_rows: bfloat16 [2, 16384, 768], P('mod', 'dp')
- grad_w_qkv: float32 [768, 2304], P('dp')
- grad_b_qv: float32 [2, 768], P(None, 'dp')
- grad_w_out: float32 [768, 768], P('dp')
- grad_gains: float32 [2, 768], P(None, 'dp')
- grad_biases: float32 [4, 768], P(None, 'dp')
- grad_w_in: float32 [768, 3072], P('dp')
- grad_b_in: float32 [3072], P('dp')
- grad_w_back: float32 [3072, 768], P('dp')
Inputs may be any that keep to these rules, and one draw needn't show every extreme that they name: `row_live`: within each pair and modality the live rows are the first ones of its 64 slots, at least one; the first pair of every index of dp is live in all its rows of both modalities. Each row partner[g] is a permutation of the 16 region slots of index g of dp.
All inputs are finite; a program needn't handle non-finite values.
Results may differ from a plain program's by a relative error of at most 0.015.
Values may be sent and summed in bfloat16 or wider, within the bound.
No kernel may reach another device: no remote copies, remote signals or barrier semaphores. Data moves between devices by JAX's collectives and lax.ppermute only.
A program may use at most 192 MiB of HBM per device.

v0:
```python
import functools

import jax
import jax.numpy as jnp
from jax import lax
from jax.experimental import pallas as pl
from jax.experimental.pallas import tpu as pltpu
from jax.sharding import PartitionSpec as P

HEADS = 12
EPSILON = 1e-12
F32 = jnp.float32
BF16 = jnp.bfloat16
VMEM_LIMIT = 255 * 2**18


def dot(left, right, left_dim=1, right_dim=0):
    return lax.dot_general(
        left, right, (((left_dim,), (right_dim,)), ((), ())), preferred_element_type=F32
    )


def flipped(value, axis, mask):
    pairs = [(source, source ^ mask) for source in range(lax.axis_size(axis))]
    return lax.ppermute(value, axis, pairs)


def params(limit=VMEM_LIMIT):
    return pltpu.CompilerParams(vmem_limit_bytes=limit)


def kept_slot(scalars, pair, half):
    groups = 2 * half
    side = scalars[groups]
    place = side * half + pair
    return jnp.where(side == 0, place, scalars[place])


def sent_slot(scalars, pair, half):
    groups = 2 * half
    side = scalars[groups]
    place = (1 - side) * half + pair
    return jnp.where(side == 0, place, scalars[place])


ANY = pl.BlockSpec(memory_space=pl.ANY)
LINE = []


def call(kernel, scalars, operands, in_specs, out_specs, out_shape, grid, name, **more):
    after = list(LINE)
    into = list(more.get("into", ()))
    into_first = more.get("into_first", 0)
    scratch = list(more.get("scratch", ()))
    taken, spare, given = len(operands), len(into) + len(after), len(out_shape)

    def wrapped(scalars_ref, *refs):
        outs = refs[taken + spare :]
        kernel(scalars_ref, *refs[:taken], *outs[:given], *outs[given + 1 :])

    outs = pl.pallas_call(
        wrapped,
        grid_spec=pltpu.PrefetchScalarGridSpec(
            num_scalar_prefetch=1,
            grid=grid,
            in_specs=list(in_specs) + [ANY] * spare,
            out_specs=list(out_specs) + [ANY],
            scratch_shapes=scratch,
        ),
        out_shape=list(out_shape) + [jax.ShapeDtypeStruct((8, 128), F32)],
        input_output_aliases={1 + taken + i: i + into_first for i in range(len(into))},
        compiler_params=params(more.get("limit", VMEM_LIMIT)),
        cost_estimate=pl.CostEstimate(
            flops=more.get("work", 4 * 10**9), bytes_accessed=2**20, transcendentals=0
        ),
        name=name,
    )(scalars, *operands, *into, *after)
    LINE[:] = [outs[-1]]
    return list(outs[:-1])


def gather_sent(partner, rows, half, first, count):
    slot_rows, width = rows.shape[1:]

    def kernel(partner_ref, rows_ref, out, sems):
        side = lax.axis_index("mod")
        copies = []
        for i in range(count):
            place = (1 - side) * half + first + i
            slot = jnp.where(side == 0, place, partner_ref[place])
            copies.append(pltpu.make_async_copy(rows_ref.at[slot], out.at[i], sems.at[i]))
        for copy in copies:
            copy.start()
        for copy in copies:
            copy.wait()

    shape = (count, slot_rows, width)
    return call(
        kernel,
        partner,
        [rows],
        [ANY],
        [pl.BlockSpec(shape, lambda i, s: (0, 0, 0))],
        [jax.ShapeDtypeStruct(shape, rows.dtype)],
        (1,),
        "gather_sent",
        work=5 * 10**8,
        scratch=[pltpu.SemaphoreType.DMA((count,))],
    )[0]


def scatter_home(scalars, kept, back, half):
    slot_rows, width = kept.shape[1:]

    def kernel(scalars_ref, kept_ref, back_ref, out, sems):
        copies = []
        for i in range(half):
            copies.append(
                pltpu.make_async_copy(
                    kept_ref.at[i], out.at[kept_slot(scalars_ref, i, half)], sems.at[0, i]
                )
            )
            copies.append(
                pltpu.make_async_copy(
                    back_ref.at[i], out.at[sent_slot(scalars_ref, i, half)], sems.at[1, i]
                )
            )
        for copy in copies:
            copy.start()
        for copy in copies:
            copy.wait()

    shape = (2 * half, slot_rows, width)
    return call(
        kernel,
        scalars,
        [kept, back],
        [ANY, ANY],
        [pl.BlockSpec(shape, lambda i, s: (0, 0, 0))],
        [jax.ShapeDtypeStruct(shape, kept.dtype)],
        (1,),
        "scatter_home",
        work=2 * 10**10,
        scratch=[pltpu.SemaphoreType.DMA((2, half))],
    )[0]


def parts_of(blocks):
    early = 2 * blocks // 3
    return (0, early), (early, blocks - early)


def split_heads(value):
    low = lax.broadcasted_iota(jnp.int32, value.shape, 1) < value.shape[1] // 2
    zero = jnp.zeros_like(value)
    return jnp.concatenate([jnp.where(low, value, zero), jnp.where(low, zero, value)], 0)


def side_by_side(value):
    rows = value.shape[0] // 2
    return jnp.concatenate([value[:rows], value[rows:]], 1)


def row_sum(value):
    return jnp.sum(value, axis=0, keepdims=True)


def normal_form(value):
    centered = value - jnp.mean(value, axis=-1, keepdims=True)
    root = lax.rsqrt(jnp.mean(centered * centered, axis=-1, keepdims=True) + EPSILON)
    return centered * root, root


def normal_back(lifted, normed, root):
    return root * (
        lifted
        - jnp.mean(lifted, axis=-1, keepdims=True)
        - normed * jnp.mean(lifted * normed, axis=-1, keepdims=True)
    )


def whole(array):
    return pl.BlockSpec(
        array.shape, lambda *_: (0,) * array.ndim, pipeline_mode=pl.Buffered(1)
    )


def attention_forward(scalars, rows, received, live, weights):
    w_qkv, b_qv, w_out, norm_gains, bias_rows = weights
    slot_rows, width = rows.shape[1:]
    pairs = half = rows.shape[0] // 2
    turn = received[0].shape[0] // 2
    length = 2 * slot_rows
    duo = 2 * width // HEADS
    blocks = width // duo
    score_scale = (width // HEADS) ** (-0.5)

    def kernel(
        scalars_ref,
        kept_a,
        kept_b,
        got_a,
        got_b,
        live_ref,
        w_qkv_ref,
        b_qv_ref,
        w_out_ref,
        gains_ref,
        biases_ref,
        joined_out,
        mixed_out,
        probs_out,
        context_out,
        normed_out,
        root_out,
    ):
        got = jnp.where(pl.program_id(0) < turn, got_a[...], got_b[...])
        joined = jnp.concatenate([kept_a[0], got[0], kept_b[0], got[1]], 0)
        joined_out[...] = joined
        mixed = dot(joined, w_qkv_ref[...])
        queries = (mixed[:, :width] + b_qv_ref[0:1, :]).astype(BF16)
        queries = (queries.astype(F32) * score_scale).astype(BF16)
        keys = mixed[:, width : 2 * width].astype(BF16)
        values = (mixed[:, 2 * width :] + b_qv_ref[1:2, :]).astype(BF16)
        for first_block, count in parts_of(blocks):
            cols = slice(first_block * duo, (first_block + count) * duo)
            at = 3 * first_block * duo
            for value in (queries, keys, values):
                mixed_out[:, at : at + count * duo] = value[:, cols]
                at += count * duo
        contexts = []
        for pair in range(2):
            seen = live_ref[pair] > 0
            span = slice(pair * length, (pair + 1) * length)
            heads = []
            for block in range(blocks):
                cols = slice(block * duo, (block + 1) * duo)
                scores = dot(split_heads(queries[span, cols]), keys[span, cols], 1, 1)
                scores = jnp.where(seen, scores, -1e30)
                powered = jnp.exp(scores - jnp.max(scores, axis=-1, keepdims=True))
                low_probs = powered * (1.0 / jnp.sum(powered, axis=-1, keepdims=True))
                low_probs = low_probs.astype(BF16)
                probs_out[pair, block] = low_probs
                heads.append(
                    dot(side_by_side(low_probs), split_heads(values[span, cols])).astype(BF16)
                )
            contexts.append(jnp.concatenate(heads, 1))
        context = jnp.concatenate(contexts, 0)
        context_out[...] = context
        pre_one = joined.astype(F32) + dot(context, w_out_ref[...]) + biases_ref[0:1, :]
        normed, root = normal_form(pre_one)
        normed_out[...] = normed.astype(BF16)
        root_out[...] = jnp.broadcast_to(root, root_out.shape)

    def by_rows(columns):
        return pl.BlockSpec((2 * length, columns), lambda i, s: (i, 0))

    slot = (1, slot_rows, width)
    two = (2, slot_rows, width)
    total = half * length
    return call(
        kernel,
        scalars,
        [rows, rows, *received, live, w_qkv, b_qv, w_out, norm_gains, bias_rows],
        [
            pl.BlockSpec(slot, lambda i, s: (kept_slot(s, 2 * i, half), 0, 0)),
            pl.BlockSpec(slot, lambda i, s: (kept_slot(s, 2 * i + 1, half), 0, 0)),
            pl.BlockSpec(two, lambda i, s: (jnp.minimum(i, turn - 1), 0, 0)),
            pl.BlockSpec(two, lambda i, s: (jnp.maximum(i - turn, 0), 0, 0)),
            pl.BlockSpec((2, 1, length), lambda i, s: (i, 0, 0)),
            whole(w_qkv),
            whole(b_qv),
            whole(w_out),
            whole(norm_gains),
            whole(bias_rows),
        ],
        [
            by_rows(width),
            by_rows(3 * width),
            pl.BlockSpec((2, blocks, 2 * length, length), lambda i, s: (i, 0, 0, 0)),
            by_rows(width),
            by_rows(width),
            by_rows(128),
        ],
        [
            jax.ShapeDtypeStruct((total, width), BF16),
            jax.ShapeDtypeStruct((total, 3 * width), BF16),
            jax.ShapeDtypeStruct((half, blocks, 2 * length, length), BF16),
            jax.ShapeDtypeStruct((total, width), BF16),
            jax.ShapeDtypeStruct((total, width), BF16),
            jax.ShapeDtypeStruct((total, 128), F32),
        ],
        (pairs // 2,),
        "attention_forward",
        work=4 * 10**10,
    )


def place_of(index, order):
    return sum(1 << bit for n, bit in enumerate(order) if index >> (len(order) - 1 - n) & 1)


def spread(grad, outs, scalars_ref, base, shard, order):
    core, place = scalars_ref[base + 1], scalars_ref[base + 2]
    for j in range(2 ** len(order)):
        row = (place ^ place_of(j, order)) * 2
        for out, which in zip(outs, (1 - core, core)):
            out[j] = grad[pl.ds(pl.multiple_of((row + which) * shard, 16), shard), :]


def feed_forward(scalars, normed, cot, far_cot, weights, half, shards, base):
    w_in, b_in, w_back, norm_gains, bias_rows = weights
    slot_rows, width = cot.shape[1:]
    inner_width = w_in.shape[1]
    length = 2 * slot_rows
    rows = 2 * length
    height = half * length
    steps = half // 2
    chunk = 768
    chunks = inner_width // chunk
    shard = inner_width // shards
    places = shards // 2
    part = 4 * shard
    parts = inner_width // part

    def kernel(
        scalars_ref,
        normed_ref,
        cot_a,
        cot_b,
        cot_far,
        w_in_hbm,
        b_in_ref,
        w_back_hbm,
        gains_ref,
        biases_ref,
        slope_out,
        branch_out,
        kept_out,
        far_out,
        sums_out,
        send,
        keep,
        w_in_ref,
        w_back_ref,
        held,
        acts,
        branches,
        grad,
        sems,
    ):
        step = pl.program_id(0)

        def fetch_in(j):
            cols = pl.ds(j * chunk, chunk)
            return pltpu.make_async_copy(
                w_in_hbm.at[:, cols], w_in_ref.at[:, cols], sems.at[0, j]
            )

        def fetch_back(j):
            cols = pl.ds(j * chunk, chunk)
            return pltpu.make_async_copy(w_back_hbm.at[cols], w_back_ref.at[cols], sems.at[1, j])

        @pl.when(step == 0)
        def _():
            sums_out[...] = jnp.zeros_like(sums_out)
            for j in range(chunks):
                fetch_in(j).start()
                fetch_back(j).start()

        def close(pre_two, row):
            scaled, root = normal_form(pre_two)
            output = (scaled * gains_ref[1:2, :] + biases_ref[3:4, :]).astype(BF16)
            for i in range(2):
                kept_out[i] = output[i * length : i * length + slot_rows]
                far_out[i] = output[i * length + slot_rows : (i + 1) * length]
            here = jnp.concatenate([cot_a[0], cot_far[0], cot_b[0], cot_far[1]], 0).astype(F32)
            d_two = normal_back(here * gains_ref[1:2, :], scaled, root)
            low = d_two.astype(BF16)
            branch_out[...] = low
            branches[pl.ds(row, rows)] = low
            return jnp.concatenate([row_sum(here * scaled), row_sum(here), row_sum(d_two)], 0)

        def forward(first):
            hidden = normed_ref[...].astype(F32) * gains_ref[0:1, :] + biases_ref[1:2, :]
            low_hidden = hidden.astype(BF16)
            total = hidden + biases_ref[2:3, :]
            for j in range(chunks):
                cols = slice(j * chunk, (j + 1) * chunk)
                if first:
                    fetch_in(j).wait()
                inner = dot(low_hidden, w_in_ref[:, cols]) + b_in_ref[:, cols]
                normal = 0.5 + 0.5 * lax.erf(inner * (0.5**0.5))
                low_act = (inner * normal).astype(BF16)
                density = jnp.exp(inner * inner * -0.5) * 0.3989422804014327
                acts[pl.ds(step * rows, rows), cols] = low_act
                slope_out[:, cols] = (normal + inner * density).astype(BF16)
                if first:
                    fetch_back(j).wait()
                total = total + dot(low_act, w_back_ref[cols, :])
            return total

        @pl.when(step == 0)
        def _():
            held[...] = forward(True)

        @pl.when((step > 0) & (step < steps))
        def _():
            before = held[...]
            held[...] = forward(False)
            sums_out[0:3, :] += close(before, (step - 1) * rows)

        @pl.when(step == steps)
        def _():
            sums_out[0:3, :] += close(held[...], (step - 1) * rows)

        @pl.when(step >= steps)
        def _():
            start = pl.multiple_of((step - steps) * part, 128)
            grad[...] = dot(acts[:, pl.ds(start, part)], branches[...], 0, 0).astype(BF16)
            core, low = scalars_ref[base + 1], scalars_ref[base + 2] & 1
            for j in range(2):
                for out, which in ((send, 1 - core), (keep, core)):
                    row = ((low ^ j) * 2 + which) * shard
                    out[j, 0] = grad[pl.ds(pl.multiple_of(row, 16), shard), :]

    def ahead(i):
        return jnp.minimum(i, steps - 1)

    def behind(i):
        return jnp.clip(i - 1, 0, steps - 1)

    def slot(j):
        return pl.BlockSpec(
            (1, slot_rows, width), lambda i, s: (kept_slot(s, 2 * behind(i) + j, half), 0, 0)
        )

    duo = pl.BlockSpec((2, slot_rows, width), lambda i, s: (behind(i), 0, 0))

    def entry(i, s):
        apart = (s[base + 2] >> 1) ^ jnp.maximum(i - steps, 0)
        return 0, (apart & 1) * 2 + (apart >> 1), 0, 0

    grads = pl.BlockSpec((2, 1, shard, width), entry)
    return call(
        kernel,
        scalars,
        [normed, cot, cot, far_cot, w_in, b_in, w_back, norm_gains, bias_rows],
        [
            pl.BlockSpec((rows, width), lambda i, s: (ahead(i), 0)),
            slot(0),
            slot(1),
            duo,
            ANY,
            whole(b_in),
            ANY,
            whole(norm_gains),
            whole(bias_rows),
        ],
        [
            pl.BlockSpec((rows, inner_width), lambda i, s: (ahead(i), 0)),
            pl.BlockSpec((rows, width), lambda i, s: (behind(i), 0)),
            duo,
            duo,
            pl.BlockSpec((8, width), lambda i, s: (0, 0)),
            grads,
            grads,
        ],
        [
            jax.ShapeDtypeStruct((height, inner_width), BF16),
            jax.ShapeDtypeStruct((height, width), BF16),
            jax.ShapeDtypeStruct((half, slot_rows, width), BF16),
            jax.ShapeDtypeStruct((half, slot_rows, width), BF16),
            jax.ShapeDtypeStruct((8, width), F32),
            jax.ShapeDtypeStruct((2, places // 2, shard, width), BF16),
            jax.ShapeDtypeStruct((2, places // 2, shard, width), BF16),
        ],
        (steps + parts,),
        "feed_forward",
        scratch=[
            pltpu.VMEM((width, inner_width), BF16),
            pltpu.VMEM((inner_width, width), BF16),
            pltpu.VMEM((rows, width), F32),
            pltpu.VMEM((height, inner_width), BF16),
            pltpu.VMEM((height, width), BF16),
            pltpu.VMEM((part, width), BF16),
            pltpu.SemaphoreType.DMA((2, chunks)),
        ],
    )


def feed_backward(scalars, branch, slope, normed, root, context, weights, shards, base, orders):
    w_in, w_back, norm_gains, bias_rows = weights
    total, width = branch.shape
    inner_width = slope.shape[1]
    chunk = 768
    steps = inner_width // chunk
    turn = steps // 2
    shard = width // shards
    places = shards // 2
    piece = 128

    def kernel(
        scalars_ref,
        branch_ref,
        slope_ref,
        normed_ref,
        root_ref,
        context_ref,
        w_in_ref,
        w_back_ref,
        gains_ref,
        biases_ref,
        low_attn_out,
        sums_out,
        inner_sum_out,
        send_a,
        keep_a,
        send_b,
        keep_b,
        held,
        low_hidden,
        grad,
    ):
        step = pl.program_id(0)

        @pl.when(step == 0)
        def _():
            hidden = normed_ref[...].astype(F32) * gains_ref[0:1, :] + biases_ref[1:2, :]
            low_hidden[...] = hidden.astype(BF16)
            held[...] = branch_ref[...].astype(F32)

        @pl.when(step < steps)
        def _():
            sums = jnp.zeros((1, chunk), F32)
            lows = []
            for r in range(0, total, 256):
                span = slice(r, r + 256)
                d_inner = dot(branch_ref[span], w_back_ref[...], 1, 1)
                d_inner = d_inner * slope_ref[span].astype(F32)
                sums = sums + row_sum(d_inner)
                low = d_inner.astype(BF16)
                lows.append(low)
                held[span] += dot(low, w_in_ref[...], 1, 1)
            inner_sum_out[...] = jnp.broadcast_to(sums, inner_sum_out.shape)
            grad[...] = dot(low_hidden[...], jnp.concatenate(lows, 0), 0, 0).astype(BF16)

        @pl.when(step == steps)
        def _():
            sums = [jnp.zeros((1, width), F32)] * 3
            lows = []
            for i in range(total // piece):
                span = slice(i * piece, (i + 1) * piece)
                d_hidden, scaled = held[span], normed_ref[span].astype(F32)
                d_one = normal_back(d_hidden * gains_ref[0:1, :], scaled, root_ref[span, 0:1])
                lows.append(d_one.astype(BF16))
                low_attn_out[span] = lows[-1]
                for j, term in enumerate((d_hidden * scaled, d_hidden, d_one)):
                    sums[j] = sums[j] + row_sum(term)
            sums_out[...] = jnp.concatenate(sums + [jnp.zeros((5, width), F32)], 0)
            grad[...] = dot(context_ref[...], jnp.concatenate(lows, 0), 0, 0).astype(BF16)

        @pl.when(step < turn)
        def _():
            spread(grad, (send_a, keep_a), scalars_ref, base, shard, orders[0])

        @pl.when(step >= turn)
        def _():
            spread(grad, (send_b, keep_b), scalars_ref, base, shard, orders[1])

    def now(i):
        return jnp.minimum(i, steps - 1)

    half_a = pl.BlockSpec((places, shard, chunk), lambda i, s: (0, 0, jnp.minimum(i, turn - 1)))
    half_b = pl.BlockSpec((places, shard, chunk), lambda i, s: (0, 0, jnp.maximum(i - turn, 0)))
    shape_a = jax.ShapeDtypeStruct((places, shard, turn * chunk), BF16)
    shape_b = jax.ShapeDtypeStruct((places, shard, (steps + 1 - turn) * chunk), BF16)
    return call(
        kernel,
        scalars,
        [branch, slope, normed, root, context, w_in, w_back, norm_gains, bias_rows],
        [
            whole(branch),
            pl.BlockSpec((total, chunk), lambda i, s: (0, now(i))),
            whole(normed),
            whole(root),
            whole(context),
            pl.BlockSpec((width, chunk), lambda i, s: (0, now(i))),
            pl.BlockSpec((chunk, width), lambda i, s: (now(i), 0)),
            whole(norm_gains),
            whole(bias_rows),
        ],
        [
            pl.BlockSpec((total, width), lambda i, s: (0, 0)),
            pl.BlockSpec((8, width), lambda i, s: (0, 0)),
            pl.BlockSpec((8, chunk), lambda i, s: (0, now(i))),
            half_a,
            half_a,
            half_b,
            half_b,
        ],
        [
            jax.ShapeDtypeStruct((total, width), BF16),
            jax.ShapeDtypeStruct((8, width), F32),
            jax.ShapeDtypeStruct((8, inner_width), F32),
            shape_a,
            shape_a,
            shape_b,
            shape_b,
        ],
        (steps + 1,),
        "feed_backward",
        scratch=[
            pltpu.VMEM((total, width), F32),
            pltpu.VMEM((total, width), BF16),
            pltpu.VMEM((width, chunk), BF16),
        ],
    )


def attention_backward(scalars, kept, weights, part, shards, base, order, earlier=(), sums=()):
    low_attn, mixed, probs, joined = kept
    w_out, w_qkv = weights
    total, width = low_attn.shape
    pairs, blocks, _, length = probs.shape
    duo = width // blocks
    first_block, mine = parts_of(blocks)[part]
    span_cols = mine * duo
    slot_rows = length // 2
    score_scale = (width // HEADS) ** (-0.5)
    steps = pairs // 2
    shard = width // shards
    places = shards // 2
    last = part == 1
    columns = 3 * span_cols + (128 if last else 0)

    def kernel(
        scalars_ref,
        low_attn_ref,
        mixed_ref,
        probs_ref,
        joined_ref,
        w_out_ref,
        *refs,
    ):
        if last:
            w_qkv_ref, earlier_ref, one, two, inner, sums_ref = refs[:6]
            kept_out, far_out, sums_out, send, keep, held, grad = refs[6:]
        else:
            d_mixed_out, sums_out, send, keep, held, grad = refs
        step = pl.program_id(0)

        @pl.when(step == 0)
        def _():
            sums_out[...] = jnp.zeros_like(sums_out)

        d_context = dot(low_attn_ref[...], w_out_ref[...], 1, 1).astype(BF16)
        rows = []
        for pair in range(2):
            span = slice(pair * length, (pair + 1) * length)
            d_heads, d_probs, d_scores = [], [], []
            for block in range(mine):
                cols = slice(block * duo, (block + 1) * duo)
                values = mixed_ref[span, 2 * span_cols + block * duo : 2 * span_cols + (block + 1) * duo]
                d_heads.append(split_heads(d_context[span, cols]))
                d_probs.append(dot(d_heads[block], values, 1, 1))
            for block in range(mine):
                wide = probs_ref[pair, block].astype(F32)
                mean = jnp.sum(wide * d_probs[block], axis=-1, keepdims=True)
                d_scores.append((wide * (d_probs[block] - mean)).astype(BF16))
            d_queries, d_keys, d_values = [], [], []
            for block in range(mine):
                cols = slice(block * duo, (block + 1) * duo)
                queries = split_heads(mixed_ref[span, cols])
                keys = mixed_ref[span, span_cols + block * duo : span_cols + (block + 1) * duo]
                keys = split_heads(keys)
                scaled = dot(side_by_side(d_scores[block]), keys) * score_scale
                d_queries.append(scaled.astype(BF16))
                d_keys.append(dot(d_scores[block], queries, 0, 0).astype(BF16))
                d_values.append(dot(probs_ref[pair, block], d_heads[block], 0, 0).astype(BF16))
            rows.append(jnp.concatenate(d_queries + d_keys + d_values, 1))
        d_mixed = jnp.concatenate(rows, 0)
        held[pl.ds(pl.multiple_of(step * 2 * length, 2 * length), 2 * length)] = d_mixed
        sums_out[0:1, :] += row_sum(d_mixed[:, :span_cols].astype(F32))
        sums_out[1:2, :] += row_sum(d_mixed[:, 2 * span_cols :].astype(F32))
        if last:
            d_rows = low_attn_ref[...].astype(F32)
            for third in range(3):
                before = earlier_ref.shape[1] // 3
                before = earlier_ref[:, third * before : (third + 1) * before]
                full = d_mixed[:, third * span_cols : (third + 1) * span_cols]
                full = jnp.concatenate([before, full], 1)
                d_rows = d_rows + dot(full, w_qkv_ref[:, third * width : (third + 1) * width], 1, 1)
            d_rows = d_rows.astype(BF16)
            for i in range(2):
                kept_out[i] = d_rows[i * length : i * length + slot_rows]
                far_out[i] = d_rows[i * length + slot_rows : (i + 1) * length]
        else:
            d_mixed_out[...] = d_mixed

        @pl.when(step == steps - 1)
        def _():
            grad[:, : 3 * span_cols] = dot(joined_ref[...], held[...], 0, 0).astype(BF16)
            if last:
                first, second = sums_ref[0:2, :], sums_out[0:2, :]
                small = [jnp.concatenate([first, second], 1), one[0:1], two[0:1]]
                small += [one[2:3], one[1:2], two[2:3], two[1:2], inner[...]]
                small.append(jnp.zeros((120 - inner.shape[0], width), F32))
                grad[:, 3 * span_cols :] = jnp.concatenate(small, 0).T.astype(BF16)
            spread(grad, (send, keep), scalars_ref, base, shard, order)

    def by_rows(count, at=0):
        return pl.BlockSpec((2 * length, count), lambda i, s: (i, at))

    two_slots = pl.BlockSpec((2, slot_rows, width), lambda i, s: (i, 0, 0))
    operands = [low_attn, mixed, probs, joined, w_out]
    in_specs = [
        by_rows(width),
        by_rows(3 * span_cols, first_block // mine),
        pl.BlockSpec((2, mine, 2 * length, length), lambda i, s: (i, first_block // mine, 0, 0)),
        whole(joined),
        pl.BlockSpec(
            (span_cols, width), lambda i, s: (first_block // mine, 0), pipeline_mode=pl.Buffered(1)
        ),
    ]
    grads = pl.BlockSpec((places, shard, columns), lambda i, s: (0, 0, 0))
    out_specs = [pl.BlockSpec((8, span_cols), lambda i, s: (0, 0)), grads, grads]
    out_shape = [
        jax.ShapeDtypeStruct((8, span_cols), F32),
        jax.ShapeDtypeStruct((places, shard, columns), BF16),
        jax.ShapeDtypeStruct((places, shard, columns), BF16),
    ]
    if last:
        operands += [w_qkv, earlier, *sums]
        in_specs += [whole(w_qkv), by_rows(earlier.shape[1])]
        in_specs += [whole(each) for each in sums]
        out_specs = [two_slots, two_slots] + out_specs
        out_shape = [jax.ShapeDtypeStruct((pairs, slot_rows, width), BF16)] * 2 + out_shape
    else:
        out_specs = [by_rows(3 * span_cols)] + out_specs
        out_shape = [jax.ShapeDtypeStruct((total, 3 * span_cols), BF16)] + out_shape
    return call(
        kernel,
        scalars,
        operands,
        in_specs,
        out_specs,
        out_shape,
        (steps,),
        "attention_backward",
        scratch=[
            pltpu.VMEM((total, 3 * span_cols), BF16),
            pltpu.VMEM((width, columns), BF16),
        ],
    )


def in_turn(value):
    value, *rest = lax.optimization_barrier((value, *LINE))
    LINE[:] = rest[:1]
    return value


def pause(scalars):
    def kernel(scalars_ref):
        del scalars_ref

    call(kernel, scalars, [], [], [], [], (1,), "pause", work=2 * 10**10)


class Shards:
    def __init__(self, send, keep, order):
        shard, width = send.shape[-2:]
        self.order = list(order)
        shape = (2 ** len(self.order), shard, width)
        self.held = [keep.reshape(shape)]
        self.coming = flipped(send, "dp", 1).reshape(shape)

    def step(self):
        self.held.append(in_turn(self.coming))
        count = self.coming.shape[0]
        first = count // 2 if self.order else 0
        total = None
        for array in self.held:
            array = lax.slice_in_dim(array, first, count, axis=0).astype(F32)
            total = array if total is None else total + array
        total = total.astype(BF16)
        if self.order:
            self.coming = flipped(total, "dp", 2 << self.order.pop(0))
        else:
            self.mine = lax.optimization_barrier(total[0])
            self.coming = flipped(self.mine, "mod", 1)
        LINE.append(total)

    def result(self):
        return self.mine.astype(F32) + in_turn(self.coming).astype(F32)


def finish_qkv(scalars, early, late, width, count):
    shard = early.mine.shape[0]
    widths = (early.mine.shape[1] // 3, (late.mine.shape[1] - 128) // 3)

    def kernel(scalars_ref, mine_a, coming_a, mine_b, coming_b, qkv, b_qv, gains, biases, inner):
        parts = [
            mine[...].astype(F32) + coming[...].astype(F32)
            for mine, coming in ((mine_a, coming_a), (mine_b, coming_b))
        ]
        at = 0
        for third in range(3):
            for part, columns in zip(parts, widths):
                qkv[:, at : at + columns] = part[:, third * columns : (third + 1) * columns]
                at += columns
        small = jnp.concatenate([parts[1][:, 3 * widths[1] :], jnp.zeros((128 - shard, 128), F32)], 0)
        small = small.T[:, :shard]
        b_qv[...] = small[0:2]
        gains[...] = small[2:4]
        biases[...] = small[4:8]
        inner[...] = small[8 : 8 + count]

    operands = [early.mine, early.coming, late.mine, late.coming]
    shapes = ((shard, 3 * width), (2, shard), (2, shard), (4, shard), (count, shard))
    return call(
        kernel,
        scalars,
        operands,
        [whole(array) for array in operands],
        [pl.BlockSpec(shape, lambda i, s: (0, 0)) for shape in shapes],
        [jax.ShapeDtypeStruct(shape, F32) for shape in shapes],
        (1,),
        "finish_qkv",
    )


def reduce_plain(send, keep, order):
    shard, columns = send.shape[-2:]
    total = jnp.stack([keep.reshape(-1, shard, columns), send.reshape(-1, shard, columns)], 1)
    places = [place_of(j, order) for j in range(total.shape[0])]
    total = jnp.stack([total[places.index(j)] for j in range(total.shape[0])])
    total = total.reshape(-1, columns).astype(F32)
    share = lax.psum_scatter(total, "dp", scatter_dimension=0, tiled=True)
    return lax.psum(share.astype(BF16), "mod").astype(F32)


def body(
    layer_rows,
    cotangent,
    row_live,
    partner,
    w_qkv,
    b_qv,
    w_out,
    norm_gains,
    bias_rows,
    w_in,
    b_in,
    w_back,
):
    side = lax.axis_index("mod")
    place = lax.axis_index("dp")
    shards = lax.axis_size("dp")
    groups = partner.shape[1]
    aligned = shards == 16 and (layer_rows.shape[2] // shards) % 16 == 0
    layout = shards if aligned else 16
    half = groups // 2
    width = layer_rows.shape[2]
    slot_rows = layer_rows.shape[1] // groups
    inner_width = w_in.shape[1]
    slots = (groups, slot_rows, width)
    rows = layer_rows[0].reshape(slots)
    cot = cotangent[0].reshape(slots)
    spot = place if aligned else 0 * place
    scalars = jnp.concatenate(
        [partner[0], jnp.stack([side, spot & 1, spot >> 1]).astype(jnp.int32)]
    )
    cut = half // 2
    LINE.clear()
    sent = gather_sent(partner[0], rows, half, 0, cut)
    got_a = flipped(sent, "mod", 1)
    sent = gather_sent(partner[0], rows, half, cut, half - cut)
    got_b = flipped(sent, "mod", 1)
    sent_cot = gather_sent(partner[0], cot, half, 0, half)
    got_a, sent_cot = lax.optimization_barrier((got_a, sent_cot))
    far_cot = flipped(sent_cot, "mod", 1)

    live = row_live.reshape(2, groups, slot_rows)
    words_live = lax.dynamic_slice_in_dim(live[0], side * half, half, 0)
    region_live = live[1][lax.dynamic_slice_in_dim(partner[0], side * half, half, 0)]
    is_first = side == 0
    seen = jnp.concatenate(
        [
            jnp.where(is_first, words_live, region_live),
            jnp.where(is_first, region_live, words_live),
        ],
        1,
    )[:, None, :]

    heads_weights = (w_qkv, b_qv, w_out, norm_gains, bias_rows)
    joined, mixed, probs, context, normed, root = attention_forward(
        scalars, rows, (got_a, got_b), seen, heads_weights
    )
    feed_weights = (w_in, b_in.reshape(1, inner_width), w_back, norm_gains, bias_rows)
    slope, branch, out_kept, out_far, sums_two, *back = feed_forward(
        scalars, normed, cot, far_cot, feed_weights, half, layout, groups
    )
    out_back = flipped(out_far, "mod", 1)
    back_weights = (w_in, w_back, norm_gains, bias_rows)
    attn_weights = (w_out, w_qkv)
    path, other = (0, 1, 2), (1, 0, 2)
    if aligned:
        back = Shards(*back, path)
        back.step()
    low_attn, sums_one, inner_sum, *inner = feed_backward(
        scalars,
        branch,
        slope,
        normed,
        root,
        context,
        back_weights,
        layout,
        groups,
        (other, path),
    )
    shard = width // shards
    count = inner_width // width
    inner_sum = inner_sum[0].reshape(shards, count, shard).transpose(1, 0, 2).reshape(count, width)
    if aligned:
        back.step()
        out_back = in_turn(out_back)
        pause(scalars)
        inner_a, inner_b = Shards(*inner[:2], other), Shards(*inner[2:], path)
        inner_a.step()
        inner_b.step()
    attn_kept = (low_attn, mixed, probs, joined)
    d_mixed, sums_qv, *qkv_a = attention_backward(
        scalars, attn_kept, attn_weights, 0, layout, groups, path
    )
    if aligned:
        back.step()
        inner_a.step()
        inner_b.step()
        pause(scalars)
        qkv_a = Shards(*qkv_a, path)
        qkv_a.step()
    sums = (sums_one, sums_two, inner_sum, sums_qv)
    d_kept, d_far, _, *qkv_b = attention_backward(
        scalars, attn_kept, attn_weights, 1, layout, groups, path, d_mixed, sums
    )
    d_back = flipped(d_far, "mod", 1)
    if aligned:
        qkv_b = Shards(*qkv_b, path)
        inner_b.step()
        qkv_b.step()
        qkv_a.step()
        inner_a.step()
        back.step()
        out_rows = scatter_home(scalars, out_kept, out_back, half).reshape(1, -1, width)
        qkv_b.step()
        qkv_a.step()
        inner_b.step()
        qkv_b.step()
        inner_a.step()
        grad_back = back.result()
        grad_rows = scatter_home(scalars, d_kept, d_back, half).reshape(1, -1, width)
        qkv_a.step()
        qkv_b.step()
        inner_a, inner_b = inner_a.result(), inner_b.result()
        grad_qkv, *small = finish_qkv(scalars, qkv_a, qkv_b, width, count)
    else:
        out_rows = scatter_home(scalars, out_kept, out_back, half).reshape(1, -1, width)
        grad_back = reduce_plain(*back, path)
        inner_a, inner_b = reduce_plain(*inner[:2], other), reduce_plain(*inner[2:], path)
        qkv_a, qkv_b = reduce_plain(*qkv_a, path), reduce_plain(*qkv_b, path)
        grad_rows = scatter_home(scalars, d_kept, d_back, half).reshape(1, -1, width)
        columns = (qkv_a.shape[1] // 3, (qkv_b.shape[1] - 128) // 3)
        thirds = []
        for third in range(3):
            for part, wide in zip((qkv_a, qkv_b), columns):
                thirds.append(part[:, third * wide : (third + 1) * wide])
        grad_qkv = jnp.concatenate(thirds, 1)
        small = qkv_b[:, 3 * columns[1] :].T
        small = small[0:2], small[2:4], small[4:8], small[8 : 8 + count]
    turn = inner_width - inner_a.shape[1]
    return (
        out_rows,
        grad_rows,
        grad_qkv,
        small[0],
        inner_b[:, turn:],
        small[1],
        small[2],
        jnp.concatenate([inner_a, inner_b[:, :turn]], 1),
        small[3].reshape(-1),
        grad_back,
    )


def solution(mesh):
    return jax.shard_map(
        body,
        mesh=mesh,
        in_specs=(
            P("mod", "dp", None),
            P("mod", "dp", None),
            P(None, "dp"),
            P("dp", None),
            P(),
            P(),
            P(),
            P(),
            P(),
            P(),
            P(),
            P(),
        ),
        out_specs=(
            P("mod", "dp", None),
            P("mod", "dp", None),
            P("dp", None),
            P(None, "dp"),
            P("dp", None),
            P(None, "dp"),
            P(None, "dp"),
            P("dp", None),
            P("dp"),
            P("dp", None),
        ),
        check_vma=False,
    )
```

profile of v0, /device:TPU:0, one launch (start us, length us, event | category | flops | bytes accessed | tf_op | source)
XLA Modules:
  0.0 230.3 jit_solution(15319213018146242543)
XLA Ops:
  0.7 2.6 %gather_sent.3 = (bf16[4,64,768]{2,1,0:T(8,128)(2,1)}, f32[8,128]{1,0:T(8,128)}) custom-call(s32[16]{0:T(128)} %bitcast.48, bf16[16,64,768]{2,1,0:T(8,128)(2,1)} %bitcast.52), custom_call_target="tpu_custom_call" | custom-call | flops 500000000 | bytes 1048576 | tf_op jit(solution)/shard_map/gather_sent/pallas_call | solution.py:61
  3.3 2.5 %gather_sent.4 = (bf16[4,64,768]{2,1,0:T(8,128)(2,1)}, f32[8,128]{1,0:T(8,128)}) custom-call(s32[16]{0:T(128)} %bitcast.49, bf16[16,64,768]{2,1,0:T(8,128)(2,1)} %bitcast.53, f32[8,128]{1,0:T(8,128)} %get-tuple-element.109.refs_1_), custom_call_target="tpu_custom_call" | custom-call | flops 500000000 | bytes 1048576 | tf_op jit(solution)/shard_map/gather_sent/pallas_call | solution.py:61
  5.8 3.0 %collective-permute-start.1 = (bf16[4,64,768]{2,1,0:T(8,128)(2,1)}, bf16[4,64,768]{2,1,0:T(8,128)(2,1)}, u32[]{:S(2)}, u32[]{:S(2)}) collective-permute-start(bf16[4,64,768]{2,1,0:T(8,128)(2,1)} %get-tuple-element.113), channel_id=1, source_target_pairs={{0,16},{16,0},{1,17},{17,1},{2,18},{18,2},{3,19},{19,3},{4,20},{20... | collective-permute-start | bytes 1179656 | tf_op jit(solution)/shard_map/ppermute | solution.py:25
  10.4 2.9 %gather_sent.5 = (bf16[8,64,768]{2,1,0:T(8,128)(2,1)}, f32[8,128]{1,0:T(8,128)}) custom-call(s32[16]{0:T(128)} %bitcast.50, bf16[16,64,768]{2,1,0:T(8,128)(2,1)} %bitcast.27, f32[8,128]{1,0:T(8,128)} %get-tuple-element.110.refs_1_), custom_call_target="tpu_custom_call" | custom-call | flops 500000000 | bytes 1048576 | tf_op jit(solution)/shard_map/gather_sent/pallas_call | solution.py:61
  13.9 12.7 %collective-permute-done.refs_2_ = bf16[4,64,768]{2,1,0:T(8,128)(2,1)} collective-permute-done((bf16[4,64,768]{2,1,0:T(8,128)(2,1)}, bf16[4,64,768]{2,1,0:T(8,128)(2,1)}, u32[]{:S(2)}, u32[]{:S(2)}) %collective-permute-start) | collective-permute-done | bytes 393248 | tf_op jit(solution)/shard_map/ppermute | solution.py:25
  26.7 1.7 collective-permute-start.2
  28.4 16.5 %attention_forward.1 = (bf16[1024,768]{1,0:T(8,128)(2,1)}, bf16[1024,2304]{1,0:T(8,128)(2,1)}, bf16[8,6,256,128]{3,2,1,0:T(8,128)(2,1)}, bf16[1024,768]{1,0:T(8,...) custom-call(s32[19]{0:T(128)} %pad_add_fusion.1.scalars_ref, ...), custom_call_target="tpu_custom_call" | custom-call | flops 40000000000 | bytes 1048576 | tf_op jit(solution)/shard_map/attention_forward/pallas_call | solution.py:61
  45.7 29.2 %feed_forward.1 = (bf16[1024,3072]{1,0:T(8,128)(2,1)}, bf16[1024,768]{1,0:T(8,128)(2,1)}, bf16[8,64,768]{2,1,0:T(8,128)(2,1)}, bf16[8,64,768]{2,1,0:T(8,128)(2,1...) custom-call(s32[19]{0:T(128)} %pad_add_fusion.1.scalars_ref, ...), custom_call_target="tpu_custom_call" | custom-call | flops 4000000000 | bytes 1048576 | tf_op jit(solution)/shard_map/feed_forward/pallas_call | solution.py:61
  75.0 4.7 %collective-permute-done.4 = bf16[2,4,192,768]{3,2,1,0:T(8,128)(2,1)S(1)} collective-permute-done((bf16[2,4,192,768]{3,2,1,0:T(8,128)(2,1)}, bf16[2,4,192,768]{3,2,1,0:T(8,128)(2,1)S(1)}, u32[]{:S(2)}, u32[]{:S(2)}) %collective-permute-start.4) | collective-permute-done | bytes 2359328 | tf_op jit(solution)/shard_map/ppermute | solution.py:25
  79.8 3.5 %fusion.refs_10_ = bf16[4,192,768]{2,1,0:T(8,128)(2,1)} fusion(bf16[8,192,768]{2,1,0:T(8,128)(2,1)S(1)} %bitcast.33, bf16[2,4,192,768]{3,2,1,0:T(8,128)(2,1)} %get-tuple-element.120), kind=kLoop, calls=%fused_computation.2 | loop fusion | flops 2359296 | bytes 3538944 | tf_op jit(solution)/shard_map/convert_element_type | solution.py:787
  83.2 1.4 collective-permute-start.5
  84.7 1.5 collective-permute-start.3
  86.2 27.3 %feed_backward.1 = (bf16[1024,768]{1,0:T(8,128)(2,1)}, f32[8,768]{1,0:T(8,128)}, f32[8,3072]{1,0:T(8,128)}, bf16[8,48,1536]{2,1,0:T(8,128)(2,1)}, bf16[8,48,1536...) custom-call(s32[19]{0:T(128)} %pad_add_fusion.1.scalars_ref, ...), custom_call_target="tpu_custom_call" | custom-call | flops 4000000000 | bytes 1048576 | tf_op jit(solution)/shard_map/feed_backward/pallas_call | solution.py:61
  115.6 2.4 %add_convert_fusion.3 = bf16[2,192,768]{2,1,0:T(8,128)(2,1)} fusion(bf16[8,192,768]{2,1,0:T(8,128)(2,1)} %bitcast.30, bf16[4,192,768]{2,1,0:T(8,128)(2,1)} %collective-permute-done.5, bf16[8,192,768]{2,1,0:T(8,128)(2,1)} %bitcast.34), kind=kLoop, calls=%fused_computation.6 | loop fusion | flops 1769472 | bytes 2359296 | tf_op jit(solution)/shard_map/convert_element_type | solution.py:787
  118.1 1.6 collective-permute-start.6
  120.4 2.3 %add_convert_fusion.2 = bf16[4,48,1536]{2,1,0:T(8,128)(2,1)} fusion(bf16[8,48,1536]{2,1,0:T(8,128)(2,1)} %collective-permute-done.8, bf16[8,48,1536]{2,1,0:T(8,128)(2,1)} %get-tuple-element.141), kind=kLoop, calls=%fused_computation.5 | loop fusion | flops 1179648 | bytes 1769472 | tf_op jit(solution)/shard_map/convert_element_type | solution.py:787
  123.1 2.3 %add_convert_fusion.refs_6_ = bf16[4,48,2304]{2,1,0:T(8,128)(2,1)} fusion(bf16[8,48,2304]{2,1,0:T(8,128)(2,1)} %collective-permute-done.7, bf16[8,48,2304]{2,1,0:T(8,128)(2,1)S(1)} %copy-done.1), kind=kLoop, calls=%fused_computation.3 | loop fusion | flops 1769472 | bytes 2654208 | tf_op jit(solution)/shard_map/convert_element_type | solution.py:787
  126.0 13.7 %attention_backward.2 = (bf16[1024,1536]{1,0:T(8,128)(2,1)}, f32[8,512]{1,0:T(8,128)}, bf16[8,48,1536]{2,1,0:T(8,128)(2,1)}, bf16[8,48,1536]{2,1,0:T(8,128)(2,1)}, f32[8,128]{1,0:T(8,128)}) custom-call(s32[19]{0:T(128)} %pad_add_fusion.1.scalars_ref, bf16[1024,768]{1,0:T(8,128)(2,1)} %get-tuple-element.133.refs_0_, ...), custom_call_target="tpu_custom_call" | custom-call | flops 4000000000 | bytes 1048576 | tf_op jit(solution)/shard_map/attention_backward/pallas_call | solution.py:61
  139.7 2.1 add_convert_fusion.9
  141.8 2.6 %collective-permute-start.9 = (bf16[1,192,768]{2,1,0:T(8,128)(2,1)}, bf16[1,192,768]{2,1,0:T(8,128)(2,1)}, u32[]{:S(2)}, u32[]{:S(2)}) collective-permute-start(bf16[1,192,768]{2,1,0:T(8,128)(2,1)} %add_convert_fusion.9), channel_id=1, source_target_pairs={{0,8},{1,9},{2,10},{3,11},{4,12},{5,13},{6,14},{7,15},{8,0},{9,1},... | collective-permute-start | bytes 884744 | tf_op jit(solution)/shard_map/ppermute | solution.py:25
  144.4 5.5 %collective-permute-done.10 = bf16[4,48,1536]{2,1,0:T(8,128)(2,1)} collective-permute-done((bf16[4,48,1536]{2,1,0:T(8,128)(2,1)}, bf16[4,48,1536]{2,1,0:T(8,128)(2,1)}, u32[]{:S(2)}, u32[]{:S(2)}) %collective-permute-start.10) | collective-permute-done | bytes 589856 | tf_op jit(solution)/shard_map/ppermute | solution.py:25
  149.9 2.0 add_convert_fusion.8
  151.9 2.2 add_convert_fusion.4.refs_1_
  155.1 2.2 add_convert_fusion.1.refs_12_
  157.3 2.0 collective-permute-start.14
  159.3 16.1 %attention_backward.3 = (bf16[8,64,768]{2,1,0:T(8,128)(2,1)}, bf16[8,64,768]{2,1,0:T(8,128)(2,1)}, f32[8,256]{1,0:T(8,128)}, bf16[8,48,896]{2,1,0:T(8,128)(2,1)}...) custom-call(s32[19]{0:T(128)} %pad_add_fusion.1.scalars_ref, bf16[1024,768]{1,0:T(8,128)(2,1)} %get-tuple-element.133.refs_0_, ...), custom_call_target="tpu_custom_call" | custom-call | flops 4000000000 | bytes 1048576 | tf_op jit(solution)/shard_map/attention_backward/pallas_call | solution.py:61
  176.0 2.1 add_convert_fusion.11
  178.0 1.8 collective-permute-start.22
  179.8 1.8 add_convert_fusion.5
  181.8 2.0 add_convert_fusion.7
  184.5 1.9 add_convert_fusion.16
  186.4 2.1 collective-permute-start.19
  188.5 2.2 add_convert_fusion.6.refs_3_
  190.7 3.4 %scatter_home.2 = (bf16[16,64,768]{2,1,0:T(8,128)(2,1)}, f32[8,128]{1,0:T(8,128)}) custom-call(s32[19]{0:T(128)} %pad_add_fusion.1.scalars_ref, bf16[8,64,768]{2,1,0:T(8,128)(2,1)} %get-tuple-element.118.refs_0_, bf16[8,64,768]{2,1,0:T(8,128)(2,1)} %collective-permute-done.3.refs_1_, f32[8,128]{1,0:T(8,128)} %get-tuple-element.173.refs_2_, ...), custom_call_target="tpu_custom_call" | custom-call | flops 20000000000 | bytes 1048576 | tf_op jit(solution)/shard_map/scatter_home/pallas_call | solution.py:61
  194.1 1.6 collective-permute-start.18
  196.9 2.4 %collective-permute-done.23 = bf16[2,48,1536]{2,1,0:T(8,128)(2,1)} collective-permute-done((bf16[2,48,1536]{2,1,0:T(8,128)(2,1)}, bf16[2,48,1536]{2,1,0:T(8,128)(2,1)}, u32[]{:S(2)}, u32[]{:S(2)}) %collective-permute-start.23) | collective-permute-done | bytes 294944 | tf_op jit(solution)/shard_map/ppermute | solution.py:25
  199.3 1.9 add_convert_fusion.15
  201.2 2.9 %collective-permute-start.24 = (bf16[1,48,1536]{2,1,0:T(8,128)(2,1)}, bf16[1,48,1536]{2,1,0:T(8,128)(2,1)}, u32[]{:S(2)}, u32[]{:S(2)}) collective-permute-start(bf16[1,48,1536]{2,1,0:T(8,128)(2,1)} %add_convert_fusion.15), channel_id=1, source_target_pairs={{0,8},{1,9},{2,10},{3,11},{4,12},{5,13},{6,14},{7,15},{8,0},{9,1},... | collective-permute-start | bytes 442376 | tf_op jit(solution)/shard_map/ppermute | solution.py:25
  204.1 2.2 add_convert_fusion.10
  206.2 1.6 collective-permute-start.28
  207.8 1.7 add_convert_fusion.18
  210.4 1.3 add_convert_fusion.14
  212.2 3.4 %scatter_home.3 = (bf16[16,64,768]{2,1,0:T(8,128)(2,1)}, f32[8,128]{1,0:T(8,128)}) custom-call(s32[19]{0:T(128)} %pad_add_fusion.1.scalars_ref, bf16[8,64,768]{2,1,0:T(8,128)(2,1)} %get-tuple-element.176.refs_0_, bf16[8,64,768]{2,1,0:T(8,128)(2,1)} %collective-permute-done.17.refs_1_, f32[8,128]{1,0:T(8,128)} %get-tuple-element.189.refs_2_), custom_call_target="tpu_custom_call" | custom-call | flops 20000000000 | bytes 1048576 | tf_op jit(solution)/shard_map/scatter_home/pallas_call | solution.py:61
  215.6 1.3 add_convert_fusion.13
  217.0 2.0 convert_add_fusion.1
  218.9 1.7 collective-permute-start.25
  226.4 2.6 %finish_qkv.1 = (f32[48,2304]{1,0:T(8,128)}, f32[2,48]{1,0:T(2,128)}, f32[2,48]{1,0:T(2,128)}, f32[4,48]{1,0:T(4,128)}, f32[4,48]{1,0:T(4,128)}, /*index=5*/f32[8,128]{1,0:T(8,128)}) custom-call(s32[19]{0:T(128)} %pad_add_fusion.1.scalars_ref, bf16[48,1536]{1,0:T(8,128)(2,1)} %bitcast.42, bf16[48,1536]{1,0:T(8,128)(2,1)} %copy-done.10, ...), custom_call_target="tpu_custom_call" | custom-call | flops 4000000000 | bytes 1048576 | tf_op jit(solution)/shard_map/finish_qkv/pallas_call | solution.py:61
  229.0 1.3 reshape.84
  (87 shorter events, 17.8 us)
Async XLA Ops:
  0.6 8.2 %copy-start.9 = (s32[1,16]{1,0:T(1,128)S(1)}, s32[1,16]{1,0:T(1,128)}, u32[]{:S(2)}) copy-start(s32[1,16]{1,0:T(1,128)} %param.15) | copy-start | bytes 196
  0.7 8.3 %copy-start.8 = (s32[2,1024]{1,0:T(2,128)S(1)}, s32[2,1024]{1,0:T(2,128)}, u32[]{:S(2)}) copy-start(s32[2,1024]{1,0:T(2,128)} %param.14) | copy-start | bytes 24580
  5.8 22.6 %collective-permute-start.1 = (bf16[4,64,768]{2,1,0:T(8,128)(2,1)}, bf16[4,64,768]{2,1,0:T(8,128)(2,1)}, u32[]{:S(2)}, u32[]{:S(2)}) collective-permute-start(bf16[4,64,768]{2,1,0:T(8,128)(2,1)} %get-tuple-element.113), channel_id=1, source_target_pairs={{0,16},{16,0},{1,17},{17,1},{2,18},{18,2},{3,19},{19,3},{4,20},{20... | collective-permute-start | bytes 1179656 | tf_op jit(solution)/shard_map/ppermute | solution.py:25
  8.8 17.9 %collective-permute-start = (bf16[4,64,768]{2,1,0:T(8,128)(2,1)}, bf16[4,64,768]{2,1,0:T(8,128)(2,1)}, u32[]{:S(2)}, u32[]{:S(2)}) collective-permute-start(bf16[4,64,768]{2,1,0:T(8,128)(2,1)} %get-tuple-element.108), channel_id=1, source_target_pairs={{0,16},{16,0},{1,17},{17,1},{2,18},{18,2},{3,19},{19,3},{4,20},{20... | collective-permute-start | bytes 1179656 | tf_op jit(solution)/shard_map/ppermute | solution.py:25
  26.7 19.0 %collective-permute-start.2 = (bf16[8,64,768]{2,1,0:T(8,128)(2,1)}, bf16[8,64,768]{2,1,0:T(8,128)(2,1)}, u32[]{:S(2)}, u32[]{:S(2)}) collective-permute-start(bf16[8,64,768]{2,1,0:T(8,128)(2,1)} %get-tuple-element.116), channel_id=1, source_target_pairs={{0,16},{16,0},{1,17},{17,1},{2,18},{18,2},{3,19},{19,3},{4,20},{20... | collective-permute-start | bytes 2359304 | tf_op jit(solution)/shard_map/ppermute | solution.py:25
  74.9 4.8 %collective-permute-start.4 = (bf16[2,4,192,768]{3,2,1,0:T(8,128)(2,1)}, bf16[2,4,192,768]{3,2,1,0:T(8,128)(2,1)S(1)}, u32[]{:S(2)}, u32[]{:S(2)}) collective-permute-start(bf16[2,4,192,768]{3,2,1,0:T(8,128)(2,1)} %get-tuple-element.121), channel_id=1, source_target_pairs={{0,1},{1,0},{2,3},{3,2},{4,5},{5,4},{6,7},{7,6},{8,9},{9,8},{10,11... | collective-permute-start | bytes 7077896 | tf_op jit(solution)/shard_map/ppermute | solution.py:25
  79.8 3.5 %copy-start = (bf16[2,4,192,768]{3,2,1,0:T(8,128)(2,1)}, bf16[2,4,192,768]{3,2,1,0:T(8,128)(2,1)S(1)}, u32[]{:S(2)}) copy-start(bf16[2,4,192,768]{3,2,1,0:T(8,128)(2,1)S(1)} %collective-permute-done.4) | copy-start | bytes 7077892
  83.2 32.4 %collective-permute-start.5 = (bf16[4,192,768]{2,1,0:T(8,128)(2,1)}, bf16[4,192,768]{2,1,0:T(8,128)(2,1)}, u32[]{:S(2)}, u32[]{:S(2)}) collective-permute-start(bf16[4,192,768]{2,1,0:T(8,128)(2,1)} %fusion.refs_10_), channel_id=1, source_target_pairs={{0,2},{1,3},{2,0},{3,1},{4,6},{5,7},{6,4},{7,5},{8,10},{9,11},{10,... | collective-permute-start | bytes 3538952 | tf_op jit(solution)/shard_map/ppermute | solution.py:25
  84.7 35.1 %collective-permute-start.3 = (bf16[8,64,768]{2,1,0:T(8,128)(2,1)}, bf16[8,64,768]{2,1,0:T(8,128)(2,1)}, u32[]{:S(2)}, u32[]{:S(2)}) collective-permute-start(bf16[8,64,768]{2,1,0:T(8,128)(2,1)} %get-tuple-element.119), channel_id=1, source_target_pairs={{0,16},{16,0},{1,17},{17,1},{2,18},{18,2},{3,19},{19,3},{4,20},{20... | collective-permute-start | bytes 2359304 | tf_op jit(solution)/shard_map/ppermute | solution.py:25
  115.1 5.3 %collective-permute-start.8 = (bf16[8,48,1536]{2,1,0:T(8,128)(2,1)}, bf16[8,48,1536]{2,1,0:T(8,128)(2,1)}, u32[]{:S(2)}, u32[]{:S(2)}) collective-permute-start(bf16[8,48,1536]{2,1,0:T(8,128)(2,1)} %get-tuple-element.138), channel_id=1, source_target_pairs={{0,1},{1,0},{2,3},{3,2},{4,5},{5,4},{6,7},{7,6},{8,9},{9,8},{10,11... | collective-permute-start | bytes 3538952 | tf_op jit(solution)/shard_map/ppermute | solution.py:25
  115.1 8.0 %collective-permute-start.7 = (bf16[8,48,2304]{2,1,0:T(8,128)(2,1)}, bf16[8,48,2304]{2,1,0:T(8,128)(2,1)}, u32[]{:S(2)}, u32[]{:S(2)}) collective-permute-start(bf16[8,48,2304]{2,1,0:T(8,128)(2,1)} %get-tuple-element.137), channel_id=1, source_target_pairs={{0,1},{1,0},{2,3},{3,2},{4,5},{5,4},{6,7},{7,6},{8,9},{9,8},{10,11... | collective-permute-start | bytes 5308424 | tf_op jit(solution)/shard_map/ppermute | solution.py:25
  118.1 21.6 %collective-permute-start.6 = (bf16[2,192,768]{2,1,0:T(8,128)(2,1)}, bf16[2,192,768]{2,1,0:T(8,128)(2,1)}, u32[]{:S(2)}, u32[]{:S(2)}) collective-permute-start(bf16[2,192,768]{2,1,0:T(8,128)(2,1)} %add_convert_fusion.3), channel_id=1, source_target_pairs={{0,4},{1,5},{2,6},{3,7},{4,0},{5,1},{6,2},{7,3},{8,12},{9,13},{10,... | collective-permute-start | bytes 1769480 | tf_op jit(solution)/shard_map/ppermute | solution.py:25
  120.4 2.7 %copy-start.1 = (bf16[8,48,2304]{2,1,0:T(8,128)(2,1)S(1)}, bf16[8,48,2304]{2,1,0:T(8,128)(2,1)}, u32[]{:S(2)}) copy-start(bf16[8,48,2304]{2,1,0:T(8,128)(2,1)} %get-tuple-element.144) | copy-start | bytes 5308420
  122.7 27.2 %collective-permute-start.10 = (bf16[4,48,1536]{2,1,0:T(8,128)(2,1)}, bf16[4,48,1536]{2,1,0:T(8,128)(2,1)}, u32[]{:S(2)}, u32[]{:S(2)}) collective-permute-start(bf16[4,48,1536]{2,1,0:T(8,128)(2,1)} %add_convert_fusion.2), channel_id=1, source_target_pairs={{0,4},{1,5},{2,6},{3,7},{4,0},{5,1},{6,2},{7,3},{8,12},{9,13},{10,... | collective-permute-start | bytes 1769480 | tf_op jit(solution)/shard_map/ppermute | solution.py:25
  125.5 26.4 %collective-permute-start.13 = (bf16[4,48,2304]{2,1,0:T(8,128)(2,1)}, bf16[4,48,2304]{2,1,0:T(8,128)(2,1)}, u32[]{:S(2)}, u32[]{:S(2)}) collective-permute-start(bf16[4,48,2304]{2,1,0:T(8,128)(2,1)} %add_convert_fusion.refs_6_), channel_id=1, source_target_pairs={{0,2},{1,3},{2,0},{3,1},{4,6},{5,7},{6,4},{7,5},{8,10},{9,11},{10,... | collective-permute-start | bytes 2654216 | tf_op jit(solution)/shard_map/ppermute | solution.py:25
  141.8 44.6 %collective-permute-start.9 = (bf16[1,192,768]{2,1,0:T(8,128)(2,1)}, bf16[1,192,768]{2,1,0:T(8,128)(2,1)}, u32[]{:S(2)}, u32[]{:S(2)}) collective-permute-start(bf16[1,192,768]{2,1,0:T(8,128)(2,1)} %add_convert_fusion.9), channel_id=1, source_target_pairs={{0,8},{1,9},{2,10},{3,11},{4,12},{5,13},{6,14},{7,15},{8,0},{9,1},... | collective-permute-start | bytes 884744 | tf_op jit(solution)/shard_map/ppermute | solution.py:25
  151.9 31.9 %collective-permute-start.11 = (bf16[2,48,1536]{2,1,0:T(8,128)(2,1)}, bf16[2,48,1536]{2,1,0:T(8,128)(2,1)}, u32[]{:S(2)}, u32[]{:S(2)}) collective-permute-start(bf16[2,48,1536]{2,1,0:T(8,128)(2,1)} %add_convert_fusion.8), channel_id=1, source_target_pairs={{0,2},{1,3},{2,0},{3,1},{4,6},{5,7},{6,4},{7,5},{8,10},{9,11},{10,... | collective-permute-start | bytes 884744 | tf_op jit(solution)/shard_map/ppermute | solution.py:25
  151.9 3.2 %collective-permute-start.12 = (bf16[8,48,1536]{2,1,0:T(8,128)(2,1)}, bf16[8,48,1536]{2,1,0:T(8,128)(2,1)}, u32[]{:S(2)}, u32[]{:S(2)}) collective-permute-start(bf16[8,48,1536]{2,1,0:T(8,128)(2,1)} %get-tuple-element.151), channel_id=1, source_target_pairs={{0,1},{1,0},{2,3},{3,2},{4,5},{5,4},{6,7},{7,6},{8,9},{9,8},{10,11... | collective-permute-start | bytes 3538952 | tf_op jit(solution)/shard_map/ppermute | solution.py:25
  154.1 21.4 %collective-permute-start.16 = (bf16[2,48,2304]{2,1,0:T(8,128)(2,1)}, bf16[2,48,2304]{2,1,0:T(8,128)(2,1)}, u32[]{:S(2)}, u32[]{:S(2)}) collective-permute-start(bf16[2,48,2304]{2,1,0:T(8,128)(2,1)} %add_convert_fusion.4.refs_1_), channel_id=1, source_target_pairs={{0,4},{1,5},{2,6},{3,7},{4,0},{5,1},{6,2},{7,3},{8,12},{9,13},{10,... | collective-permute-start | bytes 1327112 | tf_op jit(solution)/shard_map/ppermute | solution.py:25
  157.3 24.4 %collective-permute-start.14 = (bf16[4,48,1536]{2,1,0:T(8,128)(2,1)}, bf16[4,48,1536]{2,1,0:T(8,128)(2,1)}, u32[]{:S(2)}, u32[]{:S(2)}) collective-permute-start(bf16[4,48,1536]{2,1,0:T(8,128)(2,1)} %add_convert_fusion.1.refs_12_), channel_id=1, source_target_pairs={{0,2},{1,3},{2,0},{3,1},{4,6},{5,7},{6,4},{7,5},{8,10},{9,11},{10,... | collective-permute-start | bytes 1769480 | tf_op jit(solution)/shard_map/ppermute | solution.py:25
  175.4 2.7 %collective-permute-start.15 = (bf16[8,48,896]{2,1,0:T(8,128)(2,1)}, bf16[8,48,896]{2,1,0:T(8,128)(2,1)S(1)}, u32[]{:S(2)}, u32[]{:S(2)}) collective-permute-start(bf16[8,48,896]{2,1,0:T(8,128)(2,1)} %get-tuple-element.162), channel_id=1, source_target_pairs={{0,1},{1,0},{2,3},{3,2},{4,5},{5,4},{6,7},{7,6},{8,9},{9,8},{10,11... | collective-permute-start | bytes 2064392 | tf_op jit(solution)/shard_map/ppermute | solution.py:25
  175.5 36.7 %collective-permute-start.17 = (bf16[8,64,768]{2,1,0:T(8,128)(2,1)}, bf16[8,64,768]{2,1,0:T(8,128)(2,1)}, u32[]{:S(2)}, u32[]{:S(2)}) collective-permute-start(bf16[8,64,768]{2,1,0:T(8,128)(2,1)} %get-tuple-element.177), channel_id=1, source_target_pairs={{0,16},{16,0},{1,17},{17,1},{2,18},{18,2},{3,19},{19,3},{4,20},{20... | collective-permute-start | bytes 2359304 | tf_op jit(solution)/shard_map/ppermute | solution.py:25
  178.0 1.8 copy-start.2
  178.0 23.2 %collective-permute-start.22 = (bf16[1,48,2304]{2,1,0:T(8,128)(2,1)}, bf16[1,48,2304]{2,1,0:T(8,128)(2,1)}, u32[]{:S(2)}, u32[]{:S(2)}) collective-permute-start(bf16[1,48,2304]{2,1,0:T(8,128)(2,1)} %add_convert_fusion.11), channel_id=1, source_target_pairs={{0,8},{1,9},{2,10},{3,11},{4,12},{5,13},{6,14},{7,15},{8,0},{9,1},... | collective-permute-start | bytes 663560 | tf_op jit(solution)/shard_map/ppermute | solution.py:25
  181.6 12.5 %collective-permute-start.20 = (bf16[4,48,896]{2,1,0:T(8,128)(2,1)}, bf16[4,48,896]{2,1,0:T(8,128)(2,1)}, u32[]{:S(2)}, u32[]{:S(2)}) collective-permute-start(bf16[4,48,896]{2,1,0:T(8,128)(2,1)} %add_convert_fusion.5), channel_id=1, source_target_pairs={{0,2},{1,3},{2,0},{3,1},{4,6},{5,7},{6,4},{7,5},{8,10},{9,11},{10,... | collective-permute-start | bytes 1032200 | tf_op jit(solution)/shard_map/ppermute | solution.py:25
  183.7 15.6 %collective-permute-start.23 = (bf16[2,48,1536]{2,1,0:T(8,128)(2,1)}, bf16[2,48,1536]{2,1,0:T(8,128)(2,1)}, u32[]{:S(2)}, u32[]{:S(2)}) collective-permute-start(bf16[2,48,1536]{2,1,0:T(8,128)(2,1)} %add_convert_fusion.7), channel_id=1, source_target_pairs={{0,4},{1,5},{2,6},{3,7},{4,0},{5,1},{6,2},{7,3},{8,12},{9,13},{10,... | collective-permute-start | bytes 884744 | tf_op jit(solution)/shard_map/ppermute | solution.py:25
  186.4 23.1 %collective-permute-start.19 = (bf16[1,48,1536]{2,1,0:T(8,128)(2,1)}, bf16[1,48,1536]{2,1,0:T(8,128)(2,1)S(1)}, u32[]{:S(2)}, u32[]{:S(2)}) collective-permute-start(bf16[1,48,1536]{2,1,0:T(8,128)(2,1)} %add_convert_fusion.16), channel_id=1, source_target_pairs={{0,8},{1,9},{2,10},{3,11},{4,12},{5,13},{6,14},{7,15},{8,0},{9,1},... | collective-permute-start | bytes 442376 | tf_op jit(solution)/shard_map/ppermute | solution.py:25
  194.1 17.6 %collective-permute-start.18 = (bf16[192,768]{1,0:T(8,128)(2,1)}, bf16[192,768]{1,0:T(8,128)(2,1)}, u32[]{:S(2)}, u32[]{:S(2)}) collective-permute-start(bf16[192,768]{1,0:T(8,128)(2,1)} %bitcast.37), channel_id=1, source_target_pairs={{0,16},{16,0},{1,17},{17,1},{2,18},{18,2},{3,19},{19,3},{4,20},{20... | collective-permute-start | bytes 884744 | tf_op jit(solution)/shard_map/ppermute | solution.py:25
  199.3 6.9 %collective-permute-start.21 = (bf16[2,48,896]{2,1,0:T(8,128)(2,1)S(1)}, bf16[2,48,896]{2,1,0:T(8,128)(2,1)S(1)}, u32[]{:S(2)}, u32[]{:S(2)}) collective-permute-start(bf16[2,48,896]{2,1,0:T(8,128)(2,1)S(1)} %add_convert_fusion.12), channel_id=1, source_target_pairs={{0,4},{1,5},{2,6},{3,7},{4,0},{5,1},{6,2},{7,3},{8,12},{9,13},{10,... | collective-permute-start | bytes 516104 | tf_op jit(solution)/shard_map/ppermute | solution.py:25
  201.2 14.4 %collective-permute-start.24 = (bf16[1,48,1536]{2,1,0:T(8,128)(2,1)}, bf16[1,48,1536]{2,1,0:T(8,128)(2,1)}, u32[]{:S(2)}, u32[]{:S(2)}) collective-permute-start(bf16[1,48,1536]{2,1,0:T(8,128)(2,1)} %add_convert_fusion.15), channel_id=1, source_target_pairs={{0,8},{1,9},{2,10},{3,11},{4,12},{5,13},{6,14},{7,15},{8,0},{9,1},... | collective-permute-start | bytes 442376 | tf_op jit(solution)/shard_map/ppermute | solution.py:25
  206.2 5.5 %copy-start.3 = (bf16[2,48,896]{2,1,0:T(8,128)(2,1)}, bf16[2,48,896]{2,1,0:T(8,128)(2,1)S(1)}, u32[]{:S(2)}) copy-start(bf16[2,48,896]{2,1,0:T(8,128)(2,1)S(1)} %collective-permute-done.21) | copy-start | bytes 516100
  206.2 15.9 %collective-permute-start.28 = (bf16[48,2304]{1,0:T(8,128)(2,1)}, bf16[48,2304]{1,0:T(8,128)(2,1)}, u32[]{:S(2)}, u32[]{:S(2)}) collective-permute-start(bf16[48,2304]{1,0:T(8,128)(2,1)} %bitcast.19), channel_id=1, source_target_pairs={{0,16},{16,0},{1,17},{17,1},{2,18},{18,2},{3,19},{19,3},{4,20},{20... | collective-permute-start | bytes 663560 | tf_op jit(solution)/shard_map/ppermute | solution.py:25
  209.5 0.7 copy-start.5
  210.2 10.5 %collective-permute-start.26 = (bf16[1,48,896]{2,1,0:T(8,128)(2,1)}, bf16[1,48,896]{2,1,0:T(8,128)(2,1)}, u32[]{:S(2)}, u32[]{:S(2)}) collective-permute-start(bf16[1,48,896]{2,1,0:T(8,128)(2,1)} %add_convert_fusion.18), channel_id=1, source_target_pairs={{0,8},{1,9},{2,10},{3,11},{4,12},{5,13},{6,14},{7,15},{8,0},{9,1},... | collective-permute-start | bytes 258056 | tf_op jit(solution)/shard_map/ppermute | solution.py:25
  211.8 10.4 %collective-permute-start.29 = (bf16[48,1536]{1,0:T(8,128)(2,1)S(1)}, bf16[48,1536]{1,0:T(8,128)(2,1)}, u32[]{:S(2)}, u32[]{:S(2)}) collective-permute-start(bf16[48,1536]{1,0:T(8,128)(2,1)S(1)} %bitcast.39), channel_id=1, source_target_pairs={{0,16},{16,0},{1,17},{17,1},{2,18},{18,2},{3,19},{19,3},{4,20},{20... | collective-permute-start | bytes 442376 | tf_op jit(solution)/shard_map/ppermute | solution.py:25
  215.6 5.0 %copy-start.4 = (bf16[2,48,896]{2,1,0:T(8,128)(2,1)S(1)}, bf16[2,48,896]{2,1,0:T(8,128)(2,1)}, u32[]{:S(2)}) copy-start(bf16[2,48,896]{2,1,0:T(8,128)(2,1)} %copy-done.3) | copy-start | bytes 516100
  217.0 7.2 %copy-start.6 = (bf16[1,48,1536]{2,1,0:T(8,128)(2,1)}, bf16[1,48,1536]{2,1,0:T(8,128)(2,1)S(1)}, u32[]{:S(2)}) copy-start(bf16[1,48,1536]{2,1,0:T(8,128)(2,1)S(1)} %add_convert_fusion.13) | copy-start | bytes 442372
  218.9 6.8 %collective-permute-start.25 = (bf16[48,1536]{1,0:T(8,128)(2,1)S(1)}, bf16[48,1536]{1,0:T(8,128)(2,1)S(1)}, u32[]{:S(2)}, u32[]{:S(2)}) collective-permute-start(bf16[48,1536]{1,0:T(8,128)(2,1)S(1)} %bitcast.41), channel_id=1, source_target_pairs={{0,16},{16,0},{1,17},{17,1},{2,18},{18,2},{3,19},{19,3},{4,20},{20... | collective-permute-start | bytes 442376 | tf_op jit(solution)/shard_map/ppermute | solution.py:25
  221.7 3.4 %copy-start.7 = (bf16[1,48,896]{2,1,0:T(8,128)(2,1)}, bf16[1,48,896]{2,1,0:T(8,128)(2,1)S(1)}, u32[]{:S(2)}) copy-start(bf16[1,48,896]{2,1,0:T(8,128)(2,1)S(1)} %add_convert_fusion.17) | copy-start | bytes 258052
  221.7 4.7 %collective-permute-start.27 = (bf16[48,896]{1,0:T(8,128)(2,1)S(1)}, bf16[48,896]{1,0:T(8,128)(2,1)}, u32[]{:S(2)}, u32[]{:S(2)}) collective-permute-start(bf16[48,896]{1,0:T(8,128)(2,1)S(1)} %bitcast.44), channel_id=1, source_target_pairs={{0,16},{16,0},{1,17},{17,1},{2,18},{18,2},{3,19},{19,3},{4,20},{20... | collective-permute-start | bytes 258056 | tf_op jit(solution)/shard_map/ppermute | solution.py:25
  225.8 0.7 copy-start.10
where the time goes:
time: 232 us; the launch traced here: 230 us
  Pallas kernels  121 us (52%)
  other arithmetic  45.7 us (20%)
  starting transfers between devices  29.9 us (13%)
  waiting for transfers between devices  26.6 us (11%)
  local copies, waits for them, and re-layouts  5.76 us (2%)
    pallas_call x13, Pallas kernels, call(): pl.pallas_call(wrapped, grid_spec=pltpu.PrefetchScalarGridSpec(num_scalar...  121 us
    convert_element_type x20, other arithmetic, step(): total = total.astype(BF16)  39.4 us
    ppermute x30, starting transfers between devices, flipped(): return lax.ppermute(value, axis, pairs)  29.9 us
    ppermute x30, waiting for transfers between devices, flipped(): return lax.ppermute(value, axis, pairs)  26.6 us
  transfers between devices with their start and end apart: 30, of which 6 were waited for; matrix products, arithmetic and copies ran while one was open for 20% of the time, Pallas kernels for 37%

commit v1 on v0

--- a/solution.py
+++ b/solution.py
@@ -11,7 +11,7 @@
 EPSILON = 1e-12
 F32 = jnp.float32
 BF16 = jnp.bfloat16
-VMEM_LIMIT = 255 * 2**18
+VMEM_LIMIT = 26 * 2**20
 
 
 def dot(left, right, left_dim=1, right_dim=0):
@@ -44,39 +44,72 @@
 
 
 ANY = pl.BlockSpec(memory_space=pl.ANY)
+RESIDENT = pl.BlockSpec(memory_space=pltpu.VMEM)
 LINE = []
 
 
 def call(kernel, scalars, operands, in_specs, out_specs, out_shape, grid, name, **more):
     after = list(LINE)
-    into = list(more.get("into", ()))
-    into_first = more.get("into_first", 0)
     scratch = list(more.get("scratch", ()))
-    taken, spare, given = len(operands), len(into) + len(after), len(out_shape)
+    taken, given = len(operands), len(out_shape)
 
     def wrapped(scalars_ref, *refs):
-        outs = refs[taken + spare :]
+        outs = refs[taken + len(after) :]
         kernel(scalars_ref, *refs[:taken], *outs[:given], *outs[given + 1 :])
 
+    placed = [
+        pltpu.with_memory_space_constraint(array, pltpu.VMEM if spec is RESIDENT else pltpu.HBM)
+        for array, spec in zip(operands + after, list(in_specs) + [ANY] * len(after))
+    ]
+    shapes = [
+        pltpu.VMEM(shape.shape, shape.dtype) if spec is RESIDENT else shape
+        for shape, spec in zip(out_shape, out_specs)
+    ]
     outs = pl.pallas_call(
         wrapped,
         grid_spec=pltpu.PrefetchScalarGridSpec(
             num_scalar_prefetch=1,
             grid=grid,
-            in_specs=list(in_specs) + [ANY] * spare,
+            in_specs=list(in_specs) + [ANY] * len(after),
             out_specs=list(out_specs) + [ANY],
             scratch_shapes=scratch,
         ),
-        out_shape=list(out_shape) + [jax.ShapeDtypeStruct((8, 128), F32)],
-        input_output_aliases={1 + taken + i: i + into_first for i in range(len(into))},
+        out_shape=shapes + [jax.ShapeDtypeStruct((8, 128), F32)],
         compiler_params=params(more.get("limit", VMEM_LIMIT)),
         cost_estimate=pl.CostEstimate(
             flops=more.get("work", 4 * 10**9), bytes_accessed=2**20, transcendentals=0
         ),
         name=name,
-    )(scalars, *operands, *into, *after)
+    )(scalars, *placed)
     LINE[:] = [outs[-1]]
     return list(outs[:-1])
+
+
+def fetch(scalars, arrays):
+    count = len(arrays)
+
+    def kernel(scalars_ref, *refs):
+        sems = refs[-1]
+        copies = [
+            pltpu.make_async_copy(refs[i], refs[count + i], sems.at[i]) for i in range(count)
+        ]
+        for copy in copies:
+            copy.start()
+        for copy in copies:
+            copy.wait()
+
+    return call(
+        kernel,
+        scalars,
+        list(arrays),
+        [ANY] * count,
+        [RESIDENT] * count,
+        [jax.ShapeDtypeStruct(array.shape, array.dtype) for array in arrays],
+        (1,),
+        "fetch",
+        work=10**7,
+        scratch=[pltpu.SemaphoreType.DMA((count,))],
+    )
 
 
 def gather_sent(partner, rows, half, first, count):
@@ -104,7 +137,7 @@
         [jax.ShapeDtypeStruct(shape, rows.dtype)],
         (1,),
         "gather_sent",
-        work=5 * 10**8,
+        work=10**7,
         scratch=[pltpu.SemaphoreType.DMA((count,))],
     )[0]
 
@@ -214,9 +247,11 @@
         normed_out,
         root_out,
     ):
-        got = jnp.where(pl.program_id(0) < turn, got_a[...], got_b[...])
+        step = pl.program_id(0)
+        rows_here = pl.ds(pl.multiple_of(step * 2 * length, 2 * length), 2 * length)
+        got = jnp.where(step < turn, got_a[...], got_b[...])
         joined = jnp.concatenate([kept_a[0], got[0], kept_b[0], got[1]], 0)
-        joined_out[...] = joined
+        joined_out[rows_here] = joined
         mixed = dot(joined, w_qkv_ref[...])
         queries = (mixed[:, :width] + b_qv_ref[0:1, :]).astype(BF16)
         queries = (queries.astype(F32) * score_scale).astype(BF16)
@@ -226,7 +261,7 @@
             cols = slice(first_block * duo, (first_block + count) * duo)
             at = 3 * first_block * duo
             for value in (queries, keys, values):
-                mixed_out[:, at : at + count * duo] = value[:, cols]
+                mixed_out[rows_here, at : at + count * duo] = value[:, cols]
                 at += count * duo
         contexts = []
         for pair in range(2):
@@ -240,20 +275,17 @@
                 powered = jnp.exp(scores - jnp.max(scores, axis=-1, keepdims=True))
                 low_probs = powered * (1.0 / jnp.sum(powered, axis=-1, keepdims=True))
                 low_probs = low_probs.astype(BF16)
-                probs_out[pair, block] = low_probs
+                probs_out[2 * step + pair, block] = low_probs
                 heads.append(
                     dot(side_by_side(low_probs), split_heads(values[span, cols])).astype(BF16)
                 )
             contexts.append(jnp.concatenate(heads, 1))
         context = jnp.concatenate(contexts, 0)
-        context_out[...] = context
+        context_out[rows_here] = context
         pre_one = joined.astype(F32) + dot(context, w_out_ref[...]) + biases_ref[0:1, :]
         normed, root = normal_form(pre_one)
-        normed_out[...] = normed.astype(BF16)
-        root_out[...] = jnp.broadcast_to(root, root_out.shape)
-
-    def by_rows(columns):
-        return pl.BlockSpec((2 * length, columns), lambda i, s: (i, 0))
+        normed_out[rows_here] = normed.astype(BF16)
+        root_out[rows_here] = jnp.broadcast_to(root, (2 * length, 128))
 
     slot = (1, slot_rows, width)
     two = (2, slot_rows, width)
@@ -268,20 +300,13 @@
             pl.BlockSpec(two, lambda i, s: (jnp.minimum(i, turn - 1), 0, 0)),
             pl.BlockSpec(two, lambda i, s: (jnp.maximum(i - turn, 0), 0, 0)),
             pl.BlockSpec((2, 1, length), lambda i, s: (i, 0, 0)),
-            whole(w_qkv),
+            RESIDENT,
             whole(b_qv),
-            whole(w_out),
+            RESIDENT,
             whole(norm_gains),
             whole(bias_rows),
         ],
-        [
-            by_rows(width),
-            by_rows(3 * width),
-            pl.BlockSpec((2, blocks, 2 * length, length), lambda i, s: (i, 0, 0, 0)),
-            by_rows(width),
-            by_rows(width),
-            by_rows(128),
-        ],
+        [RESIDENT] * 6,
         [
             jax.ShapeDtypeStruct((total, width), BF16),
             jax.ShapeDtypeStruct((total, 3 * width), BF16),
@@ -329,9 +354,9 @@
         cot_a,
         cot_b,
         cot_far,
-        w_in_hbm,
+        w_in_ref,
         b_in_ref,
-        w_back_hbm,
+        w_back_ref,
         gains_ref,
         biases_ref,
         slope_out,
@@ -341,32 +366,15 @@
         sums_out,
         send,
         keep,
-        w_in_ref,
-        w_back_ref,
         held,
         acts,
-        branches,
         grad,
-        sems,
     ):
         step = pl.program_id(0)
 
-        def fetch_in(j):
-            cols = pl.ds(j * chunk, chunk)
-            return pltpu.make_async_copy(
-                w_in_hbm.at[:, cols], w_in_ref.at[:, cols], sems.at[0, j]
-            )
-
-        def fetch_back(j):
-            cols = pl.ds(j * chunk, chunk)
-            return pltpu.make_async_copy(w_back_hbm.at[cols], w_back_ref.at[cols], sems.at[1, j])
-
         @pl.when(step == 0)
         def _():
             sums_out[...] = jnp.zeros_like(sums_out)
-            for j in range(chunks):
-                fetch_in(j).start()
-                fetch_back(j).start()
 
         def close(pre_two, row):
             scaled, root = normal_form(pre_two)
@@ -377,37 +385,33 @@
             here = jnp.concatenate([cot_a[0], cot_far[0], cot_b[0], cot_far[1]], 0).astype(F32)
             d_two = normal_back(here * gains_ref[1:2, :], scaled, root)
             low = d_two.astype(BF16)
-            branch_out[...] = low
-            branches[pl.ds(row, rows)] = low
+            branch_out[pl.ds(pl.multiple_of(row, rows), rows)] = low
             return jnp.concatenate([row_sum(here * scaled), row_sum(here), row_sum(d_two)], 0)
 
-        def forward(first):
-            hidden = normed_ref[...].astype(F32) * gains_ref[0:1, :] + biases_ref[1:2, :]
+        def forward():
+            here = pl.ds(pl.multiple_of(step * rows, rows), rows)
+            hidden = normed_ref[here].astype(F32) * gains_ref[0:1, :] + biases_ref[1:2, :]
             low_hidden = hidden.astype(BF16)
             total = hidden + biases_ref[2:3, :]
             for j in range(chunks):
                 cols = slice(j * chunk, (j + 1) * chunk)
-                if first:
-                    fetch_in(j).wait()
                 inner = dot(low_hidden, w_in_ref[:, cols]) + b_in_ref[:, cols]
                 normal = 0.5 + 0.5 * lax.erf(inner * (0.5**0.5))
                 low_act = (inner * normal).astype(BF16)
                 density = jnp.exp(inner * inner * -0.5) * 0.3989422804014327
-                acts[pl.ds(step * rows, rows), cols] = low_act
-                slope_out[:, cols] = (normal + inner * density).astype(BF16)
-                if first:
-                    fetch_back(j).wait()
+                acts[here, cols] = low_act
+                slope_out[here, cols] = (normal + inner * density).astype(BF16)
                 total = total + dot(low_act, w_back_ref[cols, :])
             return total
 
         @pl.when(step == 0)
         def _():
-            held[...] = forward(True)
+            held[...] = forward()
 
         @pl.when((step > 0) & (step < steps))
         def _():
             before = held[...]
-            held[...] = forward(False)
+            held[...] = forward()
             sums_out[0:3, :] += close(before, (step - 1) * rows)
 
         @pl.when(step == steps)
@@ -417,15 +421,12 @@
         @pl.when(step >= steps)
         def _():
             start = pl.multiple_of((step - steps) * part, 128)
-            grad[...] = dot(acts[:, pl.ds(start, part)], branches[...], 0, 0).astype(BF16)
+            grad[...] = dot(acts[:, pl.ds(start, part)], branch_out[...], 0, 0).astype(BF16)
             core, low = scalars_ref[base + 1], scalars_ref[base + 2] & 1
             for j in range(2):
                 for out, which in ((send, 1 - core), (keep, core)):
                     row = ((low ^ j) * 2 + which) * shard
                     out[j, 0] = grad[pl.ds(pl.multiple_of(row, 16), shard), :]
-
-    def ahead(i):
-        return jnp.minimum(i, steps - 1)
 
     def behind(i):
         return jnp.clip(i - 1, 0, steps - 1)
@@ -447,19 +448,19 @@
         scalars,
         [normed, cot, cot, far_cot, w_in, b_in, w_back, norm_gains, bias_rows],
         [
-            pl.BlockSpec((rows, width), lambda i, s: (ahead(i), 0)),
+            RESIDENT,
             slot(0),
             slot(1),
             duo,
-            ANY,
+            RESIDENT,
             whole(b_in),
-            ANY,
+            RESIDENT,
             whole(norm_gains),
             whole(bias_rows),
         ],
         [
-            pl.BlockSpec((rows, inner_width), lambda i, s: (ahead(i), 0)),
-            pl.BlockSpec((rows, width), lambda i, s: (behind(i), 0)),
+            RESIDENT,
+            RESIDENT,
             duo,
             duo,
             pl.BlockSpec((8, width), lambda i, s: (0, 0)),
@@ -478,13 +479,9 @@
         (steps + parts,),
         "feed_forward",
         scratch=[
-            pltpu.VMEM((width, inner_width), BF16),
-            pltpu.VMEM((inner_width, width), BF16),
             pltpu.VMEM((rows, width), F32),
             pltpu.VMEM((height, inner_width), BF16),
-            pltpu.VMEM((height, width), BF16),
             pltpu.VMEM((part, width), BF16),
-            pltpu.SemaphoreType.DMA((2, chunks)),
         ],
     )
 
@@ -532,16 +529,17 @@
 
         @pl.when(step < steps)
         def _():
+            cols = pl.ds(pl.multiple_of(step * chunk, chunk), chunk)
             sums = jnp.zeros((1, chunk), F32)
             lows = []
             for r in range(0, total, 256):
                 span = slice(r, r + 256)
-                d_inner = dot(branch_ref[span], w_back_ref[...], 1, 1)
-                d_inner = d_inner * slope_ref[span].astype(F32)
+                d_inner = dot(branch_ref[span], w_back_ref[cols, :], 1, 1)
+                d_inner = d_inner * slope_ref[span, cols].astype(F32)
                 sums = sums + row_sum(d_inner)
                 low = d_inner.astype(BF16)
                 lows.append(low)
-                held[span] += dot(low, w_in_ref[...], 1, 1)
+                held[span] += dot(low, w_in_ref[:, cols], 1, 1)
             inner_sum_out[...] = jnp.broadcast_to(sums, inner_sum_out.shape)
             grad[...] = dot(low_hidden[...], jnp.concatenate(lows, 0), 0, 0).astype(BF16)
 
@@ -580,18 +578,18 @@
         scalars,
         [branch, slope, normed, root, context, w_in, w_back, norm_gains, bias_rows],
         [
-            whole(branch),
-            pl.BlockSpec((total, chunk), lambda i, s: (0, now(i))),
-            whole(normed),
-            whole(root),
-            whole(context),
-            pl.BlockSpec((width, chunk), lambda i, s: (0, now(i))),
-            pl.BlockSpec((chunk, width), lambda i, s: (now(i), 0)),
+            RESIDENT,
+            RESIDENT,
+            RESIDENT,
+            RESIDENT,
+            RESIDENT,
+            RESIDENT,
+            RESIDENT,
             whole(norm_gains),
             whole(bias_rows),
         ],
         [
-            pl.BlockSpec((total, width), lambda i, s: (0, 0)),
+            RESIDENT,
             pl.BlockSpec((8, width), lambda i, s: (0, 0)),
             pl.BlockSpec((8, chunk), lambda i, s: (0, now(i))),
             half_a,
@@ -647,56 +645,67 @@
             w_qkv_ref, earlier_ref, one, two, inner, sums_ref = refs[:6]
             kept_out, far_out, sums_out, send, keep, held, grad = refs[6:]
         else:
-            d_mixed_out, sums_out, send, keep, held, grad = refs
+            held, sums_out, send, keep, grad = refs
         step = pl.program_id(0)
 
         @pl.when(step == 0)
         def _():
             sums_out[...] = jnp.zeros_like(sums_out)
 
-        d_context = dot(low_attn_ref[...], w_out_ref[...], 1, 1).astype(BF16)
+        here = pl.ds(pl.multiple_of(step * 2 * length, 2 * length), 2 * length)
+        low_attn = low_attn_ref[here]
+        w_out_rows = slice(first_block * duo, (first_block + mine) * duo)
+        d_context = dot(low_attn, w_out_ref[w_out_rows, :], 1, 1).astype(BF16)
+        at = 3 * first_block * duo
+        mixed = mixed_ref[here, at : at + 3 * span_cols]
         rows = []
         for pair in range(2):
             span = slice(pair * length, (pair + 1) * length)
+            chosen = [probs_ref[2 * step + pair, first_block + block] for block in range(mine)]
+            parts = []
+            for third in range(3):
+                first = third * span_cols
+                parts.append(
+                    [
+                        mixed[span, first + block * duo : first + (block + 1) * duo]
+                        for block in range(mine)
+                    ]
+                )
+            queries, keys, values = parts
             d_heads, d_probs, d_scores = [], [], []
             for block in range(mine):
                 cols = slice(block * duo, (block + 1) * duo)
-                values = mixed_ref[span, 2 * span_cols + block * duo : 2 * span_cols + (block + 1) * duo]
                 d_heads.append(split_heads(d_context[span, cols]))
-                d_probs.append(dot(d_heads[block], values, 1, 1))
+                d_probs.append(dot(d_heads[block], values[block], 1, 1))
             for block in range(mine):
-                wide = probs_ref[pair, block].astype(F32)
+                wide = chosen[block].astype(F32)
                 mean = jnp.sum(wide * d_probs[block], axis=-1, keepdims=True)
                 d_scores.append((wide * (d_probs[block] - mean)).astype(BF16))
             d_queries, d_keys, d_values = [], [], []
             for block in range(mine):
-                cols = slice(block * duo, (block + 1) * duo)
-                queries = split_heads(mixed_ref[span, cols])
-                keys = mixed_ref[span, span_cols + block * duo : span_cols + (block + 1) * duo]
-                keys = split_heads(keys)
-                scaled = dot(side_by_side(d_scores[block]), keys) * score_scale
+                scaled = dot(side_by_side(d_scores[block]), split_heads(keys[block])) * score_scale
                 d_queries.append(scaled.astype(BF16))
-                d_keys.append(dot(d_scores[block], queries, 0, 0).astype(BF16))
-                d_values.append(dot(probs_ref[pair, block], d_heads[block], 0, 0).astype(BF16))
+                d_keys.append(dot(d_scores[block], split_heads(queries[block]), 0, 0).astype(BF16))
+                d_values.append(dot(chosen[block], d_heads[block], 0, 0).astype(BF16))
             rows.append(jnp.concatenate(d_queries + d_keys + d_values, 1))
         d_mixed = jnp.concatenate(rows, 0)
-        held[pl.ds(pl.multiple_of(step * 2 * length, 2 * length), 2 * length)] = d_mixed
+        held[here] = d_mixed
         sums_out[0:1, :] += row_sum(d_mixed[:, :span_cols].astype(F32))
         sums_out[1:2, :] += row_sum(d_mixed[:, 2 * span_cols :].astype(F32))
         if last:
-            d_rows = low_attn_ref[...].astype(F32)
+            d_rows = low_attn.astype(F32)
+            before = earlier_ref.shape[1] // 3
             for third in range(3):
-                before = earlier_ref.shape[1] // 3
-                before = earlier_ref[:, third * before : (third + 1) * before]
-                full = d_mixed[:, third * span_cols : (third + 1) * span_cols]
-                full = jnp.concatenate([before, full], 1)
-                d_rows = d_rows + dot(full, w_qkv_ref[:, third * width : (third + 1) * width], 1, 1)
+                full = [
+                    earlier_ref[here, third * before : (third + 1) * before],
+                    d_mixed[:, third * span_cols : (third + 1) * span_cols],
+                ]
+                cols = slice(third * width, (third + 1) * width)
+                d_rows = d_rows + dot(jnp.concatenate(full, 1), w_qkv_ref[:, cols], 1, 1)
             d_rows = d_rows.astype(BF16)
             for i in range(2):
                 kept_out[i] = d_rows[i * length : i * length + slot_rows]
                 far_out[i] = d_rows[i * length + slot_rows : (i + 1) * length]
-        else:
-            d_mixed_out[...] = d_mixed
 
         @pl.when(step == steps - 1)
         def _():
@@ -709,20 +718,9 @@
                 grad[:, 3 * span_cols :] = jnp.concatenate(small, 0).T.astype(BF16)
             spread(grad, (send, keep), scalars_ref, base, shard, order)
 
-    def by_rows(count, at=0):
-        return pl.BlockSpec((2 * length, count), lambda i, s: (i, at))
-
     two_slots = pl.BlockSpec((2, slot_rows, width), lambda i, s: (i, 0, 0))
     operands = [low_attn, mixed, probs, joined, w_out]
-    in_specs = [
-        by_rows(width),
-        by_rows(3 * span_cols, first_block // mine),
-        pl.BlockSpec((2, mine, 2 * length, length), lambda i, s: (i, first_block // mine, 0, 0)),
-        whole(joined),
-        pl.BlockSpec(
-            (span_cols, width), lambda i, s: (first_block // mine, 0), pipeline_mode=pl.Buffered(1)
-        ),
-    ]
+    in_specs = [RESIDENT] * 5
     grads = pl.BlockSpec((places, shard, columns), lambda i, s: (0, 0, 0))
     out_specs = [pl.BlockSpec((8, span_cols), lambda i, s: (0, 0)), grads, grads]
     out_shape = [
@@ -732,12 +730,12 @@
     ]
     if last:
         operands += [w_qkv, earlier, *sums]
-        in_specs += [whole(w_qkv), by_rows(earlier.shape[1])]
+        in_specs += [RESIDENT, RESIDENT]
         in_specs += [whole(each) for each in sums]
         out_specs = [two_slots, two_slots] + out_specs
         out_shape = [jax.ShapeDtypeStruct((pairs, slot_rows, width), BF16)] * 2 + out_shape
     else:
-        out_specs = [by_rows(3 * span_cols)] + out_specs
+        out_specs = [RESIDENT] + out_specs
         out_shape = [jax.ShapeDtypeStruct((total, 3 * span_cols), BF16)] + out_shape
     return call(
         kernel,
@@ -748,10 +746,8 @@
         out_shape,
         (steps,),
         "attention_backward",
-        scratch=[
-            pltpu.VMEM((total, 3 * span_cols), BF16),
-            pltpu.VMEM((width, columns), BF16),
-        ],
+        scratch=[pltpu.VMEM((total, 3 * span_cols), BF16)] * last
+        + [pltpu.VMEM((width, columns), BF16)],
     )
 
 
@@ -868,10 +864,6 @@
     slots = (groups, slot_rows, width)
     rows = layer_rows[0].reshape(slots)
     cot = cotangent[0].reshape(slots)
-    spot = place if aligned else 0 * place
-    scalars = jnp.concatenate(
-        [partner[0], jnp.stack([side, spot & 1, spot >> 1]).astype(jnp.int32)]
-    )
     cut = half // 2
     LINE.clear()
     sent = gather_sent(partner[0], rows, half, 0, cut)
@@ -879,8 +871,14 @@
     sent = gather_sent(partner[0], rows, half, cut, half - cut)
     got_b = flipped(sent, "mod", 1)
     sent_cot = gather_sent(partner[0], cot, half, 0, half)
-    got_a, sent_cot = lax.optimization_barrier((got_a, sent_cot))
+    got_a, sent_cot, row_live, partner = lax.optimization_barrier(
+        (got_a, sent_cot, row_live, partner)
+    )
     far_cot = flipped(sent_cot, "mod", 1)
+    spot = place if aligned else 0 * place
+    scalars = jnp.concatenate(
+        [partner[0], jnp.stack([side, spot & 1, spot >> 1]).astype(jnp.int32)]
+    )
 
     live = row_live.reshape(2, groups, slot_rows)
     words_live = lax.dynamic_slice_in_dim(live[0], side * half, half, 0)
@@ -894,6 +892,7 @@
         1,
     )[:, None, :]
 
+    w_qkv, w_out, w_in, w_back = fetch(scalars, (w_qkv, w_out, w_in, w_back))
     heads_weights = (w_qkv, b_qv, w_out, norm_gains, bias_rows)
     joined, mixed, probs, context, normed, root = attention_forward(
         scalars, rows, (got_a, got_b), seen, heads_weights

time: 232 us -> 213 us (0.918)
  other arithmetic: 45.7 us -> 10.8 us
  local copies, waits for them, and re-layouts: 5.76 us -> 22.2 us
  waiting for transfers between devices: 26.6 us -> 42.1 us
  Pallas kernels: 121 us -> 106 us
    convert_element_type x20, other arithmetic: 39.4 us -> 8.03 us  [step(): total = total.astype(BF16)]
    pallas_call x13 -> x14, Pallas kernels: 121 us -> 106 us  [call(): pl.pallas_call(wrapped, grid_spec=pltpu.PrefetchScalarGridSpec(num_scalar...]
    ppermute x30, waiting for transfers between devices: 26.6 us -> 42.1 us  [flipped(): return lax.ppermute(value, axis, pairs)]
    unnamed x22 -> x100, local copies, waits for them, and re-layouts: 1.36 us -> 16.5 us
    add x3, other arithmetic: 4.01 us -> 0.98 us  [result(): return self.mine.astype(F32) + in_turn(self.coming).astype(F32)]
  transfers between devices with their start and end apart: 30 -> 30, of which waited for: 6 -> 12; matrix products, arithmetic and copies ran while one was open for 20% -> 7% of each run, Pallas kernels for 37% -> 36%
where the time goes in v1:
time: 213 us
  Pallas kernels  106 us (50%)
  waiting for transfers between devices  42.1 us (20%)
  starting transfers between devices  30.9 us (15%)
  local copies, waits for them, and re-layouts  22.2 us (10%)
  other arithmetic  10.8 us (5%)
    pallas_call x14, Pallas kernels, call(): pl.pallas_call(wrapped, grid_spec=pltpu.PrefetchScalarGridSpec(num_scalar...  106 us
    ppermute x30, waiting for transfers between devices, flipped(): return lax.ppermute(value, axis, pairs)  42.1 us
    ppermute x30, starting transfers between devices, flipped(): return lax.ppermute(value, axis, pairs)  30.9 us
    unnamed x100, local copies, waits for them, and re-layouts  16.5 us
    convert_element_type x20, other arithmetic, step(): total = total.astype(BF16)  8.03 us
  transfers between devices with their start and end apart: 30, of which 12 were waited for; matrix products, arithmetic and copies ran while one was open for 7% of the time, Pallas kernels for 36%

profile of v1, /device:TPU:0, one launch (start us, length us, event | category | flops | bytes accessed | tf_op | source)
XLA Modules:
  0.0 212.7 jit_solution(12341709013260455407)
XLA Ops:
  1.3 1.6 gather_sent.3
  3.5 2.9 %collective-permute-start = (bf16[4,64,768]{2,1,0:T(8,128)(2,1)S(1)}, bf16[4,64,768]{2,1,0:T(8,128)(2,1)S(1)}, u32[]{:S(2)}, u32[]{:S(2)}) collective-permute-start(bf16[4,64,768]{2,1,0:T(8,128)(2,1)S(1)} %get-tuple-element.115), channel_id=1, source_target_pairs={{0,16},{16,0},{1,17},{17,1},{2,18},{18,2},{3,19},{19,3},{4,20},{20... | collective-permute-start | bytes 1179656 | tf_op jit(solution)/shard_map/ppermute | solution.py:25
  6.5 1.6 gather_sent.4
  8.7 1.8 gather_sent.5
  10.6 5.8 %collective-permute-done.refs_2_ = bf16[4,64,768]{2,1,0:T(8,128)(2,1)S(1)} collective-permute-done((bf16[4,64,768]{2,1,0:T(8,128)(2,1)S(1)}, bf16[4,64,768]{2,1,0:T(8,128)(2,1)S(1)}, u32[]{:S(2)}, u32[]{:S(2)}) %collective-permute-start) | collective-permute-done | bytes 393248 | tf_op jit(solution)/shard_map/ppermute | solution.py:25
  17.2 2.1 collective-permute-start.2
  20.1 5.7 %fetch.1 = (bf16[768,2304]{1,0:T(8,128)(2,1)S(1)}, bf16[768,768]{1,0:T(8,128)(2,1)S(1)}, bf16[768,3072]{1,0:T(8,128)(2,1)S(1)}, bf16[3072,768]{1,0:T(8,128)(2,1)S(1)}, f32[8,128]{1,0:T(8,128)S(1)}) custom-call(s32[19]{0:T(128)S(1)} %pad_add_fusion.1.scalars_ref, bf16[768,2304]{1,0:T(8,128)(2,1)} %refs_0_.1, bf16[768,768]{1,0:T(8,128)(2,1)} %refs_1_.1, ...), custom_call_target="tpu_custom_call" | custom-call | flops 10000000 | bytes 1048576 | tf_op jit(solution)/shard_map/fetch/pallas_call | solution.py:68
  27.2 14.0 %attention_forward.1 = (bf16[1024,768]{1,0:T(8,128)(2,1)S(1)}, bf16[1024,2304]{1,0:T(8,128)(2,1)S(1)}, bf16[8,6,256,128]{3,2,1,0:T(8,128)(2,1)S(1)}, bf16[1024,7...) custom-call(s32[19]{0:T(128)S(1)} %pad_add_fusion.1.scalars_ref, ...), custom_call_target="tpu_custom_call" | custom-call | flops 40000000000 | bytes 1048576 | tf_op jit(solution)/shard_map/attention_forward/pallas_call | solution.py:68
  41.2 1.1 copy-done.7
  43.9 25.5 %feed_forward.1 = (bf16[1024,3072]{1,0:T(8,128)(2,1)S(1)}, bf16[1024,768]{1,0:T(8,128)(2,1)S(1)}, bf16[8,64,768]{2,1,0:T(8,128)(2,1)S(1)}, bf16[8,64,768]{2,1,0:...) custom-call(s32[19]{0:T(128)S(1)} %pad_add_fusion.1.scalars_ref, ...), custom_call_target="tpu_custom_call" | custom-call | flops 4000000000 | bytes 1048576 | tf_op jit(solution)/shard_map/feed_forward/pallas_call | solution.py:68
  69.5 4.5 %collective-permute-done.4 = bf16[2,4,192,768]{3,2,1,0:T(8,128)(2,1)S(1)} collective-permute-done((bf16[2,4,192,768]{3,2,1,0:T(8,128)(2,1)S(1)}, bf16[2,4,192,768]{3,2,1,0:T(8,128)(2,1)S(1)}, u32[]{:S(2)}, u32[]{:S(2)}) %collective-permute-start.4) | collective-permute-done | bytes 2359328 | tf_op jit(solution)/shard_map/ppermute | solution.py:25
  74.1 1.5 fusion.refs_10_
  75.8 1.5 collective-permute-start.5
  77.9 22.4 %feed_backward.1 = (bf16[1024,768]{1,0:T(8,128)(2,1)S(1)}, f32[8,768]{1,0:T(8,128)S(1)}, f32[8,3072]{1,0:T(8,128)S(1)}, bf16[8,48,1536]{2,1,0:T(8,128)(2,1)S(1)}...) custom-call(s32[19]{0:T(128)S(1)} %pad_add_fusion.1.scalars_ref, ...), custom_call_target="tpu_custom_call" | custom-call | flops 4000000000 | bytes 1048576 | tf_op jit(solution)/shard_map/feed_backward/pallas_call | solution.py:68
  100.3 1.2 copy-done.5
  101.5 1.1 copy-done.9
  102.7 1.0 copy-done.11
  104.3 1.2 copy-done.24
  105.5 1.0 copy-done.25
  107.9 1.4 copy.24
  109.3 1.4 reshape.81.refs_9_
  111.2 1.6 add_convert_fusion.3
  112.9 1.6 collective-permute-start.6
  118.2 9.8 %attention_backward.2 = (bf16[1024,1536]{1,0:T(8,128)(2,1)S(1)}, f32[8,512]{1,0:T(8,128)S(1)}, bf16[8,48,1536]{2,1,0:T(8,128)(2,1)S(1)}, bf16[8,48,1536]{2,1,0:T(8,128)(2,1)S(1)}, f32[8,128]{1,0:T(8,128)S(1)}) custom-call(s32[19]{0:T(128)S(1)} %pad_add_fusion.1.scalars_ref, bf16[1024,768]{1,0:T(8,128)(2,1)S(1)} %copy-done.10, ...), custom_call_target="tpu_custom_call" | custom-call | flops 4000000000 | bytes 1048576 | tf_op jit(solution)/shard_map/attention_backward/pallas_call | solution.py:68
  128.1 1.0 collective-permute-done.6
  129.1 1.2 add_convert_fusion.9
  130.3 2.7 %collective-permute-start.9 = (bf16[1,192,768]{2,1,0:T(8,128)(2,1)S(1)}, bf16[1,192,768]{2,1,0:T(8,128)(2,1)S(1)}, u32[]{:S(2)}, u32[]{:S(2)}) collective-permute-start(bf16[1,192,768]{2,1,0:T(8,128)(2,1)S(1)} %add_convert_fusion.9), channel_id=1, source_target_pairs={{0,8},{1,9},{2,10},{3,11},{4,12},{5,13},{6,14},{7,15},{8,0},{9,1},... | collective-permute-start | bytes 884744 | tf_op jit(solution)/shard_map/ppermute | solution.py:25
  133.0 14.1 %collective-permute-done.10 = bf16[4,48,1536]{2,1,0:T(8,128)(2,1)S(1)} collective-permute-done((bf16[4,48,1536]{2,1,0:T(8,128)(2,1)S(1)}, bf16[4,48,1536]{2,1,0:T(8,128)(2,1)S(1)}, u32[]{:S(2)}, u32[]{:S(2)}) %collective-permute-start.10) | collective-permute-done | bytes 589856 | tf_op jit(solution)/shard_map/ppermute | solution.py:25
  149.2 1.3 collective-permute-done.12
  150.6 1.7 collective-permute-start.14
  152.4 12.9 %attention_backward.3 = (bf16[8,64,768]{2,1,0:T(8,128)(2,1)S(1)}, bf16[8,64,768]{2,1,0:T(8,128)(2,1)S(1)}, f32[8,256]{1,0:T(8,128)}, bf16[8,48,896]{2,1,0:T(8,12...) custom-call(s32[19]{0:T(128)S(1)} %pad_add_fusion.1.scalars_ref, bf16[1024,768]{1,0:T(8,128)(2,1)S(1)} %copy-done.10, ...), custom_call_target="tpu_custom_call" | custom-call | flops 4000000000 | bytes 1048576 | tf_op jit(solution)/shard_map/attention_backward/pallas_call | solution.py:68
  165.3 1.6 collective-permute-start.17
  167.4 2.2 %collective-permute-start.22 = (bf16[1,48,2304]{2,1,0:T(8,128)(2,1)S(1)}, bf16[1,48,2304]{2,1,0:T(8,128)(2,1)S(1)}, u32[]{:S(2)}, u32[]{:S(2)}) collective-permute-start(bf16[1,48,2304]{2,1,0:T(8,128)(2,1)S(1)} %add_convert_fusion.11), channel_id=1, source_target_pairs={{0,8},{1,9},{2,10},{3,11},{4,12},{5,13},{6,14},{7,15},{8,0},{9,1},... | collective-permute-start | bytes 663560 | tf_op jit(solution)/shard_map/ppermute | solution.py:25
  169.7 1.5 collective-permute-start.20
  171.3 1.4 collective-permute-start.23
  173.0 1.9 add_convert_fusion.6.refs_3_
  175.0 3.3 %scatter_home.2 = (bf16[16,64,768]{2,1,0:T(8,128)(2,1)}, f32[8,128]{1,0:T(8,128)S(1)}) custom-call(s32[19]{0:T(128)S(1)} %pad_add_fusion.1.scalars_ref, bf16[8,64,768]{2,1,0:T(8,128)(2,1)} %copy-done.26, bf16[8,64,768]{2,1,0:T(8,128)(2,1)} %collective-permute-done.3.refs_1_, f32[8,128]{1,0:T(8,128)} %copy-done.28, bf16[1,192,768]{2,1,0:T(8,128)(2,1)} %add_convert_fusion.6.refs_3_), custom_call_target="tpu_custom_call" | custom-call | flops 20000000000 | bytes 1048576 | tf_op jit(solution)/shard_map/scatter_home/pallas_call | solution.py:68
  178.3 1.3 collective-permute-done.20
  179.6 1.5 collective-permute-start.18
  181.2 5.1 %collective-permute-done.23 = bf16[2,48,1536]{2,1,0:T(8,128)(2,1)S(1)} collective-permute-done((bf16[2,48,1536]{2,1,0:T(8,128)(2,1)S(1)}, bf16[2,48,1536]{2,1,0:T(8,128)(2,1)S(1)}, u32[]{:S(2)}, u32[]{:S(2)}) %collective-permute-start.23) | collective-permute-done | bytes 294944 | tf_op jit(solution)/shard_map/ppermute | solution.py:25
  186.4 1.7 collective-permute-start.24
  188.2 5.1 %collective-permute-done.21 = bf16[2,48,896]{2,1,0:T(8,128)(2,1)S(1)} collective-permute-done((bf16[2,48,896]{2,1,0:T(8,128)(2,1)S(1)}, bf16[2,48,896]{2,1,0:T(8,128)(2,1)S(1)}, u32[]{:S(2)}, u32[]{:S(2)}) %collective-permute-start.21) | collective-permute-done | bytes 172064 | tf_op jit(solution)/shard_map/ppermute | solution.py:25
  193.3 1.5 collective-permute-start.28
  194.9 1.6 collective-permute-start.26
  198.1 3.3 %scatter_home.3 = (bf16[16,64,768]{2,1,0:T(8,128)(2,1)}, f32[8,128]{1,0:T(8,128)S(1)}) custom-call(s32[19]{0:T(128)S(1)} %pad_add_fusion.1.scalars_ref, bf16[8,64,768]{2,1,0:T(8,128)(2,1)} %copy-done.27, bf16[8,64,768]{2,1,0:T(8,128)(2,1)} %copy-done.44, f32[8,128]{1,0:T(8,128)} %copy-done.34), custom_call_target="tpu_custom_call" | custom-call | flops 20000000000 | bytes 1048576 | tf_op jit(solution)/shard_map/scatter_home/pallas_call | solution.py:68
  202.5 1.5 collective-permute-start.25
  206.3 1.8 collective-permute-done.25.refs_1_
  209.7 2.4 %finish_qkv.1 = (f32[48,2304]{1,0:T(8,128)}, f32[2,48]{1,0:T(2,128)}, f32[2,48]{1,0:T(2,128)}, f32[4,48]{1,0:T(4,128)}, f32[4,48]{1,0:T(4,128)S(1)}, /*index=5*/f32[8,128]{1,0:T(8,128)}) custom-call(s32[19]{0:T(128)S(1)} %pad_add_fusion.1.scalars_ref, bf16[48,1536]{1,0:T(8,128)(2,1)} %bitcast.55, bf16[48,1536]{1,0:T(8,128)(2,1)} %copy-done.46, ...), custom_call_target="tpu_custom_call" | custom-call | flops 4000000000 | bytes 1048576 | tf_op jit(solution)/shard_map/finish_qkv/pallas_call | solution.py:68
  (167 shorter events, 23.9 us)
Async XLA Ops:
  1.3 7.4 %copy-start.17 = (s32[1,16]{1,0:T(1,128)S(1)}, s32[1,16]{1,0:T(1,128)}, u32[]{:S(2)}) copy-start(s32[1,16]{1,0:T(1,128)} %param.15) | copy-start | bytes 196
  3.5 12.9 %collective-permute-start = (bf16[4,64,768]{2,1,0:T(8,128)(2,1)S(1)}, bf16[4,64,768]{2,1,0:T(8,128)(2,1)S(1)}, u32[]{:S(2)}, u32[]{:S(2)}) collective-permute-start(bf16[4,64,768]{2,1,0:T(8,128)(2,1)S(1)} %get-tuple-element.115), channel_id=1, source_target_pairs={{0,16},{16,0},{1,17},{17,1},{2,18},{18,2},{3,19},{19,3},{4,20},{20... | collective-permute-start | bytes 1179656 | tf_op jit(solution)/shard_map/ppermute | solution.py:25
  6.5 10.7 %copy-start.43 = (s32[2,1024]{1,0:T(2,128)S(1)}, s32[2,1024]{1,0:T(2,128)}, u32[]{:S(2)}) copy-start(s32[2,1024]{1,0:T(2,128)} %param.14) | copy-start | bytes 24580
  8.7 18.5 %collective-permute-start.1 = (bf16[4,64,768]{2,1,0:T(8,128)(2,1)S(1)}, bf16[4,64,768]{2,1,0:T(8,128)(2,1)}, u32[]{:S(2)}, u32[]{:S(2)}) collective-permute-start(bf16[4,64,768]{2,1,0:T(8,128)(2,1)S(1)} %get-tuple-element.121), channel_id=1, source_target_pairs={{0,16},{16,0},{1,17},{17,1},{2,18},{18,2},{3,19},{19,3},{4,20},{20... | collective-permute-start | bytes 1179656 | tf_op jit(solution)/shard_map/ppermute | solution.py:25
  10.5 8.9 %copy-start.20 = (f32[8,128]{1,0:T(8,128)}, f32[8,128]{1,0:T(8,128)S(1)}, u32[]{:S(2)}) copy-start(f32[8,128]{1,0:T(8,128)S(1)} %get-tuple-element.123.refs_4_) | copy-start | bytes 12292
  17.2 25.8 %collective-permute-start.2 = (bf16[8,64,768]{2,1,0:T(8,128)(2,1)S(1)}, bf16[8,64,768]{2,1,0:T(8,128)(2,1)S(1)}, u32[]{:S(2)}, u32[]{:S(2)}) collective-permute-start(bf16[8,64,768]{2,1,0:T(8,128)(2,1)S(1)} %get-tuple-element.128), channel_id=1, source_target_pairs={{0,16},{16,0},{1,17},{17,1},{2,18},{18,2},{3,19},{19,3},{4,20},{20... | collective-permute-start | bytes 2359304 | tf_op jit(solution)/shard_map/ppermute | solution.py:25
  26.4 14.8 %copy-start.1 = (bf16[768,2304]{1,0:T(8,128)(2,1)}, bf16[768,2304]{1,0:T(8,128)(2,1)S(1)}, u32[]{:S(2)}) copy-start(bf16[768,2304]{1,0:T(8,128)(2,1)S(1)} %get-tuple-element.124.refs_5_) | copy-start | bytes 10616836
  43.0 26.4 %copy-start = (bf16[1024,2304]{1,0:T(8,128)(2,1)}, bf16[1024,2304]{1,0:T(8,128)(2,1)S(1)}, u32[]{:S(2)}) copy-start(bf16[1024,2304]{1,0:T(8,128)(2,1)S(1)} %get-tuple-element.148.refs_1_) | copy-start | bytes 14155780
  43.0 26.4 %copy-start.3 = (bf16[8,6,256,128]{3,2,1,0:T(8,128)(2,1)}, bf16[8,6,256,128]{3,2,1,0:T(8,128)(2,1)S(1)}, u32[]{:S(2)}) copy-start(bf16[8,6,256,128]{3,2,1,0:T(8,128)(2,1)S(1)} %get-tuple-element.149.refs_2_) | copy-start | bytes 9437188
  69.4 6.2 %copy-start.13 = (f32[8,768]{1,0:T(8,128)}, f32[8,768]{1,0:T(8,128)S(1)}, u32[]{:S(2)}) copy-start(f32[8,768]{1,0:T(8,128)S(1)} %get-tuple-element.172.refs_8_) | copy-start | bytes 73732
  69.4 6.2 %copy-start.18 = (f32[8,128]{1,0:T(8,128)}, f32[8,128]{1,0:T(8,128)S(1)}, u32[]{:S(2)}) copy-start(f32[8,128]{1,0:T(8,128)S(1)} %get-tuple-element.142.refs_9_) | copy-start | bytes 12292
  69.4 6.2 %copy-start.26 = (bf16[8,64,768]{2,1,0:T(8,128)(2,1)}, bf16[8,64,768]{2,1,0:T(8,128)(2,1)S(1)}, u32[]{:S(2)}) copy-start(bf16[8,64,768]{2,1,0:T(8,128)(2,1)S(1)} %get-tuple-element.132.refs_0_) | copy-start | bytes 2359300
  69.5 4.6 %collective-permute-start.4 = (bf16[2,4,192,768]{3,2,1,0:T(8,128)(2,1)S(1)}, bf16[2,4,192,768]{3,2,1,0:T(8,128)(2,1)S(1)}, u32[]{:S(2)}, u32[]{:S(2)}) collective-permute-start(bf16[2,4,192,768]{3,2,1,0:T(8,128)(2,1)S(1)} %get-tuple-element.135), channel_id=1, source_target_pairs={{0,1},{1,0},{2,3},{3,2},{4,5},{5,4},{6,7},{7,6},{8,9},{9,8},{10,11... | collective-permute-start | bytes 7077896 | tf_op jit(solution)/shard_map/ppermute | solution.py:25
  75.8 35.4 %collective-permute-start.5 = (bf16[4,192,768]{2,1,0:T(8,128)(2,1)}, bf16[4,192,768]{2,1,0:T(8,128)(2,1)}, u32[]{:S(2)}, u32[]{:S(2)}) collective-permute-start(bf16[4,192,768]{2,1,0:T(8,128)(2,1)} %fusion.refs_10_), channel_id=1, source_target_pairs={{0,2},{1,3},{2,0},{3,1},{4,6},{5,7},{6,4},{7,5},{8,10},{9,11},{10,... | collective-permute-start | bytes 3538952 | tf_op jit(solution)/shard_map/ppermute | solution.py:25
  77.4 37.1 %collective-permute-start.3 = (bf16[8,64,768]{2,1,0:T(8,128)(2,1)}, bf16[8,64,768]{2,1,0:T(8,128)(2,1)}, u32[]{:S(2)}, u32[]{:S(2)}) collective-permute-start(bf16[8,64,768]{2,1,0:T(8,128)(2,1)} %get-tuple-element.133), channel_id=1, source_target_pairs={{0,16},{16,0},{1,17},{17,1},{2,18},{18,2},{3,19},{19,3},{4,20},{20... | collective-permute-start | bytes 2359304 | tf_op jit(solution)/shard_map/ppermute | solution.py:25
  110.7 4.4 %collective-permute-start.8 = (bf16[8,48,1536]{2,1,0:T(8,128)(2,1)}, bf16[8,48,1536]{2,1,0:T(8,128)(2,1)S(1)}, u32[]{:S(2)}, u32[]{:S(2)}) collective-permute-start(bf16[8,48,1536]{2,1,0:T(8,128)(2,1)} %copy-done.25), channel_id=1, source_target_pairs={{0,1},{1,0},{2,3},{3,2},{4,5},{5,4},{6,7},{7,6},{8,9},{9,8},{10,11... | collective-permute-start | bytes 3538952 | tf_op jit(solution)/shard_map/ppermute | solution.py:25
  110.7 5.6 %collective-permute-start.7 = (bf16[8,48,2304]{2,1,0:T(8,128)(2,1)}, bf16[8,48,2304]{2,1,0:T(8,128)(2,1)S(1)}, u32[]{:S(2)}, u32[]{:S(2)}) collective-permute-start(bf16[8,48,2304]{2,1,0:T(8,128)(2,1)} %copy-done.24), channel_id=1, source_target_pairs={{0,1},{1,0},{2,3},{3,2},{4,5},{5,4},{6,7},{7,6},{8,9},{9,8},{10,11... | collective-permute-start | bytes 5308424 | tf_op jit(solution)/shard_map/ppermute | solution.py:25
  111.2 6.2 %slice-start = ((s8[4718592]{0:T(1024)(128)(4,1)}), s8[4194304]{0:T(1024)(128)(4,1)S(1)}, s32[]{:S(2)}) async-start(s8[4718592]{0:T(1024)(128)(4,1)} %bitcast.28), calls=%async_computation | async-start | bytes 8388608
  112.8 4.6 %slice-start.1 = ((s8[4718592]{0:T(1024)(128)(4,1)}), s8[524288]{0:T(1024)(128)(4,1)S(1)}, s32[]{:S(2)}) async-start(s8[4718592]{0:T(1024)(128)(4,1)} %bitcast.28), calls=%async_computation.1 | async-start | bytes 1048576
  112.9 16.3 %collective-permute-start.6 = (bf16[2,192,768]{2,1,0:T(8,128)(2,1)S(1)}, bf16[2,192,768]{2,1,0:T(8,128)(2,1)S(1)}, u32[]{:S(2)}, u32[]{:S(2)}) collective-permute-start(bf16[2,192,768]{2,1,0:T(8,128)(2,1)S(1)} %add_convert_fusion.3), channel_id=1, source_target_pairs={{0,4},{1,5},{2,6},{3,7},{4,0},{5,1},{6,2},{7,3},{8,12},{9,13},{10,... | collective-permute-start | bytes 1769480 | tf_op jit(solution)/shard_map/ppermute | solution.py:25
  115.3 31.9 %collective-permute-start.10 = (bf16[4,48,1536]{2,1,0:T(8,128)(2,1)S(1)}, bf16[4,48,1536]{2,1,0:T(8,128)(2,1)S(1)}, u32[]{:S(2)}, u32[]{:S(2)}) collective-permute-start(bf16[4,48,1536]{2,1,0:T(8,128)(2,1)S(1)} %add_convert_fusion.2), channel_id=1, source_target_pairs={{0,4},{1,5},{2,6},{3,7},{4,0},{5,1},{6,2},{7,3},{8,12},{9,13},{10,... | collective-permute-start | bytes 1769480 | tf_op jit(solution)/shard_map/ppermute | solution.py:25
  116.5 31.1 %collective-permute-start.13 = (bf16[4,48,2304]{2,1,0:T(8,128)(2,1)S(1)}, bf16[4,48,2304]{2,1,0:T(8,128)(2,1)S(1)}, u32[]{:S(2)}, u32[]{:S(2)}) collective-permute-start(bf16[4,48,2304]{2,1,0:T(8,128)(2,1)S(1)} %add_convert_fusion.refs_6_), channel_id=1, source_target_pairs={{0,2},{1,3},{2,0},{3,1},{4,6},{5,7},{6,4},{7,5},{8,10},{9,11},{10,... | collective-permute-start | bytes 2654216 | tf_op jit(solution)/shard_map/ppermute | solution.py:25
  128.0 19.8 %copy-start.15 = (f32[8,512]{1,0:T(8,128)}, f32[8,512]{1,0:T(8,128)S(1)}, u32[]{:S(2)}) copy-start(f32[8,512]{1,0:T(8,128)S(1)} %get-tuple-element.174.refs_10_) | copy-start | bytes 49156
  128.1 19.8 %copy-start.31 = (f32[8,128]{1,0:T(8,128)}, f32[8,128]{1,0:T(8,128)S(1)}, u32[]{:S(2)}) copy-start(f32[8,128]{1,0:T(8,128)S(1)} %get-tuple-element.167.refs_0_) | copy-start | bytes 12292
  130.3 42.5 %collective-permute-start.9 = (bf16[1,192,768]{2,1,0:T(8,128)(2,1)S(1)}, bf16[1,192,768]{2,1,0:T(8,128)(2,1)S(1)}, u32[]{:S(2)}, u32[]{:S(2)}) collective-permute-start(bf16[1,192,768]{2,1,0:T(8,128)(2,1)S(1)} %add_convert_fusion.9), channel_id=1, source_target_pairs={{0,8},{1,9},{2,10},{3,11},{4,12},{5,13},{6,14},{7,15},{8,0},{9,1},... | collective-permute-start | bytes 884744 | tf_op jit(solution)/shard_map/ppermute | solution.py:25
  147.2 24.1 %collective-permute-start.11 = (bf16[2,48,1536]{2,1,0:T(8,128)(2,1)S(1)}, bf16[2,48,1536]{2,1,0:T(8,128)(2,1)S(1)}, u32[]{:S(2)}, u32[]{:S(2)}) collective-permute-start(bf16[2,48,1536]{2,1,0:T(8,128)(2,1)S(1)} %add_convert_fusion.8), channel_id=1, source_target_pairs={{0,2},{1,3},{2,0},{3,1},{4,6},{5,7},{6,4},{7,5},{8,10},{9,11},{10,... | collective-permute-start | bytes 884744 | tf_op jit(solution)/shard_map/ppermute | solution.py:25
  147.6 2.8 %collective-permute-start.12 = (bf16[8,48,1536]{2,1,0:T(8,128)(2,1)S(1)}, bf16[8,48,1536]{2,1,0:T(8,128)(2,1)S(1)}, u32[]{:S(2)}, u32[]{:S(2)}) collective-permute-start(bf16[8,48,1536]{2,1,0:T(8,128)(2,1)S(1)} %get-tuple-element.165), channel_id=1, source_target_pairs={{0,1},{1,0},{2,3},{3,2},{4,5},{5,4},{6,7},{7,6},{8,9},{9,8},{10,11... | collective-permute-start | bytes 3538952 | tf_op jit(solution)/shard_map/ppermute | solution.py:25
  147.8 17.4 %collective-permute-start.16 = (bf16[2,48,2304]{2,1,0:T(8,128)(2,1)S(1)}, bf16[2,48,2304]{2,1,0:T(8,128)(2,1)S(1)}, u32[]{:S(2)}, u32[]{:S(2)}) collective-permute-start(bf16[2,48,2304]{2,1,0:T(8,128)(2,1)S(1)} %add_convert_fusion.4.refs_1_), channel_id=1, source_target_pairs={{0,4},{1,5},{2,6},{3,7},{4,0},{5,1},{6,2},{7,3},{8,12},{9,13},{10,... | collective-permute-start | bytes 1327112 | tf_op jit(solution)/shard_map/ppermute | solution.py:25
  148.6 3.8 %copy-start.2 = (bf16[768,2304]{1,0:T(8,128)(2,1)S(1)}, bf16[768,2304]{1,0:T(8,128)(2,1)}, u32[]{:S(2)}) copy-start(bf16[768,2304]{1,0:T(8,128)(2,1)} %copy-done.1) | copy-start | bytes 10616836
  150.6 19.0 %collective-permute-start.14 = (bf16[4,48,1536]{2,1,0:T(8,128)(2,1)S(1)}, bf16[4,48,1536]{2,1,0:T(8,128)(2,1)S(1)}, u32[]{:S(2)}, u32[]{:S(2)}) collective-permute-start(bf16[4,48,1536]{2,1,0:T(8,128)(2,1)S(1)} %add_convert_fusion.1.refs_12_), channel_id=1, source_target_pairs={{0,2},{1,3},{2,0},{3,1},{4,6},{5,7},{6,4},{7,5},{8,10},{9,11},{10,... | collective-permute-start | bytes 1769480 | tf_op jit(solution)/shard_map/ppermute | solution.py:25
  165.3 6.0 %copy-start.27 = (bf16[8,64,768]{2,1,0:T(8,128)(2,1)}, bf16[8,64,768]{2,1,0:T(8,128)(2,1)S(1)}, u32[]{:S(2)}) copy-start(bf16[8,64,768]{2,1,0:T(8,128)(2,1)S(1)} %get-tuple-element.190.refs_0_) | copy-start | bytes 2359300
  165.3 6.0 %copy-start.28 = (f32[8,128]{1,0:T(8,128)}, f32[8,128]{1,0:T(8,128)S(1)}, u32[]{:S(2)}) copy-start(f32[8,128]{1,0:T(8,128)S(1)} %get-tuple-element.187.refs_2_) | copy-start | bytes 12292
  165.3 2.1 %collective-permute-start.15 = (bf16[8,48,896]{2,1,0:T(8,128)(2,1)S(1)}, bf16[8,48,896]{2,1,0:T(8,128)(2,1)S(1)}, u32[]{:S(2)}, u32[]{:S(2)}) collective-permute-start(bf16[8,48,896]{2,1,0:T(8,128)(2,1)S(1)} %get-tuple-element.176), channel_id=1, source_target_pairs={{0,1},{1,0},{2,3},{3,2},{4,5},{5,4},{6,7},{7,6},{8,9},{9,8},{10,11... | collective-permute-start | bytes 2064392 | tf_op jit(solution)/shard_map/ppermute | solution.py:25
  165.3 31.9 %collective-permute-start.17 = (bf16[8,64,768]{2,1,0:T(8,128)(2,1)S(1)}, bf16[8,64,768]{2,1,0:T(8,128)(2,1)S(1)}, u32[]{:S(2)}, u32[]{:S(2)}) collective-permute-start(bf16[8,64,768]{2,1,0:T(8,128)(2,1)S(1)} %get-tuple-element.191), channel_id=1, source_target_pairs={{0,16},{16,0},{1,17},{17,1},{2,18},{18,2},{3,19},{19,3},{4,20},{20... | collective-permute-start | bytes 2359304 | tf_op jit(solution)/shard_map/ppermute | solution.py:25
  167.4 18.9 %collective-permute-start.22 = (bf16[1,48,2304]{2,1,0:T(8,128)(2,1)S(1)}, bf16[1,48,2304]{2,1,0:T(8,128)(2,1)S(1)}, u32[]{:S(2)}, u32[]{:S(2)}) collective-permute-start(bf16[1,48,2304]{2,1,0:T(8,128)(2,1)S(1)} %add_convert_fusion.11), channel_id=1, source_target_pairs={{0,8},{1,9},{2,10},{3,11},{4,12},{5,13},{6,14},{7,15},{8,0},{9,1},... | collective-permute-start | bytes 663560 | tf_op jit(solution)/shard_map/ppermute | solution.py:25
  169.7 9.9 %collective-permute-start.20 = (bf16[4,48,896]{2,1,0:T(8,128)(2,1)S(1)}, bf16[4,48,896]{2,1,0:T(8,128)(2,1)S(1)}, u32[]{:S(2)}, u32[]{:S(2)}) collective-permute-start(bf16[4,48,896]{2,1,0:T(8,128)(2,1)S(1)} %add_convert_fusion.5), channel_id=1, source_target_pairs={{0,2},{1,3},{2,0},{3,1},{4,6},{5,7},{6,4},{7,5},{8,10},{9,11},{10,... | collective-permute-start | bytes 1032200 | tf_op jit(solution)/shard_map/ppermute | solution.py:25
  171.3 15.0 %collective-permute-start.23 = (bf16[2,48,1536]{2,1,0:T(8,128)(2,1)S(1)}, bf16[2,48,1536]{2,1,0:T(8,128)(2,1)S(1)}, u32[]{:S(2)}, u32[]{:S(2)}) collective-permute-start(bf16[2,48,1536]{2,1,0:T(8,128)(2,1)S(1)} %add_convert_fusion.7), channel_id=1, source_target_pairs={{0,4},{1,5},{2,6},{3,7},{4,0},{5,1},{6,2},{7,3},{8,12},{9,13},{10,... | collective-permute-start | bytes 884744 | tf_op jit(solution)/shard_map/ppermute | solution.py:25
  172.8 22.1 %collective-permute-start.19 = (bf16[1,48,1536]{2,1,0:T(8,128)(2,1)S(1)}, bf16[1,48,1536]{2,1,0:T(8,128)(2,1)S(1)}, u32[]{:S(2)}, u32[]{:S(2)}) collective-permute-start(bf16[1,48,1536]{2,1,0:T(8,128)(2,1)S(1)} %add_convert_fusion.16), channel_id=1, source_target_pairs={{0,8},{1,9},{2,10},{3,11},{4,12},{5,13},{6,14},{7,15},{8,0},{9,1},... | collective-permute-start | bytes 442376 | tf_op jit(solution)/shard_map/ppermute | solution.py:25
  175.0 4.6 %copy-start.37 = (bf16[1,192,768]{2,1,0:T(8,128)(2,1)S(1)}, bf16[1,192,768]{2,1,0:T(8,128)(2,1)}, u32[]{:S(2)}) copy-start(bf16[1,192,768]{2,1,0:T(8,128)(2,1)} %add_convert_fusion.6.refs_3_) | copy-start | bytes 884740
  178.3 16.6 %copy-start.34 = (f32[8,128]{1,0:T(8,128)}, f32[8,128]{1,0:T(8,128)S(1)}, u32[]{:S(2)}) copy-start(f32[8,128]{1,0:T(8,128)S(1)} %get-tuple-element.203.refs_2_) | copy-start | bytes 12292
  179.6 17.0 %collective-permute-start.18 = (bf16[192,768]{1,0:T(8,128)(2,1)S(1)}, bf16[192,768]{1,0:T(8,128)(2,1)S(1)}, u32[]{:S(2)}, u32[]{:S(2)}) collective-permute-start(bf16[192,768]{1,0:T(8,128)(2,1)S(1)} %bitcast.48), channel_id=1, source_target_pairs={{0,16},{16,0},{1,17},{17,1},{2,18},{18,2},{3,19},{19,3},{4,20},{20... | collective-permute-start | bytes 884744 | tf_op jit(solution)/shard_map/ppermute | solution.py:25
  186.3 7.1 %collective-permute-start.21 = (bf16[2,48,896]{2,1,0:T(8,128)(2,1)S(1)}, bf16[2,48,896]{2,1,0:T(8,128)(2,1)S(1)}, u32[]{:S(2)}, u32[]{:S(2)}) collective-permute-start(bf16[2,48,896]{2,1,0:T(8,128)(2,1)S(1)} %add_convert_fusion.12), channel_id=1, source_target_pairs={{0,4},{1,5},{2,6},{3,7},{4,0},{5,1},{6,2},{7,3},{8,12},{9,13},{10,... | collective-permute-start | bytes 516104 | tf_op jit(solution)/shard_map/ppermute | solution.py:25
  186.4 15.1 %collective-permute-start.24 = (bf16[1,48,1536]{2,1,0:T(8,128)(2,1)S(1)}, bf16[1,48,1536]{2,1,0:T(8,128)(2,1)S(1)}, u32[]{:S(2)}, u32[]{:S(2)}) collective-permute-start(bf16[1,48,1536]{2,1,0:T(8,128)(2,1)S(1)} %add_convert_fusion.15), channel_id=1, source_target_pairs={{0,8},{1,9},{2,10},{3,11},{4,12},{5,13},{6,14},{7,15},{8,0},{9,1},... | collective-permute-start | bytes 442376 | tf_op jit(solution)/shard_map/ppermute | solution.py:25
  193.3 11.3 %collective-permute-start.28 = (bf16[48,2304]{1,0:T(8,128)(2,1)S(1)}, bf16[48,2304]{1,0:T(8,128)(2,1)S(1)}, u32[]{:S(2)}, u32[]{:S(2)}) collective-permute-start(bf16[48,2304]{1,0:T(8,128)(2,1)S(1)} %bitcast.50), channel_id=1, source_target_pairs={{0,16},{16,0},{1,17},{17,1},{2,18},{18,2},{3,19},{19,3},{4,20},{20... | collective-permute-start | bytes 663560 | tf_op jit(solution)/shard_map/ppermute | solution.py:25
  194.9 9.1 %collective-permute-start.26 = (bf16[1,48,896]{2,1,0:T(8,128)(2,1)S(1)}, bf16[1,48,896]{2,1,0:T(8,128)(2,1)S(1)}, u32[]{:S(2)}, u32[]{:S(2)}) collective-permute-start(bf16[1,48,896]{2,1,0:T(8,128)(2,1)S(1)} %add_convert_fusion.18), channel_id=1, source_target_pairs={{0,8},{1,9},{2,10},{3,11},{4,12},{5,13},{6,14},{7,15},{8,0},{9,1},... | collective-permute-start | bytes 258056 | tf_op jit(solution)/shard_map/ppermute | solution.py:25
  196.6 8.0 %collective-permute-start.29 = (bf16[48,1536]{1,0:T(8,128)(2,1)S(1)}, bf16[48,1536]{1,0:T(8,128)(2,1)S(1)}, u32[]{:S(2)}, u32[]{:S(2)}) collective-permute-start(bf16[48,1536]{1,0:T(8,128)(2,1)S(1)} %bitcast.52), channel_id=1, source_target_pairs={{0,16},{16,0},{1,17},{17,1},{2,18},{18,2},{3,19},{19,3},{4,20},{20... | collective-permute-start | bytes 442376 | tf_op jit(solution)/shard_map/ppermute | solution.py:25
  202.5 5.7 %collective-permute-start.25 = (bf16[48,1536]{1,0:T(8,128)(2,1)S(1)}, bf16[48,1536]{1,0:T(8,128)(2,1)S(1)}, u32[]{:S(2)}, u32[]{:S(2)}) collective-permute-start(bf16[48,1536]{1,0:T(8,128)(2,1)S(1)} %bitcast.54), channel_id=1, source_target_pairs={{0,16},{16,0},{1,17},{17,1},{2,18},{18,2},{3,19},{19,3},{4,20},{20... | collective-permute-start | bytes 442376 | tf_op jit(solution)/shard_map/ppermute | solution.py:25
  204.0 5.0 %collective-permute-start.27 = (bf16[48,896]{1,0:T(8,128)(2,1)S(1)}, bf16[48,896]{1,0:T(8,128)(2,1)S(1)}, u32[]{:S(2)}, u32[]{:S(2)}) collective-permute-start(bf16[48,896]{1,0:T(8,128)(2,1)S(1)} %bitcast.57), channel_id=1, source_target_pairs={{0,16},{16,0},{1,17},{17,1},{2,18},{18,2},{3,19},{19,3},{4,20},{20... | collective-permute-start | bytes 258056 | tf_op jit(solution)/shard_map/ppermute | solution.py:25
  (32 other events, 46.2 us)

commit v2 on v1

--- a/solution.py
+++ b/solution.py
@@ -49,7 +49,9 @@
 
 
 def call(kernel, scalars, operands, in_specs, out_specs, out_shape, grid, name, **more):
-    after = list(LINE)
+    after = LINE[1:]
+    if LINE:
+        after.append(pltpu.with_memory_space_constraint(LINE[0], pltpu.HBM))
     scratch = list(more.get("scratch", ()))
     taken, given = len(operands), len(out_shape)
 
@@ -57,12 +59,14 @@
         outs = refs[taken + len(after) :]
         kernel(scalars_ref, *refs[:taken], *outs[:given], *outs[given + 1 :])
 
-    placed = [
-        pltpu.with_memory_space_constraint(array, pltpu.VMEM if spec is RESIDENT else pltpu.HBM)
-        for array, spec in zip(operands + after, list(in_specs) + [ANY] * len(after))
-    ]
+    placed = []
+    for i, (array, spec) in enumerate(zip(operands, in_specs)):
+        if i not in more.get("anywhere", ()):
+            space = pltpu.VMEM if spec is RESIDENT else pltpu.HBM
+            array = pltpu.with_memory_space_constraint(array, space)
+        placed.append(array)
     shapes = [
-        pltpu.VMEM(shape.shape, shape.dtype) if spec is RESIDENT else shape
+        (pltpu.VMEM if spec is RESIDENT else pltpu.HBM)(shape.shape, shape.dtype)
         for shape, spec in zip(out_shape, out_specs)
     ]
     outs = pl.pallas_call(
@@ -74,13 +78,13 @@
             out_specs=list(out_specs) + [ANY],
             scratch_shapes=scratch,
         ),
-        out_shape=shapes + [jax.ShapeDtypeStruct((8, 128), F32)],
+        out_shape=shapes + [pltpu.HBM((8, 128), F32)],
         compiler_params=params(more.get("limit", VMEM_LIMIT)),
         cost_estimate=pl.CostEstimate(
             flops=more.get("work", 4 * 10**9), bytes_accessed=2**20, transcendentals=0
         ),
         name=name,
-    )(scalars, *placed)
+    )(scalars, *placed, *after)
     LINE[:] = [outs[-1]]
     return list(outs[:-1])
 
@@ -114,6 +118,8 @@
 
 def gather_sent(partner, rows, half, first, count):
     slot_rows, width = rows.shape[1:]
+
+    partner = pltpu.with_memory_space_constraint(partner, pltpu.HBM)
 
     def kernel(partner_ref, rows_ref, out, sems):
         side = lax.axis_index("mod")
@@ -173,7 +179,8 @@
         [jax.ShapeDtypeStruct(shape, kept.dtype)],
         (1,),
         "scatter_home",
-        work=2 * 10**10,
+        anywhere=(1,),
+        work=10**7,
         scratch=[pltpu.SemaphoreType.DMA((2, half))],
     )[0]
 
@@ -261,7 +268,7 @@
             cols = slice(first_block * duo, (first_block + count) * duo)
             at = 3 * first_block * duo
             for value in (queries, keys, values):
-                mixed_out[rows_here, at : at + count * duo] = value[:, cols]
+                mixed_out[:, at : at + count * duo] = value[:, cols]
                 at += count * duo
         contexts = []
         for pair in range(2):
@@ -275,7 +282,7 @@
                 powered = jnp.exp(scores - jnp.max(scores, axis=-1, keepdims=True))
                 low_probs = powered * (1.0 / jnp.sum(powered, axis=-1, keepdims=True))
                 low_probs = low_probs.astype(BF16)
-                probs_out[2 * step + pair, block] = low_probs
+                probs_out[pair, block] = low_probs
                 heads.append(
                     dot(side_by_side(low_probs), split_heads(values[span, cols])).astype(BF16)
                 )
@@ -306,7 +313,14 @@
             whole(norm_gains),
             whole(bias_rows),
         ],
-        [RESIDENT] * 6,
+        [
+            RESIDENT,
+            pl.BlockSpec((2 * length, 3 * width), lambda i, s: (i, 0)),
+            pl.BlockSpec((2, blocks, 2 * length, length), lambda i, s: (i, 0, 0, 0)),
+            RESIDENT,
+            RESIDENT,
+            RESIDENT,
+        ],
         [
             jax.ShapeDtypeStruct((total, width), BF16),
             jax.ShapeDtypeStruct((total, 3 * width), BF16),
@@ -317,6 +331,7 @@
         ],
         (pairs // 2,),
         "attention_forward",
+        limit=16 * 2**20,
         work=4 * 10**10,
     )
 
@@ -478,6 +493,8 @@
         ],
         (steps + parts,),
         "feed_forward",
+        limit=18 * 2**20,
+        anywhere=(3,),
         scratch=[
             pltpu.VMEM((rows, width), F32),
             pltpu.VMEM((height, inner_width), BF16),
@@ -608,6 +625,7 @@
         ],
         (steps + 1,),
         "feed_backward",
+        limit=21 * 2**20,
         scratch=[
             pltpu.VMEM((total, width), F32),
             pltpu.VMEM((total, width), BF16),
@@ -656,12 +674,11 @@
         low_attn = low_attn_ref[here]
         w_out_rows = slice(first_block * duo, (first_block + mine) * duo)
         d_context = dot(low_attn, w_out_ref[w_out_rows, :], 1, 1).astype(BF16)
-        at = 3 * first_block * duo
-        mixed = mixed_ref[here, at : at + 3 * span_cols]
+        mixed = mixed_ref[...]
         rows = []
         for pair in range(2):
             span = slice(pair * length, (pair + 1) * length)
-            chosen = [probs_ref[2 * step + pair, first_block + block] for block in range(mine)]
+            chosen = [probs_ref[pair, block] for block in range(mine)]
             parts = []
             for third in range(3):
                 first = third * span_cols
@@ -712,15 +729,29 @@
             grad[:, : 3 * span_cols] = dot(joined_ref[...], held[...], 0, 0).astype(BF16)
             if last:
                 first, second = sums_ref[0:2, :], sums_out[0:2, :]
+                count = inner.shape[1] // width
                 small = [jnp.concatenate([first, second], 1), one[0:1], two[0:1]]
-                small += [one[2:3], one[1:2], two[2:3], two[1:2], inner[...]]
-                small.append(jnp.zeros((120 - inner.shape[0], width), F32))
+                small += [one[2:3], one[1:2], two[2:3], two[1:2]]
+                for at in range(count):
+                    runs = [
+                        inner[0:1, (start * count + at) * shard : (start * count + at + 1) * shard]
+                        for start in range(shards)
+                    ]
+                    small.append(jnp.concatenate(runs, 1))
+                small.append(jnp.zeros((120 - count, width), F32))
                 grad[:, 3 * span_cols :] = jnp.concatenate(small, 0).T.astype(BF16)
             spread(grad, (send, keep), scalars_ref, base, shard, order)
 
     two_slots = pl.BlockSpec((2, slot_rows, width), lambda i, s: (i, 0, 0))
     operands = [low_attn, mixed, probs, joined, w_out]
-    in_specs = [RESIDENT] * 5
+    skip = first_block // mine
+    in_specs = [
+        RESIDENT,
+        pl.BlockSpec((2 * length, 3 * span_cols), lambda i, s: (i, skip)),
+        pl.BlockSpec((2, mine, 2 * length, length), lambda i, s: (i, skip, 0, 0)),
+        RESIDENT,
+        RESIDENT,
+    ]
     grads = pl.BlockSpec((places, shard, columns), lambda i, s: (0, 0, 0))
     out_specs = [pl.BlockSpec((8, span_cols), lambda i, s: (0, 0)), grads, grads]
     out_shape = [
@@ -746,6 +777,7 @@
         out_shape,
         (steps,),
         "attention_backward",
+        limit=16 * 2**20,
         scratch=[pltpu.VMEM((total, 3 * span_cols), BF16)] * last
         + [pltpu.VMEM((width, columns), BF16)],
     )
@@ -824,6 +856,7 @@
         [jax.ShapeDtypeStruct(shape, F32) for shape in shapes],
         (1,),
         "finish_qkv",
+        anywhere=(0, 1, 2, 3),
     )
 
 
@@ -918,16 +951,15 @@
         back_weights,
         layout,
         groups,
-        (other, path),
+        (path, other),
     )
     shard = width // shards
     count = inner_width // width
-    inner_sum = inner_sum[0].reshape(shards, count, shard).transpose(1, 0, 2).reshape(count, width)
     if aligned:
         back.step()
         out_back = in_turn(out_back)
         pause(scalars)
-        inner_a, inner_b = Shards(*inner[:2], other), Shards(*inner[2:], path)
+        inner_a, inner_b = Shards(*inner[:2], path), Shards(*inner[2:], other)
         inner_a.step()
         inner_b.step()
     attn_kept = (low_attn, mixed, probs, joined)
@@ -937,10 +969,13 @@
     if aligned:
         back.step()
         inner_a.step()
-        inner_b.step()
         pause(scalars)
         qkv_a = Shards(*qkv_a, path)
         qkv_a.step()
+    if layout != shards:
+        inner_sum = inner_sum.reshape(8, shards, count, shard).transpose(0, 2, 1, 3)
+        inner_sum = inner_sum.reshape(8, count, layout, width // layout).transpose(0, 2, 1, 3)
+        inner_sum = inner_sum.reshape(8, inner_width)
     sums = (sums_one, sums_two, inner_sum, sums_qv)
     d_kept, d_far, _, *qkv_b = attention_backward(
         scalars, attn_kept, attn_weights, 1, layout, groups, path, d_mixed, sums
@@ -948,18 +983,19 @@
     d_back = flipped(d_far, "mod", 1)
     if aligned:
         qkv_b = Shards(*qkv_b, path)
+        back.step()
         inner_b.step()
+        inner_a.step()
         qkv_b.step()
         qkv_a.step()
-        inner_a.step()
-        back.step()
         out_rows = scatter_home(scalars, out_kept, out_back, half).reshape(1, -1, width)
-        qkv_b.step()
-        qkv_a.step()
         inner_b.step()
         qkv_b.step()
         inner_a.step()
+        qkv_a.step()
         grad_back = back.result()
+        qkv_b.step()
+        inner_b.step()
         grad_rows = scatter_home(scalars, d_kept, d_back, half).reshape(1, -1, width)
         qkv_a.step()
         qkv_b.step()
@@ -968,7 +1004,7 @@
     else:
         out_rows = scatter_home(scalars, out_kept, out_back, half).reshape(1, -1, width)
         grad_back = reduce_plain(*back, path)
-        inner_a, inner_b = reduce_plain(*inner[:2], other), reduce_plain(*inner[2:], path)
+        inner_a, inner_b = reduce_plain(*inner[:2], path), reduce_plain(*inner[2:], other)
         qkv_a, qkv_b = reduce_plain(*qkv_a, path), reduce_plain(*qkv_b, path)
         grad_rows = scatter_home(scalars, d_kept, d_back, half).reshape(1, -1, width)
         columns = (qkv_a.shape[1] // 3, (qkv_b.shape[1] - 128) // 3)

time: 213 us -> 200 us (0.939)
  local copies, waits for them, and re-layouts: 22.2 us -> 3.52 us
  starting transfers between devices: 30.9 us -> 41.7 us
  waiting for transfers between devices: 42.1 us -> 32.6 us
  Pallas kernels: 106 us -> 114 us
  other arithmetic: 10.8 us -> 6.6 us
    unnamed x100 -> x26, local copies, waits for them, and re-layouts: 16.5 us -> 0.8 us
    ppermute x30, starting transfers between devices: 30.9 us -> 41.7 us  [flipped(): return lax.ppermute(value, axis, pairs)]
    ppermute x30, waiting for transfers between devices: 42.1 us -> 32.6 us  [flipped(): return lax.ppermute(value, axis, pairs)]
    pallas_call x14, Pallas kernels: 106 us -> 114 us  [call(): pl.pallas_call(wrapped, grid_spec=pltpu.PrefetchScalarGridSpec(num_scalar...]
    convert_element_type x20, other arithmetic: 8.03 us -> 3.96 us  [step(): total = total.astype(BF16)]
  transfers between devices with their start and end apart: 30 -> 30, of which waited for: 12 -> 12; matrix products, arithmetic and copies ran while one was open for 7% -> 3% of each run, Pallas kernels for 36% -> 43%
where the time goes in v2:
time: 200 us; the launch traced here: 199 us
  Pallas kernels  114 us (57%)
  starting transfers between devices  41.7 us (21%)
  waiting for transfers between devices  32.6 us (16%)
  other arithmetic  6.6 us (3%)
  local copies, waits for them, and re-layouts  3.52 us (2%)
    pallas_call x14, Pallas kernels, call(): pl.pallas_call(wrapped, grid_spec=pltpu.PrefetchScalarGridSpec(num_scalar...  114 us
    ppermute x30, starting transfers between devices, flipped(): return lax.ppermute(value, axis, pairs)  41.7 us
    ppermute x30, waiting for transfers between devices, flipped(): return lax.ppermute(value, axis, pairs)  32.6 us
  transfers between devices with their start and end apart: 30, of which 12 were waited for; matrix products, arithmetic and copies ran while one was open for 3% of the time, Pallas kernels for 43%

profile of v2, /device:TPU:0, one launch (start us, length us, event | category | flops | bytes accessed | tf_op | source)
XLA Modules:
  0.0 199.2 jit_solution(6478441397605490695)
XLA Ops:
  0.6 2.5 %gather_sent.3 = (bf16[4,64,768]{2,1,0:T(8,128)(2,1)}, f32[8,128]{1,0:T(8,128)}) custom-call(s32[16]{0:T(128)} %bitcast.50, bf16[16,64,768]{2,1,0:T(8,128)(2,1)} %bitcast.34), custom_call_target="tpu_custom_call" | custom-call | flops 10000000 | bytes 1048576 | tf_op jit(solution)/shard_map/gather_sent/pallas_call | solution.py:72
  3.1 3.0 %collective-permute-start = (bf16[4,64,768]{2,1,0:T(8,128)(2,1)}, bf16[4,64,768]{2,1,0:T(8,128)(2,1)S(1)}, u32[]{:S(2)}, u32[]{:S(2)}) collective-permute-start(bf16[4,64,768]{2,1,0:T(8,128)(2,1)} %get-tuple-element.115), channel_id=1, source_target_pairs={{0,16},{16,0},{1,17},{17,1},{2,18},{18,2},{3,19},{19,3},{4,20},{20... | collective-permute-start | bytes 1179656 | tf_op jit(solution)/shard_map/ppermute | solution.py:25
  6.2 2.6 %gather_sent.4 = (bf16[4,64,768]{2,1,0:T(8,128)(2,1)}, f32[8,128]{1,0:T(8,128)}) custom-call(s32[16]{0:T(128)} %bitcast.51, bf16[16,64,768]{2,1,0:T(8,128)(2,1)} %bitcast.35, f32[8,128]{1,0:T(8,128)} %get-tuple-element.116.refs_1_), custom_call_target="tpu_custom_call" | custom-call | flops 10000000 | bytes 1048576 | tf_op jit(solution)/shard_map/gather_sent/pallas_call | solution.py:72
  8.9 2.8 %gather_sent.5 = (bf16[8,64,768]{2,1,0:T(8,128)(2,1)}, f32[8,128]{1,0:T(8,128)}) custom-call(s32[16]{0:T(128)} %bitcast.52, bf16[16,64,768]{2,1,0:T(8,128)(2,1)} %bitcast.31, f32[8,128]{1,0:T(8,128)} %get-tuple-element.117.refs_1_), custom_call_target="tpu_custom_call" | custom-call | flops 10000000 | bytes 1048576 | tf_op jit(solution)/shard_map/gather_sent/pallas_call | solution.py:72
  11.7 4.6 %collective-permute-done.refs_2_ = bf16[4,64,768]{2,1,0:T(8,128)(2,1)S(1)} collective-permute-done((bf16[4,64,768]{2,1,0:T(8,128)(2,1)}, bf16[4,64,768]{2,1,0:T(8,128)(2,1)S(1)}, u32[]{:S(2)}, u32[]{:S(2)}) %collective-permute-start) | collective-permute-done | bytes 393248 | tf_op jit(solution)/shard_map/ppermute | solution.py:25
  16.4 2.1 %collective-permute-start.2 = (bf16[8,64,768]{2,1,0:T(8,128)(2,1)}, bf16[8,64,768]{2,1,0:T(8,128)(2,1)S(1)}, u32[]{:S(2)}, u32[]{:S(2)}) collective-permute-start(bf16[8,64,768]{2,1,0:T(8,128)(2,1)} %get-tuple-element.128), channel_id=1, source_target_pairs={{0,16},{16,0},{1,17},{17,1},{2,18},{18,2},{3,19},{19,3},{4,20},{20... | collective-permute-start | bytes 2359304 | tf_op jit(solution)/shard_map/ppermute | solution.py:25
  19.3 5.7 %fetch.1 = (bf16[768,2304]{1,0:T(8,128)(2,1)S(1)}, bf16[768,768]{1,0:T(8,128)(2,1)S(1)}, bf16[768,3072]{1,0:T(8,128)(2,1)S(1)}, bf16[3072,768]{1,0:T(8,128)(2,1)S(1)}, f32[8,128]{1,0:T(8,128)}) custom-call(s32[19]{0:T(128)S(1)} %pad_add_fusion.1.scalars_ref, bf16[768,2304]{1,0:T(8,128)(2,1)} %refs_0_.1, bf16[768,768]{1,0:T(8,128)(2,1)} %refs_1_.1, ...), custom_call_target="tpu_custom_call" | custom-call | flops 10000000 | bytes 1048576 | tf_op jit(solution)/shard_map/fetch/pallas_call | solution.py:72
  26.5 14.8 %attention_forward.1 = (bf16[1024,768]{1,0:T(8,128)(2,1)S(1)}, bf16[1024,2304]{1,0:T(8,128)(2,1)}, bf16[8,6,256,128]{3,2,1,0:T(8,128)(2,1)}, bf16[1024,768]{1,0:...) custom-call(s32[19]{0:T(128)S(1)} %pad_add_fusion.1.scalars_ref, ...), custom_call_target="tpu_custom_call" | custom-call | flops 40000000000 | bytes 1048576 | tf_op jit(solution)/shard_map/attention_forward/pallas_call | solution.py:72
  41.3 25.2 %feed_forward.1 = (bf16[1024,3072]{1,0:T(8,128)(2,1)S(1)}, bf16[1024,768]{1,0:T(8,128)(2,1)S(1)}, bf16[8,64,768]{2,1,0:T(8,128)(2,1)}, bf16[8,64,768]{2,1,0:T(8,...) custom-call(s32[19]{0:T(128)S(1)} %pad_add_fusion.1.scalars_ref, ...), custom_call_target="tpu_custom_call" | custom-call | flops 4000000000 | bytes 1048576 | tf_op jit(solution)/shard_map/feed_forward/pallas_call | solution.py:72
  66.6 4.7 %collective-permute-done.4 = bf16[2,4,192,768]{3,2,1,0:T(8,128)(2,1)S(1)} collective-permute-done((bf16[2,4,192,768]{3,2,1,0:T(8,128)(2,1)}, bf16[2,4,192,768]{3,2,1,0:T(8,128)(2,1)S(1)}, u32[]{:S(2)}, u32[]{:S(2)}) %collective-permute-start.4) | collective-permute-done | bytes 2359328 | tf_op jit(solution)/shard_map/ppermute | solution.py:25
  71.3 1.7 fusion.refs_9_
  73.0 1.6 collective-permute-start.5
  74.5 1.2 collective-permute-start.3
  75.7 23.8 %feed_backward.1 = (bf16[1024,768]{1,0:T(8,128)(2,1)S(1)}, f32[8,768]{1,0:T(8,128)}, f32[8,3072]{1,0:T(8,128)}, bf16[8,48,1536]{2,1,0:T(8,128)(2,1)}, bf16[8,48,...) custom-call(s32[19]{0:T(128)S(1)} %pad_add_fusion.1.scalars_ref, ...), custom_call_target="tpu_custom_call" | custom-call | flops 4000000000 | bytes 1048576 | tf_op jit(solution)/shard_map/feed_backward/pallas_call | solution.py:72
  100.0 1.0 collective-permute-done.5
  101.3 1.7 collective-permute-start.10
  103.7 1.6 collective-permute-start.9
  105.5 1.5 collective-permute-start.14
  107.0 12.3 %attention_backward.2 = (bf16[1024,1536]{1,0:T(8,128)(2,1)S(1)}, f32[8,512]{1,0:T(8,128)}, bf16[8,48,1536]{2,1,0:T(8,128)(2,1)}, bf16[8,48,1536]{2,1,0:T(8,128)(2,1)}, f32[8,128]{1,0:T(8,128)}) custom-call(s32[19]{0:T(128)S(1)} %pad_add_fusion.1.scalars_ref, bf16[1024,768]{1,0:T(8,128)(2,1)S(1)} %get-tuple-element.147.refs_0_, ...), custom_call_target="tpu_custom_call" | custom-call | flops 4000000000 | bytes 1048576 | tf_op jit(solution)/shard_map/attention_backward/pallas_call | solution.py:72
  119.5 2.6 %collective-permute-start.15 = (bf16[1,192,768]{2,1,0:T(8,128)(2,1)S(1)}, bf16[1,192,768]{2,1,0:T(8,128)(2,1)S(1)}, u32[]{:S(2)}, u32[]{:S(2)}) collective-permute-start(bf16[1,192,768]{2,1,0:T(8,128)(2,1)S(1)} %add_convert_fusion.9), channel_id=1, source_target_pairs={{0,8},{1,9},{2,10},{3,11},{4,12},{5,13},{6,14},{7,15},{8,0},{9,1},... | collective-permute-start | bytes 884744 | tf_op jit(solution)/shard_map/ppermute | solution.py:25
  123.4 2.3 %collective-permute-done.8 = bf16[8,48,1536]{2,1,0:T(8,128)(2,1)S(1)} collective-permute-done((bf16[8,48,1536]{2,1,0:T(8,128)(2,1)S(1)}, bf16[8,48,1536]{2,1,0:T(8,128)(2,1)S(1)}, u32[]{:S(2)}, u32[]{:S(2)}) %collective-permute-start.8) | collective-permute-done | bytes 1179680 | tf_op jit(solution)/shard_map/ppermute | solution.py:25
  125.9 1.3 collective-permute-start.11
  127.2 14.2 %attention_backward.3 = (bf16[8,64,768]{2,1,0:T(8,128)(2,1)}, bf16[8,64,768]{2,1,0:T(8,128)(2,1)}, f32[8,256]{1,0:T(8,128)}, bf16[8,48,896]{2,1,0:T(8,128)(2,1)}...) custom-call(s32[19]{0:T(128)S(1)} %pad_add_fusion.1.scalars_ref, bf16[1024,768]{1,0:T(8,128)(2,1)S(1)} %get-tuple-element.147.refs_0_, ...), custom_call_target="tpu_custom_call" | custom-call | flops 4000000000 | bytes 1048576 | tf_op jit(solution)/shard_map/attention_backward/pallas_call | solution.py:72
  142.9 1.2 collective-permute-start.21
  144.2 1.6 collective-permute-start.17
  145.8 1.7 collective-permute-done.13
  147.6 2.7 %collective-permute-start.23 = (bf16[1,48,1536]{2,1,0:T(8,128)(2,1)S(1)}, bf16[1,48,1536]{2,1,0:T(8,128)(2,1)S(1)}, u32[]{:S(2)}, u32[]{:S(2)}) collective-permute-start(bf16[1,48,1536]{2,1,0:T(8,128)(2,1)S(1)} %add_convert_fusion.16), channel_id=1, source_target_pairs={{0,8},{1,9},{2,10},{3,11},{4,12},{5,13},{6,14},{7,15},{8,0},{9,1},... | collective-permute-start | bytes 442376 | tf_op jit(solution)/shard_map/ppermute | solution.py:25
  150.2 1.2 collective-permute-start.16
  151.6 1.7 collective-permute-start.22
  153.3 3.7 %scatter_home.2 = (bf16[16,64,768]{2,1,0:T(8,128)(2,1)}, f32[8,128]{1,0:T(8,128)}) custom-call(s32[19]{0:T(128)S(1)} %pad_add_fusion.1.scalars_ref, bf16[8,64,768]{2,1,0:T(8,128)(2,1)} %get-tuple-element.132.refs_0_, bf16[8,64,768]{2,1,0:T(8,128)(2,1)S(1)} %collective-permute-done.3.refs_1_, bf16[2,48,1536]{2,1,0:T(8,128)(2,1)S(1)} %add_convert_fusion.6.refs_2_, ...), custom_call_target="tpu_custom_call" | custom-call | flops 10000000 | bytes 1048576 | tf_op jit(solution)/shard_map/scatter_home/pallas_call | solution.py:72
  157.0 1.6 collective-permute-start.19
  158.7 7.9 %collective-permute-done.19 = bf16[4,48,896]{2,1,0:T(8,128)(2,1)S(1)} collective-permute-done((bf16[4,48,896]{2,1,0:T(8,128)(2,1)S(1)}, bf16[4,48,896]{2,1,0:T(8,128)(2,1)S(1)}, u32[]{:S(2)}, u32[]{:S(2)}) %collective-permute-start.19) | collective-permute-done | bytes 344096 | tf_op jit(solution)/shard_map/ppermute | solution.py:25
  166.6 2.8 %collective-permute-start.18 = (bf16[1,48,2304]{2,1,0:T(8,128)(2,1)S(1)}, bf16[1,48,2304]{2,1,0:T(8,128)(2,1)S(1)}, u32[]{:S(2)}, u32[]{:S(2)}) collective-permute-start(bf16[1,48,2304]{2,1,0:T(8,128)(2,1)S(1)} %add_convert_fusion.11), channel_id=1, source_target_pairs={{0,8},{1,9},{2,10},{3,11},{4,12},{5,13},{6,14},{7,15},{8,0},{9,1},... | collective-permute-start | bytes 663560 | tf_op jit(solution)/shard_map/ppermute | solution.py:25
  169.4 1.4 collective-permute-start.20
  171.1 1.7 collective-permute-start.24
  172.8 0.9 collective-permute-start.29
  173.6 0.9 convert_add_fusion.1
  174.5 3.9 %collective-permute-done.20 = bf16[2,48,896]{2,1,0:T(8,128)(2,1)S(1)} collective-permute-done((bf16[2,48,896]{2,1,0:T(8,128)(2,1)S(1)}, bf16[2,48,896]{2,1,0:T(8,128)(2,1)S(1)}, u32[]{:S(2)}, u32[]{:S(2)}) %collective-permute-start.20) | collective-permute-done | bytes 172064 | tf_op jit(solution)/shard_map/ppermute | solution.py:25
  178.4 4.1 %collective-permute-start.26 = (bf16[1,48,896]{2,1,0:T(8,128)(2,1)S(1)}, bf16[1,48,896]{2,1,0:T(8,128)(2,1)S(1)}, u32[]{:S(2)}, u32[]{:S(2)}) collective-permute-start(bf16[1,48,896]{2,1,0:T(8,128)(2,1)S(1)} %add_convert_fusion.18), channel_id=1, source_target_pairs={{0,8},{1,9},{2,10},{3,11},{4,12},{5,13},{6,14},{7,15},{8,0},{9,1},... | collective-permute-start | bytes 258056 | tf_op jit(solution)/shard_map/ppermute | solution.py:25
  182.5 2.1 %collective-permute-done.18 = bf16[1,48,2304]{2,1,0:T(8,128)(2,1)S(1)} collective-permute-done((bf16[1,48,2304]{2,1,0:T(8,128)(2,1)S(1)}, bf16[1,48,2304]{2,1,0:T(8,128)(2,1)S(1)}, u32[]{:S(2)}, u32[]{:S(2)}) %collective-permute-start.18) | collective-permute-done | bytes 221216 | tf_op jit(solution)/shard_map/ppermute | solution.py:25
  184.8 0.9 collective-permute-start.28
  185.7 3.7 %scatter_home.3 = (bf16[16,64,768]{2,1,0:T(8,128)(2,1)}, f32[8,128]{1,0:T(8,128)}) custom-call(s32[19]{0:T(128)S(1)} %pad_add_fusion.1.scalars_ref, bf16[8,64,768]{2,1,0:T(8,128)(2,1)} %get-tuple-element.188.refs_0_, bf16[8,64,768]{2,1,0:T(8,128)(2,1)S(1)} %collective-permute-done.16.refs_1_, bf16[1,48,2304]{2,1,0:T(8,128)(2,1)S(1)} %add_convert_fusion.10.refs_2_, ...), custom_call_target="tpu_custom_call" | custom-call | flops 10000000 | bytes 1048576 | tf_op jit(solution)/shard_map/scatter_home/pallas_call | solution.py:72
  189.6 1.2 collective-permute-start.25
  190.9 0.9 collective-permute-start.27
  192.6 2.2 %collective-permute-done.25.refs_1_ = bf16[48,1536]{1,0:T(8,128)(2,1)S(1)} collective-permute-done((bf16[48,1536]{1,0:T(8,128)(2,1)S(1)}, bf16[48,1536]{1,0:T(8,128)(2,1)S(1)}, u32[]{:S(2)}, u32[]{:S(2)}) %collective-permute-start.25) | collective-permute-done | bytes 147488 | tf_op jit(solution)/shard_map/ppermute | solution.py:25
  194.8 0.9 collective-permute-done.27.refs_3_
  195.7 1.4 finish_qkv.1
  197.0 1.3 reshape.80
  (88 shorter events, 10.0 us)
Async XLA Ops:
  3.1 13.2 %collective-permute-start = (bf16[4,64,768]{2,1,0:T(8,128)(2,1)}, bf16[4,64,768]{2,1,0:T(8,128)(2,1)S(1)}, u32[]{:S(2)}, u32[]{:S(2)}) collective-permute-start(bf16[4,64,768]{2,1,0:T(8,128)(2,1)} %get-tuple-element.115), channel_id=1, source_target_pairs={{0,16},{16,0},{1,17},{17,1},{2,18},{18,2},{3,19},{19,3},{4,20},{20... | collective-permute-start | bytes 1179656 | tf_op jit(solution)/shard_map/ppermute | solution.py:25
  6.1 10.2 %copy-start.5 = (s32[1,16]{1,0:T(1,128)S(1)}, s32[1,16]{1,0:T(1,128)}, u32[]{:S(2)}) copy-start(s32[1,16]{1,0:T(1,128)} %param.15) | copy-start | bytes 196
  6.1 10.2 %copy-start.6 = (s32[2,1024]{1,0:T(2,128)S(1)}, s32[2,1024]{1,0:T(2,128)}, u32[]{:S(2)}) copy-start(s32[2,1024]{1,0:T(2,128)} %param.14) | copy-start | bytes 24580
  8.8 16.9 %collective-permute-start.1 = (bf16[4,64,768]{2,1,0:T(8,128)(2,1)}, bf16[4,64,768]{2,1,0:T(8,128)(2,1)S(1)}, u32[]{:S(2)}, u32[]{:S(2)}) collective-permute-start(bf16[4,64,768]{2,1,0:T(8,128)(2,1)} %get-tuple-element.121), channel_id=1, source_target_pairs={{0,16},{16,0},{1,17},{17,1},{2,18},{18,2},{3,19},{19,3},{4,20},{20... | collective-permute-start | bytes 1179656 | tf_op jit(solution)/shard_map/ppermute | solution.py:25
  16.3 8.7 %copy-start.11 = (bf16[4,64,768]{2,1,0:T(8,128)(2,1)}, bf16[4,64,768]{2,1,0:T(8,128)(2,1)S(1)}, u32[]{:S(2)}) copy-start(bf16[4,64,768]{2,1,0:T(8,128)(2,1)S(1)} %collective-permute-done.refs_2_) | copy-start | bytes 1179652
  16.4 24.9 %collective-permute-start.2 = (bf16[8,64,768]{2,1,0:T(8,128)(2,1)}, bf16[8,64,768]{2,1,0:T(8,128)(2,1)S(1)}, u32[]{:S(2)}, u32[]{:S(2)}) collective-permute-start(bf16[8,64,768]{2,1,0:T(8,128)(2,1)} %get-tuple-element.128), channel_id=1, source_target_pairs={{0,16},{16,0},{1,17},{17,1},{2,18},{18,2},{3,19},{19,3},{4,20},{20... | collective-permute-start | bytes 2359304 | tf_op jit(solution)/shard_map/ppermute | solution.py:25
  25.7 0.7 copy-start.12
  66.6 4.7 %collective-permute-start.4 = (bf16[2,4,192,768]{3,2,1,0:T(8,128)(2,1)}, bf16[2,4,192,768]{3,2,1,0:T(8,128)(2,1)S(1)}, u32[]{:S(2)}, u32[]{:S(2)}) collective-permute-start(bf16[2,4,192,768]{3,2,1,0:T(8,128)(2,1)} %get-tuple-element.135), channel_id=1, source_target_pairs={{0,1},{1,0},{2,3},{3,2},{4,5},{5,4},{6,7},{7,6},{8,9},{9,8},{10,11... | collective-permute-start | bytes 7077896 | tf_op jit(solution)/shard_map/ppermute | solution.py:25
  71.3 3.2 %copy-start.9 = (bf16[8,64,768]{2,1,0:T(8,128)(2,1)S(1)}, bf16[8,64,768]{2,1,0:T(8,128)(2,1)}, u32[]{:S(2)}) copy-start(bf16[8,64,768]{2,1,0:T(8,128)(2,1)} %get-tuple-element.133) | copy-start | bytes 2359300
  73.0 28.1 %collective-permute-start.5 = (bf16[4,192,768]{2,1,0:T(8,128)(2,1)S(1)}, bf16[4,192,768]{2,1,0:T(8,128)(2,1)S(1)}, u32[]{:S(2)}, u32[]{:S(2)}) collective-permute-start(bf16[4,192,768]{2,1,0:T(8,128)(2,1)S(1)} %fusion.refs_9_), channel_id=1, source_target_pairs={{0,2},{1,3},{2,0},{3,1},{4,6},{5,7},{6,4},{7,5},{8,10},{9,11},{10,... | collective-permute-start | bytes 3538952 | tf_op jit(solution)/shard_map/ppermute | solution.py:25
  74.5 28.4 %collective-permute-start.3 = (bf16[8,64,768]{2,1,0:T(8,128)(2,1)S(1)}, bf16[8,64,768]{2,1,0:T(8,128)(2,1)S(1)}, u32[]{:S(2)}, u32[]{:S(2)}) collective-permute-start(bf16[8,64,768]{2,1,0:T(8,128)(2,1)S(1)} %copy-done.9), channel_id=1, source_target_pairs={{0,16},{16,0},{1,17},{17,1},{2,18},{18,2},{3,19},{19,3},{4,20},{20... | collective-permute-start | bytes 2359304 | tf_op jit(solution)/shard_map/ppermute | solution.py:25
  75.7 25.3 %copy-start = (bf16[2,4,192,768]{3,2,1,0:T(8,128)(2,1)S(1)}, bf16[2,4,192,768]{3,2,1,0:T(8,128)(2,1)}, u32[]{:S(2)}) copy-start(bf16[2,4,192,768]{3,2,1,0:T(8,128)(2,1)} %get-tuple-element.134) | copy-start | bytes 7077892
  99.5 4.0 %collective-permute-start.7 = (bf16[8,48,1536]{2,1,0:T(8,128)(2,1)}, bf16[8,48,1536]{2,1,0:T(8,128)(2,1)S(1)}, u32[]{:S(2)}, u32[]{:S(2)}) collective-permute-start(bf16[8,48,1536]{2,1,0:T(8,128)(2,1)} %get-tuple-element.153), channel_id=1, source_target_pairs={{0,1},{1,0},{2,3},{3,2},{4,5},{5,4},{6,7},{7,6},{8,9},{9,8},{10,11... | collective-permute-start | bytes 3538952 | tf_op jit(solution)/shard_map/ppermute | solution.py:25
  99.5 5.7 %collective-permute-start.6 = (bf16[8,48,2304]{2,1,0:T(8,128)(2,1)}, bf16[8,48,2304]{2,1,0:T(8,128)(2,1)S(1)}, u32[]{:S(2)}, u32[]{:S(2)}) collective-permute-start(bf16[8,48,2304]{2,1,0:T(8,128)(2,1)} %get-tuple-element.152), channel_id=1, source_target_pairs={{0,1},{1,0},{2,3},{3,2},{4,5},{5,4},{6,7},{7,6},{8,9},{9,8},{10,11... | collective-permute-start | bytes 5308424 | tf_op jit(solution)/shard_map/ppermute | solution.py:25
  101.3 2.3 %copy-start.3 = (bf16[8,48,1536]{2,1,0:T(8,128)(2,1)S(1)}, bf16[8,48,1536]{2,1,0:T(8,128)(2,1)}, u32[]{:S(2)}) copy-start(bf16[8,48,1536]{2,1,0:T(8,128)(2,1)} %get-tuple-element.156) | copy-start | bytes 3538948
  101.3 18.0 %collective-permute-start.10 = (bf16[2,192,768]{2,1,0:T(8,128)(2,1)S(1)}, bf16[2,192,768]{2,1,0:T(8,128)(2,1)S(1)}, u32[]{:S(2)}, u32[]{:S(2)}) collective-permute-start(bf16[2,192,768]{2,1,0:T(8,128)(2,1)S(1)} %add_convert_fusion.3), channel_id=1, source_target_pairs={{0,4},{1,5},{2,6},{3,7},{4,0},{5,1},{6,2},{7,3},{8,12},{9,13},{10,... | collective-permute-start | bytes 1769480 | tf_op jit(solution)/shard_map/ppermute | solution.py:25
  103.5 1.8 copy-start.1
  103.7 18.4 %collective-permute-start.9 = (bf16[4,48,1536]{2,1,0:T(8,128)(2,1)S(1)}, bf16[4,48,1536]{2,1,0:T(8,128)(2,1)S(1)}, u32[]{:S(2)}, u32[]{:S(2)}) collective-permute-start(bf16[4,48,1536]{2,1,0:T(8,128)(2,1)S(1)} %add_convert_fusion.2), channel_id=1, source_target_pairs={{0,2},{1,3},{2,0},{3,1},{4,6},{5,7},{6,4},{7,5},{8,10},{9,11},{10,... | collective-permute-start | bytes 1769480 | tf_op jit(solution)/shard_map/ppermute | solution.py:25
  105.5 37.4 %collective-permute-start.14 = (bf16[4,48,2304]{2,1,0:T(8,128)(2,1)S(1)}, bf16[4,48,2304]{2,1,0:T(8,128)(2,1)S(1)}, u32[]{:S(2)}, u32[]{:S(2)}) collective-permute-start(bf16[4,48,2304]{2,1,0:T(8,128)(2,1)S(1)} %add_convert_fusion.refs_5_), channel_id=1, source_target_pairs={{0,4},{1,5},{2,6},{3,7},{4,0},{5,1},{6,2},{7,3},{8,12},{9,13},{10,... | collective-permute-start | bytes 2654216 | tf_op jit(solution)/shard_map/ppermute | solution.py:25
  119.3 3.6 %copy-start.7 = (bf16[8,48,1536]{2,1,0:T(8,128)(2,1)S(1)}, bf16[8,48,1536]{2,1,0:T(8,128)(2,1)}, u32[]{:S(2)}) copy-start(bf16[8,48,1536]{2,1,0:T(8,128)(2,1)} %get-tuple-element.161) | copy-start | bytes 3538948
  119.5 22.5 %collective-permute-start.15 = (bf16[1,192,768]{2,1,0:T(8,128)(2,1)S(1)}, bf16[1,192,768]{2,1,0:T(8,128)(2,1)S(1)}, u32[]{:S(2)}, u32[]{:S(2)}) collective-permute-start(bf16[1,192,768]{2,1,0:T(8,128)(2,1)S(1)} %add_convert_fusion.9), channel_id=1, source_target_pairs={{0,8},{1,9},{2,10},{3,11},{4,12},{5,13},{6,14},{7,15},{8,0},{9,1},... | collective-permute-start | bytes 884744 | tf_op jit(solution)/shard_map/ppermute | solution.py:25
  122.2 25.2 %collective-permute-start.13 = (bf16[2,48,1536]{2,1,0:T(8,128)(2,1)S(1)}, bf16[2,48,1536]{2,1,0:T(8,128)(2,1)S(1)}, u32[]{:S(2)}, u32[]{:S(2)}) collective-permute-start(bf16[2,48,1536]{2,1,0:T(8,128)(2,1)S(1)} %add_convert_fusion.8.refs_0_), channel_id=1, source_target_pairs={{0,4},{1,5},{2,6},{3,7},{4,0},{5,1},{6,2},{7,3},{8,12},{9,13},{10,... | collective-permute-start | bytes 884744 | tf_op jit(solution)/shard_map/ppermute | solution.py:25
  122.9 2.9 %copy-start.2 = (bf16[8,48,1536]{2,1,0:T(8,128)(2,1)S(1)}, bf16[8,48,1536]{2,1,0:T(8,128)(2,1)}, u32[]{:S(2)}) copy-start(bf16[8,48,1536]{2,1,0:T(8,128)(2,1)} %get-tuple-element.160) | copy-start | bytes 3538948
  122.9 2.8 %collective-permute-start.8 = (bf16[8,48,1536]{2,1,0:T(8,128)(2,1)S(1)}, bf16[8,48,1536]{2,1,0:T(8,128)(2,1)S(1)}, u32[]{:S(2)}, u32[]{:S(2)}) collective-permute-start(bf16[8,48,1536]{2,1,0:T(8,128)(2,1)S(1)} %copy-done.7), channel_id=1, source_target_pairs={{0,1},{1,0},{2,3},{3,2},{4,5},{5,4},{6,7},{7,6},{8,9},{9,8},{10,11... | collective-permute-start | bytes 3538952 | tf_op jit(solution)/shard_map/ppermute | solution.py:25
  125.9 25.6 %collective-permute-start.11 = (bf16[4,48,1536]{2,1,0:T(8,128)(2,1)S(1)}, bf16[4,48,1536]{2,1,0:T(8,128)(2,1)S(1)}, u32[]{:S(2)}, u32[]{:S(2)}) collective-permute-start(bf16[4,48,1536]{2,1,0:T(8,128)(2,1)S(1)} %add_convert_fusion.1.refs_11_), channel_id=1, source_target_pairs={{0,2},{1,3},{2,0},{3,1},{4,6},{5,7},{6,4},{7,5},{8,10},{9,11},{10,... | collective-permute-start | bytes 1769480 | tf_op jit(solution)/shard_map/ppermute | solution.py:25
  141.3 2.7 %copy-start.10 = (bf16[8,48,896]{2,1,0:T(8,128)(2,1)S(1)}, bf16[8,48,896]{2,1,0:T(8,128)(2,1)}, u32[]{:S(2)}) copy-start(bf16[8,48,896]{2,1,0:T(8,128)(2,1)} %get-tuple-element.174) | copy-start | bytes 2064388
  142.2 8.0 %copy-start.8 = (bf16[8,64,768]{2,1,0:T(8,128)(2,1)S(1)}, bf16[8,64,768]{2,1,0:T(8,128)(2,1)}, u32[]{:S(2)}) copy-start(bf16[8,64,768]{2,1,0:T(8,128)(2,1)} %get-tuple-element.189) | copy-start | bytes 2359300
  142.2 9.2 %copy-start.4 = (bf16[8,48,896]{2,1,0:T(8,128)(2,1)S(1)}, bf16[8,48,896]{2,1,0:T(8,128)(2,1)}, u32[]{:S(2)}) copy-start(bf16[8,48,896]{2,1,0:T(8,128)(2,1)} %get-tuple-element.183) | copy-start | bytes 2064388
  142.9 29.9 %collective-permute-start.21 = (bf16[192,768]{1,0:T(8,128)(2,1)S(1)}, bf16[192,768]{1,0:T(8,128)(2,1)S(1)}, u32[]{:S(2)}, u32[]{:S(2)}) collective-permute-start(bf16[192,768]{1,0:T(8,128)(2,1)S(1)} %bitcast.45), channel_id=1, source_target_pairs={{0,16},{16,0},{1,17},{17,1},{2,18},{18,2},{3,19},{19,3},{4,20},{20... | collective-permute-start | bytes 884744 | tf_op jit(solution)/shard_map/ppermute | solution.py:25
  144.1 6.2 %collective-permute-start.12 = (bf16[8,48,896]{2,1,0:T(8,128)(2,1)S(1)}, bf16[8,48,896]{2,1,0:T(8,128)(2,1)S(1)}, u32[]{:S(2)}, u32[]{:S(2)}) collective-permute-start(bf16[8,48,896]{2,1,0:T(8,128)(2,1)S(1)} %copy-done.10), channel_id=1, source_target_pairs={{0,1},{1,0},{2,3},{3,2},{4,5},{5,4},{6,7},{7,6},{8,9},{9,8},{10,11... | collective-permute-start | bytes 2064392 | tf_op jit(solution)/shard_map/ppermute | solution.py:25
  144.2 12.8 %collective-permute-start.17 = (bf16[2,48,2304]{2,1,0:T(8,128)(2,1)S(1)}, bf16[2,48,2304]{2,1,0:T(8,128)(2,1)S(1)}, u32[]{:S(2)}, u32[]{:S(2)}) collective-permute-start(bf16[2,48,2304]{2,1,0:T(8,128)(2,1)S(1)} %add_convert_fusion.4), channel_id=1, source_target_pairs={{0,2},{1,3},{2,0},{3,1},{4,6},{5,7},{6,4},{7,5},{8,10},{9,11},{10,... | collective-permute-start | bytes 1327112 | tf_op jit(solution)/shard_map/ppermute | solution.py:25
  147.6 21.9 %collective-permute-start.23 = (bf16[1,48,1536]{2,1,0:T(8,128)(2,1)S(1)}, bf16[1,48,1536]{2,1,0:T(8,128)(2,1)S(1)}, u32[]{:S(2)}, u32[]{:S(2)}) collective-permute-start(bf16[1,48,1536]{2,1,0:T(8,128)(2,1)S(1)} %add_convert_fusion.16), channel_id=1, source_target_pairs={{0,8},{1,9},{2,10},{3,11},{4,12},{5,13},{6,14},{7,15},{8,0},{9,1},... | collective-permute-start | bytes 442376 | tf_op jit(solution)/shard_map/ppermute | solution.py:25
  150.2 35.5 %collective-permute-start.16 = (bf16[8,64,768]{2,1,0:T(8,128)(2,1)S(1)}, bf16[8,64,768]{2,1,0:T(8,128)(2,1)S(1)}, u32[]{:S(2)}, u32[]{:S(2)}) collective-permute-start(bf16[8,64,768]{2,1,0:T(8,128)(2,1)S(1)} %copy-done.8), channel_id=1, source_target_pairs={{0,16},{16,0},{1,17},{17,1},{2,18},{18,2},{3,19},{19,3},{4,20},{20... | collective-permute-start | bytes 2359304 | tf_op jit(solution)/shard_map/ppermute | solution.py:25
  151.6 19.4 %collective-permute-start.22 = (bf16[2,48,1536]{2,1,0:T(8,128)(2,1)S(1)}, bf16[2,48,1536]{2,1,0:T(8,128)(2,1)S(1)}, u32[]{:S(2)}, u32[]{:S(2)}) collective-permute-start(bf16[2,48,1536]{2,1,0:T(8,128)(2,1)S(1)} %add_convert_fusion.6.refs_2_), channel_id=1, source_target_pairs={{0,4},{1,5},{2,6},{3,7},{4,0},{5,1},{6,2},{7,3},{8,12},{9,13},{10,... | collective-permute-start | bytes 884744 | tf_op jit(solution)/shard_map/ppermute | solution.py:25
  157.0 9.6 %collective-permute-start.19 = (bf16[4,48,896]{2,1,0:T(8,128)(2,1)S(1)}, bf16[4,48,896]{2,1,0:T(8,128)(2,1)S(1)}, u32[]{:S(2)}, u32[]{:S(2)}) collective-permute-start(bf16[4,48,896]{2,1,0:T(8,128)(2,1)S(1)} %add_convert_fusion.5), channel_id=1, source_target_pairs={{0,2},{1,3},{2,0},{3,1},{4,6},{5,7},{6,4},{7,5},{8,10},{9,11},{10,... | collective-permute-start | bytes 1032200 | tf_op jit(solution)/shard_map/ppermute | solution.py:25
  166.6 18.1 %collective-permute-start.18 = (bf16[1,48,2304]{2,1,0:T(8,128)(2,1)S(1)}, bf16[1,48,2304]{2,1,0:T(8,128)(2,1)S(1)}, u32[]{:S(2)}, u32[]{:S(2)}) collective-permute-start(bf16[1,48,2304]{2,1,0:T(8,128)(2,1)S(1)} %add_convert_fusion.11), channel_id=1, source_target_pairs={{0,8},{1,9},{2,10},{3,11},{4,12},{5,13},{6,14},{7,15},{8,0},{9,1},... | collective-permute-start | bytes 663560 | tf_op jit(solution)/shard_map/ppermute | solution.py:25
  169.4 8.9 %collective-permute-start.20 = (bf16[2,48,896]{2,1,0:T(8,128)(2,1)S(1)}, bf16[2,48,896]{2,1,0:T(8,128)(2,1)S(1)}, u32[]{:S(2)}, u32[]{:S(2)}) collective-permute-start(bf16[2,48,896]{2,1,0:T(8,128)(2,1)S(1)} %add_convert_fusion.12), channel_id=1, source_target_pairs={{0,4},{1,5},{2,6},{3,7},{4,0},{5,1},{6,2},{7,3},{8,12},{9,13},{10,... | collective-permute-start | bytes 516104 | tf_op jit(solution)/shard_map/ppermute | solution.py:25
  171.1 18.3 %collective-permute-start.24 = (bf16[1,48,1536]{2,1,0:T(8,128)(2,1)S(1)}, bf16[1,48,1536]{2,1,0:T(8,128)(2,1)S(1)}, u32[]{:S(2)}, u32[]{:S(2)}) collective-permute-start(bf16[1,48,1536]{2,1,0:T(8,128)(2,1)S(1)} %add_convert_fusion.14), channel_id=1, source_target_pairs={{0,8},{1,9},{2,10},{3,11},{4,12},{5,13},{6,14},{7,15},{8,0},{9,1},... | collective-permute-start | bytes 442376 | tf_op jit(solution)/shard_map/ppermute | solution.py:25
  172.8 18.1 %collective-permute-start.29 = (bf16[48,1536]{1,0:T(8,128)(2,1)S(1)}, bf16[48,1536]{1,0:T(8,128)(2,1)S(1)}, u32[]{:S(2)}, u32[]{:S(2)}) collective-permute-start(bf16[48,1536]{1,0:T(8,128)(2,1)S(1)} %bitcast.47), channel_id=1, source_target_pairs={{0,16},{16,0},{1,17},{17,1},{2,18},{18,2},{3,19},{19,3},{4,20},{20... | collective-permute-start | bytes 442376 | tf_op jit(solution)/shard_map/ppermute | solution.py:25
  178.4 12.4 %collective-permute-start.26 = (bf16[1,48,896]{2,1,0:T(8,128)(2,1)S(1)}, bf16[1,48,896]{2,1,0:T(8,128)(2,1)S(1)}, u32[]{:S(2)}, u32[]{:S(2)}) collective-permute-start(bf16[1,48,896]{2,1,0:T(8,128)(2,1)S(1)} %add_convert_fusion.18), channel_id=1, source_target_pairs={{0,8},{1,9},{2,10},{3,11},{4,12},{5,13},{6,14},{7,15},{8,0},{9,1},... | collective-permute-start | bytes 258056 | tf_op jit(solution)/shard_map/ppermute | solution.py:25
  184.8 7.0 %collective-permute-start.28 = (bf16[48,2304]{1,0:T(8,128)(2,1)S(1)}, bf16[48,2304]{1,0:T(8,128)(2,1)S(1)}, u32[]{:S(2)}, u32[]{:S(2)}) collective-permute-start(bf16[48,2304]{1,0:T(8,128)(2,1)S(1)} %bitcast.25), channel_id=1, source_target_pairs={{0,16},{16,0},{1,17},{17,1},{2,18},{18,2},{3,19},{19,3},{4,20},{20... | collective-permute-start | bytes 663560 | tf_op jit(solution)/shard_map/ppermute | solution.py:25
  189.6 5.2 %collective-permute-start.25 = (bf16[48,1536]{1,0:T(8,128)(2,1)S(1)}, bf16[48,1536]{1,0:T(8,128)(2,1)S(1)}, u32[]{:S(2)}, u32[]{:S(2)}) collective-permute-start(bf16[48,1536]{1,0:T(8,128)(2,1)S(1)} %bitcast.27), channel_id=1, source_target_pairs={{0,16},{16,0},{1,17},{17,1},{2,18},{18,2},{3,19},{19,3},{4,20},{20... | collective-permute-start | bytes 442376 | tf_op jit(solution)/shard_map/ppermute | solution.py:25
  190.9 4.8 %collective-permute-start.27 = (bf16[48,896]{1,0:T(8,128)(2,1)S(1)}, bf16[48,896]{1,0:T(8,128)(2,1)S(1)}, u32[]{:S(2)}, u32[]{:S(2)}) collective-permute-start(bf16[48,896]{1,0:T(8,128)(2,1)S(1)} %bitcast.29), channel_id=1, source_target_pairs={{0,16},{16,0},{1,17},{17,1},{2,18},{18,2},{3,19},{19,3},{4,20},{20... | collective-permute-start | bytes 258056 | tf_op jit(solution)/shard_map/ppermute | solution.py:25

commit v3 on v2

--- a/solution.py
+++ b/solution.py
@@ -180,7 +180,7 @@
         (1,),
         "scatter_home",
         anywhere=(1,),
-        work=10**7,
+        work=2 * 10**10,
         scratch=[pltpu.SemaphoreType.DMA((2, half))],
     )[0]
 
@@ -342,10 +342,15 @@
 
 def spread(grad, outs, scalars_ref, base, shard, order):
     core, place = scalars_ref[base + 1], scalars_ref[base + 2]
-    for j in range(2 ** len(order)):
+    count = 2 ** len(order)
+    for j in range(count):
         row = (place ^ place_of(j, order)) * 2
         for out, which in zip(outs, (1 - core, core)):
-            out[j] = grad[pl.ds(pl.multiple_of((row + which) * shard, 16), shard), :]
+            if isinstance(out, tuple):
+                out = out[2 * j // count].at[j % (count // 2)]
+            else:
+                out = out.at[j]
+            out[...] = grad[pl.ds(pl.multiple_of((row + which) * shard, 16), shard), :]
 
 
 def feed_forward(scalars, normed, cot, far_cot, weights, half, shards, base):
@@ -379,7 +384,8 @@
         kept_out,
         far_out,
         sums_out,
-        send,
+        near,
+        away,
         keep,
         held,
         acts,
@@ -439,9 +445,9 @@
             grad[...] = dot(acts[:, pl.ds(start, part)], branch_out[...], 0, 0).astype(BF16)
             core, low = scalars_ref[base + 1], scalars_ref[base + 2] & 1
             for j in range(2):
-                for out, which in ((send, 1 - core), (keep, core)):
+                for out, which in (((near, away)[j].at[0, 0], 1 - core), (keep.at[j, 0], core)):
                     row = ((low ^ j) * 2 + which) * shard
-                    out[j, 0] = grad[pl.ds(pl.multiple_of(row, 16), shard), :]
+                    out[...] = grad[pl.ds(pl.multiple_of(row, 16), shard), :]
 
     def behind(i):
         return jnp.clip(i - 1, 0, steps - 1)
@@ -457,7 +463,7 @@
         apart = (s[base + 2] >> 1) ^ jnp.maximum(i - steps, 0)
         return 0, (apart & 1) * 2 + (apart >> 1), 0, 0
 
-    grads = pl.BlockSpec((2, 1, shard, width), entry)
+    grads = [pl.BlockSpec((count, 1, shard, width), entry) for count in (1, 1, 2)]
     return call(
         kernel,
         scalars,
@@ -479,8 +485,7 @@
             duo,
             duo,
             pl.BlockSpec((8, width), lambda i, s: (0, 0)),
-            grads,
-            grads,
+            *grads,
         ],
         [
             jax.ShapeDtypeStruct((height, inner_width), BF16),
@@ -488,7 +493,8 @@
             jax.ShapeDtypeStruct((half, slot_rows, width), BF16),
             jax.ShapeDtypeStruct((half, slot_rows, width), BF16),
             jax.ShapeDtypeStruct((8, width), F32),
-            jax.ShapeDtypeStruct((2, places // 2, shard, width), BF16),
+            jax.ShapeDtypeStruct((1, places // 2, shard, width), BF16),
+            jax.ShapeDtypeStruct((1, places // 2, shard, width), BF16),
             jax.ShapeDtypeStruct((2, places // 2, shard, width), BF16),
         ],
         (steps + parts,),
@@ -503,13 +509,12 @@
     )
 
 
-def feed_backward(scalars, branch, slope, normed, root, context, weights, shards, base, orders):
+def feed_backward(scalars, branch, slope, normed, root, weights, shards, base, order):
     w_in, w_back, norm_gains, bias_rows = weights
     total, width = branch.shape
     inner_width = slope.shape[1]
     chunk = 768
     steps = inner_width // chunk
-    turn = steps // 2
     shard = width // shards
     places = shards // 2
     piece = 128
@@ -520,7 +525,6 @@
         slope_ref,
         normed_ref,
         root_ref,
-        context_ref,
         w_in_ref,
         w_back_ref,
         gains_ref,
@@ -528,10 +532,8 @@
         low_attn_out,
         sums_out,
         inner_sum_out,
-        send_a,
-        keep_a,
-        send_b,
-        keep_b,
+        send,
+        keep,
         held,
         low_hidden,
         grad,
@@ -544,58 +546,42 @@
             low_hidden[...] = hidden.astype(BF16)
             held[...] = branch_ref[...].astype(F32)
 
-        @pl.when(step < steps)
-        def _():
-            cols = pl.ds(pl.multiple_of(step * chunk, chunk), chunk)
-            sums = jnp.zeros((1, chunk), F32)
-            lows = []
-            for r in range(0, total, 256):
-                span = slice(r, r + 256)
-                d_inner = dot(branch_ref[span], w_back_ref[cols, :], 1, 1)
-                d_inner = d_inner * slope_ref[span, cols].astype(F32)
-                sums = sums + row_sum(d_inner)
-                low = d_inner.astype(BF16)
-                lows.append(low)
-                held[span] += dot(low, w_in_ref[:, cols], 1, 1)
-            inner_sum_out[...] = jnp.broadcast_to(sums, inner_sum_out.shape)
-            grad[...] = dot(low_hidden[...], jnp.concatenate(lows, 0), 0, 0).astype(BF16)
-
-        @pl.when(step == steps)
+        cols = pl.ds(pl.multiple_of(step * chunk, chunk), chunk)
+        sums = jnp.zeros((1, chunk), F32)
+        lows = []
+        for r in range(0, total, 512):
+            span = slice(r, r + 512)
+            d_inner = dot(branch_ref[span], w_back_ref[cols, :], 1, 1)
+            d_inner = d_inner * slope_ref[span, cols].astype(F32)
+            sums = sums + row_sum(d_inner)
+            low = d_inner.astype(BF16)
+            lows.append(low)
+            held[span] += dot(low, w_in_ref[:, cols], 1, 1)
+        inner_sum_out[...] = jnp.broadcast_to(sums, inner_sum_out.shape)
+        grad[...] = dot(low_hidden[...], jnp.concatenate(lows, 0), 0, 0).astype(BF16)
+
+        spread(grad, (send, keep), scalars_ref, base, shard, order)
+
+        @pl.when(step == steps - 1)
         def _():
             sums = [jnp.zeros((1, width), F32)] * 3
-            lows = []
             for i in range(total // piece):
                 span = slice(i * piece, (i + 1) * piece)
                 d_hidden, scaled = held[span], normed_ref[span].astype(F32)
                 d_one = normal_back(d_hidden * gains_ref[0:1, :], scaled, root_ref[span, 0:1])
-                lows.append(d_one.astype(BF16))
-                low_attn_out[span] = lows[-1]
+                low_attn_out[span] = d_one.astype(BF16)
                 for j, term in enumerate((d_hidden * scaled, d_hidden, d_one)):
                     sums[j] = sums[j] + row_sum(term)
             sums_out[...] = jnp.concatenate(sums + [jnp.zeros((5, width), F32)], 0)
-            grad[...] = dot(context_ref[...], jnp.concatenate(lows, 0), 0, 0).astype(BF16)
-
-        @pl.when(step < turn)
-        def _():
-            spread(grad, (send_a, keep_a), scalars_ref, base, shard, orders[0])
-
-        @pl.when(step >= turn)
-        def _():
-            spread(grad, (send_b, keep_b), scalars_ref, base, shard, orders[1])
-
-    def now(i):
-        return jnp.minimum(i, steps - 1)
-
-    half_a = pl.BlockSpec((places, shard, chunk), lambda i, s: (0, 0, jnp.minimum(i, turn - 1)))
-    half_b = pl.BlockSpec((places, shard, chunk), lambda i, s: (0, 0, jnp.maximum(i - turn, 0)))
-    shape_a = jax.ShapeDtypeStruct((places, shard, turn * chunk), BF16)
-    shape_b = jax.ShapeDtypeStruct((places, shard, (steps + 1 - turn) * chunk), BF16)
+    grads = pl.BlockSpec(
+        (places, shard, chunk), lambda i, s: (0, 0, i ^ (s[base + 3] * (steps // 2)))
+    )
+    shape = jax.ShapeDtypeStruct((places, shard, inner_width), BF16)
     return call(
         kernel,
         scalars,
-        [branch, slope, normed, root, context, w_in, w_back, norm_gains, bias_rows],
+        [branch, slope, normed, root, w_in, w_back, norm_gains, bias_rows],
         [
-            RESIDENT,
             RESIDENT,
             RESIDENT,
             RESIDENT,
@@ -608,22 +594,18 @@
         [
             RESIDENT,
             pl.BlockSpec((8, width), lambda i, s: (0, 0)),
-            pl.BlockSpec((8, chunk), lambda i, s: (0, now(i))),
-            half_a,
-            half_a,
-            half_b,
-            half_b,
+            pl.BlockSpec((8, chunk), lambda i, s: (0, i)),
+            grads,
+            grads,
         ],
         [
             jax.ShapeDtypeStruct((total, width), BF16),
             jax.ShapeDtypeStruct((8, width), F32),
             jax.ShapeDtypeStruct((8, inner_width), F32),
-            shape_a,
-            shape_a,
-            shape_b,
-            shape_b,
-        ],
-        (steps + 1,),
+            shape,
+            shape,
+        ],
+        (steps,),
         "feed_backward",
         limit=21 * 2**20,
         scratch=[
@@ -635,7 +617,7 @@
 
 
 def attention_backward(scalars, kept, weights, part, shards, base, order, earlier=(), sums=()):
-    low_attn, mixed, probs, joined = kept
+    low_attn, mixed, probs, joined, context = kept
     w_out, w_qkv = weights
     total, width = low_attn.shape
     pairs, blocks, _, length = probs.shape
@@ -648,7 +630,7 @@
     shard = width // shards
     places = shards // 2
     last = part == 1
-    columns = 3 * span_cols + (128 if last else 0)
+    columns = 3 * span_cols + (128 if last else width)
 
     def kernel(
         scalars_ref,
@@ -661,9 +643,9 @@
     ):
         if last:
             w_qkv_ref, earlier_ref, one, two, inner, sums_ref = refs[:6]
-            kept_out, far_out, sums_out, send, keep, held, grad = refs[6:]
+            kept_out, far_out, sums_out, near, away, keep, held, grad = refs[6:]
         else:
-            held, sums_out, send, keep, grad = refs
+            context_ref, held, sums_out, near, away, keep, grad = refs
         step = pl.program_id(0)
 
         @pl.when(step == 0)
@@ -740,7 +722,10 @@
                     small.append(jnp.concatenate(runs, 1))
                 small.append(jnp.zeros((120 - count, width), F32))
                 grad[:, 3 * span_cols :] = jnp.concatenate(small, 0).T.astype(BF16)
-            spread(grad, (send, keep), scalars_ref, base, shard, order)
+            else:
+                outer = dot(context_ref[...], low_attn_ref[...], 0, 0)
+                grad[:, 3 * span_cols :] = outer.astype(BF16)
+            spread(grad, ((near, away), keep), scalars_ref, base, shard, order)
 
     two_slots = pl.BlockSpec((2, slot_rows, width), lambda i, s: (i, 0, 0))
     operands = [low_attn, mixed, probs, joined, w_out]
@@ -752,13 +737,12 @@
         RESIDENT,
         RESIDENT,
     ]
-    grads = pl.BlockSpec((places, shard, columns), lambda i, s: (0, 0, 0))
-    out_specs = [pl.BlockSpec((8, span_cols), lambda i, s: (0, 0)), grads, grads]
-    out_shape = [
-        jax.ShapeDtypeStruct((8, span_cols), F32),
-        jax.ShapeDtypeStruct((places, shard, columns), BF16),
-        jax.ShapeDtypeStruct((places, shard, columns), BF16),
-    ]
+    out_specs = [pl.BlockSpec((8, span_cols), lambda i, s: (0, 0))]
+    out_shape = [jax.ShapeDtypeStruct((8, span_cols), F32)]
+    for entries in (places // 2, places // 2, places):
+        shape = (entries, shard, columns)
+        out_specs.append(pl.BlockSpec(shape, lambda i, s: (0, 0, 0)))
+        out_shape.append(jax.ShapeDtypeStruct(shape, BF16))
     if last:
         operands += [w_qkv, earlier, *sums]
         in_specs += [RESIDENT, RESIDENT]
@@ -766,6 +750,8 @@
         out_specs = [two_slots, two_slots] + out_specs
         out_shape = [jax.ShapeDtypeStruct((pairs, slot_rows, width), BF16)] * 2 + out_shape
     else:
+        operands.append(context)
+        in_specs.append(RESIDENT)
         out_specs = [RESIDENT] + out_specs
         out_shape = [jax.ShapeDtypeStruct((total, 3 * span_cols), BF16)] + out_shape
     return call(
@@ -797,42 +783,67 @@
 
 
 class Shards:
-    def __init__(self, send, keep, order):
-        shard, width = send.shape[-2:]
+    def __init__(self, *arrays, order):
+        *sends, keep = arrays
+        shard, width = keep.shape[-2:]
         self.order = list(order)
-        shape = (2 ** len(self.order), shard, width)
-        self.held = [keep.reshape(shape)]
-        self.coming = flipped(send, "dp", 1).reshape(shape)
+        self.columns = width // 2 if "mod" in self.order else width
+        count = 2 ** sum(step != "mod" for step in self.order)
+        self.held = [(0, keep.reshape((count, shard, width)))]
+        self.count = count
+        shape = (count // len(sends), shard, width)
+        self.coming = []
+        for i in range(len(sends))[::-1]:
+            self.coming.append((i * shape[0], flipped(sends[i], "dp", 1).reshape(shape)))
 
     def step(self):
-        self.held.append(in_turn(self.coming))
-        count = self.coming.shape[0]
-        first = count // 2 if self.order else 0
+        bit = self.order.pop(0) if self.order else None
+        count = self.count
+        first = count // 2 if bit in (0, 1, 2) else 0
+        column = self.columns if bit == "mod" else 0
+        late = []
+        for at, array in self.coming:
+            if at + array.shape[0] > first:
+                self.held.append((at, in_turn(array)))
+            else:
+                late.append((at, array))
         total = None
-        for array in self.held:
-            array = lax.slice_in_dim(array, first, count, axis=0).astype(F32)
+        for at, array in self.held:
+            if at >= count or at + array.shape[0] <= first:
+                continue
+            array = lax.slice_in_dim(array, first - at if first > at else 0, count - at, axis=0)
+            array = lax.slice_in_dim(array, column, column + self.columns, axis=2)
+            array = array.astype(F32)
             total = array if total is None else total + array
         total = total.astype(BF16)
-        if self.order:
-            self.coming = flipped(total, "dp", 2 << self.order.pop(0))
-        else:
+        if bit is None:
             self.mine = lax.optimization_barrier(total[0])
             self.coming = flipped(self.mine, "mod", 1)
+        elif bit == "mod":
+            self.coming = late + [(0, flipped(total, "mod", 1))]
+        else:
+            self.coming = late + [(0, flipped(total, "dp", 2 << bit))]
+            self.count = first
         LINE.append(total)
 
     def result(self):
         return self.mine.astype(F32) + in_turn(self.coming).astype(F32)
 
 
-def finish_qkv(scalars, early, late, width, count):
+def finish(scalars, inner, early, late, width, inner_width, base):
+    pieces = [inner, early, late]
     shard = early.mine.shape[0]
-    widths = (early.mine.shape[1] // 3, (late.mine.shape[1] - 128) // 3)
-
-    def kernel(scalars_ref, mine_a, coming_a, mine_b, coming_b, qkv, b_qv, gains, biases, inner):
-        parts = [
-            mine[...].astype(F32) + coming[...].astype(F32)
-            for mine, coming in ((mine_a, coming_a), (mine_b, coming_b))
-        ]
+    count = inner_width // width
+    turn = inner.mine.shape[1]
+    widths = ((early.mine.shape[1] - width) // 3, (late.mine.shape[1] - 128) // 3)
+
+    def kernel(scalars_ref, *refs):
+        ins, (grad_in, grad_out, qkv, b_qv, gains, biases, b_in) = refs[:6], refs[6:]
+        first = scalars_ref[base + 3] == 0
+        grad_in[:, :turn] = jnp.where(first, ins[0][...], ins[1][...]).astype(F32)
+        grad_in[:, turn:] = jnp.where(first, ins[1][...], ins[0][...]).astype(F32)
+        parts = [ins[2 * i][...].astype(F32) + ins[2 * i + 1][...].astype(F32) for i in (1, 2)]
+        grad_out[...] = parts[0][:, 3 * widths[0] :]
         at = 0
         for third in range(3):
             for part, columns in zip(parts, widths):
@@ -843,10 +854,11 @@
         b_qv[...] = small[0:2]
         gains[...] = small[2:4]
         biases[...] = small[4:8]
-        inner[...] = small[8 : 8 + count]
-
-    operands = [early.mine, early.coming, late.mine, late.coming]
-    shapes = ((shard, 3 * width), (2, shard), (2, shard), (4, shard), (count, shard))
+        b_in[...] = small[8 : 8 + count]
+
+    operands = [each for piece in pieces for each in (piece.mine, piece.coming)]
+    shapes = [(shard, inner_width), (shard, width), (shard, 3 * width)]
+    shapes += [(2, shard), (2, shard), (4, shard), (count, shard)]
     return call(
         kernel,
         scalars,
@@ -855,13 +867,15 @@
         [pl.BlockSpec(shape, lambda i, s: (0, 0)) for shape in shapes],
         [jax.ShapeDtypeStruct(shape, F32) for shape in shapes],
         (1,),
-        "finish_qkv",
-        anywhere=(0, 1, 2, 3),
-    )
-
-
-def reduce_plain(send, keep, order):
-    shard, columns = send.shape[-2:]
+        "finish",
+        anywhere=range(6),
+    )
+
+
+def reduce_plain(*arrays, order):
+    *sends, keep = arrays
+    shard, columns = keep.shape[-2:]
+    send = jnp.concatenate([each.reshape(-1, shard, columns) for each in sends], 0)
     total = jnp.stack([keep.reshape(-1, shard, columns), send.reshape(-1, shard, columns)], 1)
     places = [place_of(j, order) for j in range(total.shape[0])]
     total = jnp.stack([total[places.index(j)] for j in range(total.shape[0])])
@@ -910,7 +924,7 @@
     far_cot = flipped(sent_cot, "mod", 1)
     spot = place if aligned else 0 * place
     scalars = jnp.concatenate(
-        [partner[0], jnp.stack([side, spot & 1, spot >> 1]).astype(jnp.int32)]
+        [partner[0], jnp.stack([side, spot & 1, spot >> 1, side * aligned]).astype(jnp.int32)]
     )
 
     live = row_live.reshape(2, groups, slot_rows)
@@ -937,21 +951,12 @@
     out_back = flipped(out_far, "mod", 1)
     back_weights = (w_in, w_back, norm_gains, bias_rows)
     attn_weights = (w_out, w_qkv)
-    path, other = (0, 1, 2), (1, 0, 2)
+    path = (0, 1, 2)
     if aligned:
-        back = Shards(*back, path)
+        back = Shards(*back, order=path)
         back.step()
     low_attn, sums_one, inner_sum, *inner = feed_backward(
-        scalars,
-        branch,
-        slope,
-        normed,
-        root,
-        context,
-        back_weights,
-        layout,
-        groups,
-        (path, other),
+        scalars, branch, slope, normed, root, back_weights, layout, groups, path
     )
     shard = width // shards
     count = inner_width // width
@@ -959,18 +964,16 @@
         back.step()
         out_back = in_turn(out_back)
         pause(scalars)
-        inner_a, inner_b = Shards(*inner[:2], path), Shards(*inner[2:], other)
-        inner_a.step()
-        inner_b.step()
-    attn_kept = (low_attn, mixed, probs, joined)
+        inner = Shards(*inner, order=("mod", 0, 1, 2))
+        inner.step()
+    attn_kept = (low_attn, mixed, probs, joined, context)
     d_mixed, sums_qv, *qkv_a = attention_backward(
         scalars, attn_kept, attn_weights, 0, layout, groups, path
     )
     if aligned:
         back.step()
-        inner_a.step()
-        pause(scalars)
-        qkv_a = Shards(*qkv_a, path)
+        out_rows = scatter_home(scalars, out_kept, out_back, half).reshape(1, -1, width)
+        qkv_a = Shards(*qkv_a, order=path)
         qkv_a.step()
     if layout != shards:
         inner_sum = inner_sum.reshape(8, shards, count, shard).transpose(0, 2, 1, 3)
@@ -982,32 +985,33 @@
     )
     d_back = flipped(d_far, "mod", 1)
     if aligned:
-        qkv_b = Shards(*qkv_b, path)
+        qkv_b = Shards(*qkv_b, order=path)
+        inner.step()
         back.step()
-        inner_b.step()
-        inner_a.step()
-        qkv_b.step()
-        qkv_a.step()
-        out_rows = scatter_home(scalars, out_kept, out_back, half).reshape(1, -1, width)
-        inner_b.step()
-        qkv_b.step()
-        inner_a.step()
-        qkv_a.step()
-        grad_back = back.result()
-        qkv_b.step()
-        inner_b.step()
-        grad_rows = scatter_home(scalars, d_kept, d_back, half).reshape(1, -1, width)
         qkv_a.step()
         qkv_b.step()
-        inner_a, inner_b = inner_a.result(), inner_b.result()
-        grad_qkv, *small = finish_qkv(scalars, qkv_a, qkv_b, width, count)
+        inner.step()
+        pause(scalars)
+        qkv_a.step()
+        qkv_b.step()
+        grad_back = back.result()
+        inner.step()
+        pause(scalars)
+        qkv_a.step()
+        qkv_b.step()
+        inner.step()
+        grad_rows = scatter_home(scalars, d_kept, d_back, half).reshape(1, -1, width)
+        qkv_b.step()
+        grad_in, grad_out, grad_qkv, *small = finish(
+            scalars, inner, qkv_a, qkv_b, width, inner_width, groups
+        )
     else:
         out_rows = scatter_home(scalars, out_kept, out_back, half).reshape(1, -1, width)
-        grad_back = reduce_plain(*back, path)
-        inner_a, inner_b = reduce_plain(*inner[:2], path), reduce_plain(*inner[2:], other)
-        qkv_a, qkv_b = reduce_plain(*qkv_a, path), reduce_plain(*qkv_b, path)
+        grad_back = reduce_plain(*back, order=path)
+        grad_in = reduce_plain(*inner, order=path)
+        qkv_a, qkv_b = reduce_plain(*qkv_a, order=path), reduce_plain(*qkv_b, order=path)
         grad_rows = scatter_home(scalars, d_kept, d_back, half).reshape(1, -1, width)
-        columns = (qkv_a.shape[1] // 3, (qkv_b.shape[1] - 128) // 3)
+        columns = ((qkv_a.shape[1] - width) // 3, (qkv_b.shape[1] - 128) // 3)
         thirds = []
         for third in range(3):
             for part, wide in zip((qkv_a, qkv_b), columns):
@@ -1015,16 +1019,16 @@
         grad_qkv = jnp.concatenate(thirds, 1)
         small = qkv_b[:, 3 * columns[1] :].T
         small = small[0:2], small[2:4], small[4:8], small[8 : 8 + count]
-    turn = inner_width - inner_a.shape[1]
+        grad_out = qkv_a[:, 3 * columns[0] :]
     return (
         out_rows,
         grad_rows,
         grad_qkv,
         small[0],
-        inner_b[:, turn:],
+        grad_out,
         small[1],
         small[2],
-        jnp.concatenate([inner_a, inner_b[:, :turn]], 1),
+        grad_in,
         small[3].reshape(-1),
         grad_back,
     )

time: 200 us -> 197 us (0.985)
  starting transfers between devices: 41.7 us -> 28.2 us
  waiting for transfers between devices: 32.6 us -> 43.6 us
    ppermute x30 -> x29, starting transfers between devices: 41.7 us -> 28.2 us  [flipped(): return lax.ppermute(value, axis, pairs)]
    ppermute x30 -> x29, waiting for transfers between devices: 32.6 us -> 43.6 us  [flipped(): return lax.ppermute(value, axis, pairs)]
    convert_element_type x20 -> x17, other arithmetic: 3.96 us -> 4.22 us  [step(): total = total.astype(BF16)]
    pallas_call x14 -> x15, Pallas kernels: 114 us -> 114 us  [call(): pl.pallas_call(wrapped, grid_spec=pltpu.PrefetchScalarGridSpec(num_scalar...]
  transfers between devices with their start and end apart: 30 -> 29, of which waited for: 12 -> 10; matrix products, arithmetic and copies ran while one was open for 3% -> 3% of each run, Pallas kernels for 43% -> 43%
where the time goes in v3:
time: 197 us; the launch traced here: 196 us
  Pallas kernels  114 us (58%)
  waiting for transfers between devices  43.6 us (22%)
  starting transfers between devices  28.2 us (14%)
  other arithmetic  5.86 us (3%)
  local copies, waits for them, and re-layouts  3.15 us (2%)
    pallas_call x15, Pallas kernels, call(): pl.pallas_call(wrapped, grid_spec=pltpu.PrefetchScalarGridSpec(num_scalar...  114 us
    ppermute x29, waiting for transfers between devices, flipped(): return lax.ppermute(value, axis, pairs)  43.6 us
    ppermute x29, starting transfers between devices, flipped(): return lax.ppermute(value, axis, pairs)  28.2 us
    convert_element_type x17, other arithmetic, step(): total = total.astype(BF16)  4.22 us
  transfers between devices with their start and end apart: 29, of which 10 were waited for; matrix products, arithmetic and copies ran while one was open for 3% of the time, Pallas kernels for 43%

profile of v3, /device:TPU:0, one launch (start us, length us, event | category | flops | bytes accessed | tf_op | source)
XLA Modules:
  0.0 195.9 jit_solution(1102496535054197190)
XLA Ops:
  0.6 2.5 %gather_sent.3 = (bf16[4,64,768]{2,1,0:T(8,128)(2,1)}, f32[8,128]{1,0:T(8,128)}) custom-call(s32[16]{0:T(128)} %bitcast.48, bf16[16,64,768]{2,1,0:T(8,128)(2,1)} %bitcast.34), custom_call_target="tpu_custom_call" | custom-call | flops 10000000 | bytes 1048576 | tf_op jit(solution)/shard_map/gather_sent/pallas_call | solution.py:72
  3.1 3.0 %collective-permute-start = (bf16[4,64,768]{2,1,0:T(8,128)(2,1)}, bf16[4,64,768]{2,1,0:T(8,128)(2,1)S(1)}, u32[]{:S(2)}, u32[]{:S(2)}) collective-permute-start(bf16[4,64,768]{2,1,0:T(8,128)(2,1)} %get-tuple-element.114), channel_id=1, source_target_pairs={{0,16},{16,0},{1,17},{17,1},{2,18},{18,2},{3,19},{19,3},{4,20},{20... | collective-permute-start | bytes 1179656 | tf_op jit(solution)/shard_map/ppermute | solution.py:25
  6.2 2.6 %gather_sent.4 = (bf16[4,64,768]{2,1,0:T(8,128)(2,1)}, f32[8,128]{1,0:T(8,128)}) custom-call(s32[16]{0:T(128)} %bitcast.49, bf16[16,64,768]{2,1,0:T(8,128)(2,1)} %bitcast.35, f32[8,128]{1,0:T(8,128)} %get-tuple-element.115.refs_1_), custom_call_target="tpu_custom_call" | custom-call | flops 10000000 | bytes 1048576 | tf_op jit(solution)/shard_map/gather_sent/pallas_call | solution.py:72
  8.9 2.8 %gather_sent.5 = (bf16[8,64,768]{2,1,0:T(8,128)(2,1)}, f32[8,128]{1,0:T(8,128)}) custom-call(s32[16]{0:T(128)} %bitcast.50, bf16[16,64,768]{2,1,0:T(8,128)(2,1)} %bitcast.31, f32[8,128]{1,0:T(8,128)} %get-tuple-element.116.refs_1_), custom_call_target="tpu_custom_call" | custom-call | flops 10000000 | bytes 1048576 | tf_op jit(solution)/shard_map/gather_sent/pallas_call | solution.py:72
  11.7 4.6 %collective-permute-done.refs_2_ = bf16[4,64,768]{2,1,0:T(8,128)(2,1)S(1)} collective-permute-done((bf16[4,64,768]{2,1,0:T(8,128)(2,1)}, bf16[4,64,768]{2,1,0:T(8,128)(2,1)S(1)}, u32[]{:S(2)}, u32[]{:S(2)}) %collective-permute-start) | collective-permute-done | bytes 393248 | tf_op jit(solution)/shard_map/ppermute | solution.py:25
  16.6 2.1 %collective-permute-start.2 = (bf16[8,64,768]{2,1,0:T(8,128)(2,1)}, bf16[8,64,768]{2,1,0:T(8,128)(2,1)S(1)}, u32[]{:S(2)}, u32[]{:S(2)}) collective-permute-start(bf16[8,64,768]{2,1,0:T(8,128)(2,1)} %get-tuple-element.127), channel_id=1, source_target_pairs={{0,16},{16,0},{1,17},{17,1},{2,18},{18,2},{3,19},{19,3},{4,20},{20... | collective-permute-start | bytes 2359304 | tf_op jit(solution)/shard_map/ppermute | solution.py:25
  18.6 0.6 gather_fusion
  19.3 5.7 %fetch.1 = (bf16[768,2304]{1,0:T(8,128)(2,1)S(1)}, bf16[768,768]{1,0:T(8,128)(2,1)S(1)}, bf16[768,3072]{1,0:T(8,128)(2,1)S(1)}, bf16[3072,768]{1,0:T(8,128)(2,1)S(1)}, f32[8,128]{1,0:T(8,128)}) custom-call(s32[20]{0:T(128)S(1)} %concatenate.6.scalars_ref, bf16[768,2304]{1,0:T(8,128)(2,1)} %refs_0_.1, bf16[768,768]{1,0:T(8,128)(2,1)} %refs_1_.1, ...), custom_call_target="tpu_custom_call" | custom-call | flops 10000000 | bytes 1048576 | tf_op jit(solution)/shard_map/fetch/pallas_call | solution.py:72
  25.0 0.7 pad_add_fusion
  25.7 0.7 copy-done.9
  26.4 14.8 %attention_forward.1 = (bf16[1024,768]{1,0:T(8,128)(2,1)S(1)}, bf16[1024,2304]{1,0:T(8,128)(2,1)}, bf16[8,6,256,128]{3,2,1,0:T(8,128)(2,1)}, bf16[1024,768]{1,0:...) custom-call(s32[20]{0:T(128)S(1)} %concatenate.6.scalars_ref, ...), custom_call_target="tpu_custom_call" | custom-call | flops 40000000000 | bytes 1048576 | tf_op jit(solution)/shard_map/attention_forward/pallas_call | solution.py:72
  41.2 25.3 %feed_forward.1 = (bf16[1024,3072]{1,0:T(8,128)(2,1)S(1)}, bf16[1024,768]{1,0:T(8,128)(2,1)S(1)}, bf16[8,64,768]{2,1,0:T(8,128)(2,1)}, bf16[8,64,768]{2,1,0:T(8,...) custom-call(s32[20]{0:T(128)S(1)} %concatenate.6.scalars_ref, ...), custom_call_target="tpu_custom_call" | custom-call | flops 4000000000 | bytes 1048576 | tf_op jit(solution)/shard_map/feed_forward/pallas_call | solution.py:72
  67.0 2.5 %collective-permute-done.4 = bf16[1,4,192,768]{3,2,1,0:T(8,128)(2,1)S(1)} collective-permute-done((bf16[1,4,192,768]{3,2,1,0:T(8,128)(2,1)}, bf16[1,4,192,768]{3,2,1,0:T(8,128)(2,1)S(1)}, u32[]{:S(2)}, u32[]{:S(2)}) %collective-permute-start.4) | collective-permute-done | bytes 1179680 | tf_op jit(solution)/shard_map/ppermute | solution.py:25
  69.6 1.7 fusion.refs_8_
  71.2 1.6 collective-permute-start.5
  72.8 1.2 collective-permute-start.3
  74.1 21.7 %feed_backward.1 = (bf16[1024,768]{1,0:T(8,128)(2,1)S(1)}, f32[8,768]{1,0:T(8,128)}, f32[8,3072]{1,0:T(8,128)}, bf16[8,48,3072]{2,1,0:T(8,128)(2,1)}, bf16[8,48,3072]{2,1,0:T(8,128)(2,1)}, /*index=5*/f32[8,128]{1,0:T(8,128)}) custom-call(s32[20]{0:T(128)S(1)} %concatenate.6.scalars_ref, bf16[1024,768]{1,0:T(8,128)(2,1)S(1)} %get-tuple-element.138.refs_0_, ...), custom_call_target="tpu_custom_call" | custom-call | flops 4000000000 | bytes 1048576 | tf_op jit(solution)/shard_map/feed_backward/pallas_call | solution.py:72
  95.7 3.6 %collective-permute-done.5 = bf16[4,192,768]{2,1,0:T(8,128)(2,1)S(1)} collective-permute-done((bf16[4,192,768]{2,1,0:T(8,128)(2,1)S(1)}, bf16[4,192,768]{2,1,0:T(8,128)(2,1)S(1)}, u32[]{:S(2)}, u32[]{:S(2)}) %collective-permute-start.5) | collective-permute-done | bytes 1179680 | tf_op jit(solution)/shard_map/ppermute | solution.py:25
  99.6 1.6 collective-permute-start.7
  101.2 0.5 pause.3.refs_7_
  102.2 1.3 collective-permute-start.11
  103.5 14.1 %attention_backward.2 = (bf16[1024,1536]{1,0:T(8,128)(2,1)S(1)}, f32[8,512]{1,0:T(8,128)}, bf16[4,48,2304]{2,1,0:T(8,128)(2,1)}, bf16[4,48,2304]{2,1,0:T(8,128)(...) custom-call(s32[20]{0:T(128)S(1)} %concatenate.6.scalars_ref, bf16[1024,768]{1,0:T(8,128)(2,1)S(1)} %get-tuple-element.148.refs_0_, ...), custom_call_target="tpu_custom_call" | custom-call | flops 4000000000 | bytes 1048576 | tf_op jit(solution)/shard_map/attention_backward/pallas_call | solution.py:72
  117.8 2.7 %collective-permute-start.16 = (bf16[1,192,768]{2,1,0:T(8,128)(2,1)S(1)}, bf16[1,192,768]{2,1,0:T(8,128)(2,1)S(1)}, u32[]{:S(2)}, u32[]{:S(2)}) collective-permute-start(bf16[1,192,768]{2,1,0:T(8,128)(2,1)S(1)} %add_convert_fusion.8.refs_2_), channel_id=1, source_target_pairs={{0,8},{1,9},{2,10},{3,11},{4,12},{5,13},{6,14},{7,15},{8,0},{9,1},... | collective-permute-start | bytes 884744 | tf_op jit(solution)/shard_map/ppermute | solution.py:25
  120.9 3.7 %scatter_home.2 = (bf16[16,64,768]{2,1,0:T(8,128)(2,1)}, f32[8,128]{1,0:T(8,128)}) custom-call(s32[20]{0:T(128)S(1)} %concatenate.6.scalars_ref, bf16[8,64,768]{2,1,0:T(8,128)(2,1)} %get-tuple-element.131.refs_0_, bf16[8,64,768]{2,1,0:T(8,128)(2,1)S(1)} %collective-permute-done.3.refs_1_, bf16[1,192,768]{2,1,0:T(8,128)(2,1)S(1)} %add_convert_fusion.8.refs_2_, ...), custom_call_target="tpu_custom_call" | custom-call | flops 20000000000 | bytes 1048576 | tf_op jit(solution)/shard_map/scatter_home/pallas_call | solution.py:72
  124.9 1.6 collective-permute-start.14
  126.5 14.0 %attention_backward.3 = (bf16[8,64,768]{2,1,0:T(8,128)(2,1)}, bf16[8,64,768]{2,1,0:T(8,128)(2,1)}, f32[8,256]{1,0:T(8,128)}, bf16[4,48,896]{2,1,0:T(8,128)(2,1)}...) custom-call(s32[20]{0:T(128)S(1)} %concatenate.6.scalars_ref, ...), custom_call_target="tpu_custom_call" | custom-call | flops 4000000000 | bytes 1048576 | tf_op jit(solution)/shard_map/attention_backward/pallas_call | solution.py:72
  141.6 0.8 collective-permute-start.10
  142.6 0.6 collective-permute-start.12
  143.2 4.3 %collective-permute-done.14 = bf16[4,48,2304]{2,1,0:T(8,128)(2,1)S(1)} collective-permute-done((bf16[4,48,2304]{2,1,0:T(8,128)(2,1)S(1)}, bf16[4,48,2304]{2,1,0:T(8,128)(2,1)S(1)}, u32[]{:S(2)}, u32[]{:S(2)}) %collective-permute-start.14) | collective-permute-done | bytes 884768 | tf_op jit(solution)/shard_map/ppermute | solution.py:25
  147.5 0.8 collective-permute-start.18
  148.5 1.1 collective-permute-start.21
  149.6 9.5 %collective-permute-done.12 = bf16[4,48,1536]{2,1,0:T(8,128)(2,1)S(1)} collective-permute-done((bf16[4,48,1536]{2,1,0:T(8,128)(2,1)S(1)}, bf16[4,48,1536]{2,1,0:T(8,128)(2,1)S(1)}, u32[]{:S(2)}, u32[]{:S(2)}) %collective-permute-start.12) | collective-permute-done | bytes 589856 | tf_op jit(solution)/shard_map/ppermute | solution.py:25
  159.3 1.1 collective-permute-start.17
  161.0 1.6 collective-permute-start.19
  163.0 6.8 %collective-permute-done.19 = bf16[4,48,896]{2,1,0:T(8,128)(2,1)S(1)} collective-permute-done((bf16[4,48,896]{2,1,0:T(8,128)(2,1)S(1)}, bf16[4,48,896]{2,1,0:T(8,128)(2,1)S(1)}, u32[]{:S(2)}, u32[]{:S(2)}) %collective-permute-start.19) | collective-permute-done | bytes 344096 | tf_op jit(solution)/shard_map/ppermute | solution.py:25
  169.9 1.1 collective-permute-start.23
  171.1 1.1 collective-permute-start.22
  172.7 4.3 %collective-permute-done.24 = bf16[1,48,2304]{2,1,0:T(8,128)(2,1)S(1)} collective-permute-done((bf16[1,48,2304]{2,1,0:T(8,128)(2,1)S(1)}, bf16[1,48,2304]{2,1,0:T(8,128)(2,1)S(1)}, u32[]{:S(2)}, u32[]{:S(2)}) %collective-permute-start.24) | collective-permute-done | bytes 221216 | tf_op jit(solution)/shard_map/ppermute | solution.py:25
  177.2 0.6 collective-permute-done.23
  177.9 4.5 %collective-permute-done.22 = bf16[1,48,1536]{2,1,0:T(8,128)(2,1)S(1)} collective-permute-done((bf16[1,48,1536]{2,1,0:T(8,128)(2,1)S(1)}, bf16[1,48,1536]{2,1,0:T(8,128)(2,1)S(1)}, u32[]{:S(2)}, u32[]{:S(2)}) %collective-permute-start.22) | collective-permute-done | bytes 147488 | tf_op jit(solution)/shard_map/ppermute | solution.py:25
  182.6 0.8 collective-permute-start.25
  183.4 1.2 collective-permute-start.26
  184.7 3.7 %scatter_home.3 = (bf16[16,64,768]{2,1,0:T(8,128)(2,1)}, f32[8,128]{1,0:T(8,128)}) custom-call(s32[20]{0:T(128)S(1)} %concatenate.6.scalars_ref, bf16[8,64,768]{2,1,0:T(8,128)(2,1)} %get-tuple-element.172.refs_0_, bf16[8,64,768]{2,1,0:T(8,128)(2,1)S(1)} %collective-permute-done.10.refs_1_, bf16[1,48,1536]{2,1,0:T(8,128)(2,1)S(1)} %add_convert_fusion.12.refs_2_, ...), custom_call_target="tpu_custom_call" | custom-call | flops 20000000000 | bytes 1048576 | tf_op jit(solution)/shard_map/scatter_home/pallas_call | solution.py:72
  188.5 0.8 collective-permute-start.28
  189.3 0.9 convert_add_fusion.1
  190.2 2.8 %collective-permute-done.28.refs_5_ = bf16[48,896]{1,0:T(8,128)(2,1)S(1)} collective-permute-done((bf16[48,896]{1,0:T(8,128)(2,1)S(1)}, bf16[48,896]{1,0:T(8,128)(2,1)S(1)}, u32[]{:S(2)}, u32[]{:S(2)}) %collective-permute-start.28) | collective-permute-done | bytes 86048 | tf_op jit(solution)/shard_map/ppermute | solution.py:25
  193.0 1.6 finish.1
  194.6 1.3 reshape.84
  (73 shorter events, 6.5 us)
Async XLA Ops:
  3.1 13.2 %collective-permute-start = (bf16[4,64,768]{2,1,0:T(8,128)(2,1)}, bf16[4,64,768]{2,1,0:T(8,128)(2,1)S(1)}, u32[]{:S(2)}, u32[]{:S(2)}) collective-permute-start(bf16[4,64,768]{2,1,0:T(8,128)(2,1)} %get-tuple-element.114), channel_id=1, source_target_pairs={{0,16},{16,0},{1,17},{17,1},{2,18},{18,2},{3,19},{19,3},{4,20},{20... | collective-permute-start | bytes 1179656 | tf_op jit(solution)/shard_map/ppermute | solution.py:25
  6.1 10.2 %copy-start.5 = (s32[2,1024]{1,0:T(2,128)S(1)}, s32[2,1024]{1,0:T(2,128)}, u32[]{:S(2)}) copy-start(s32[2,1024]{1,0:T(2,128)} %param.14) | copy-start | bytes 24580
  6.1 10.2 %copy-start.4 = (s32[1,16]{1,0:T(1,128)S(1)}, s32[1,16]{1,0:T(1,128)}, u32[]{:S(2)}) copy-start(s32[1,16]{1,0:T(1,128)} %param.15) | copy-start | bytes 196
  8.8 16.9 %collective-permute-start.1 = (bf16[4,64,768]{2,1,0:T(8,128)(2,1)}, bf16[4,64,768]{2,1,0:T(8,128)(2,1)S(1)}, u32[]{:S(2)}, u32[]{:S(2)}) collective-permute-start(bf16[4,64,768]{2,1,0:T(8,128)(2,1)} %get-tuple-element.120), channel_id=1, source_target_pairs={{0,16},{16,0},{1,17},{17,1},{2,18},{18,2},{3,19},{19,3},{4,20},{20... | collective-permute-start | bytes 1179656 | tf_op jit(solution)/shard_map/ppermute | solution.py:25
  16.3 8.7 %copy-start.8 = (bf16[4,64,768]{2,1,0:T(8,128)(2,1)}, bf16[4,64,768]{2,1,0:T(8,128)(2,1)S(1)}, u32[]{:S(2)}) copy-start(bf16[4,64,768]{2,1,0:T(8,128)(2,1)S(1)} %collective-permute-done.refs_2_) | copy-start | bytes 1179652
  16.6 24.7 %collective-permute-start.2 = (bf16[8,64,768]{2,1,0:T(8,128)(2,1)}, bf16[8,64,768]{2,1,0:T(8,128)(2,1)S(1)}, u32[]{:S(2)}, u32[]{:S(2)}) collective-permute-start(bf16[8,64,768]{2,1,0:T(8,128)(2,1)} %get-tuple-element.127), channel_id=1, source_target_pairs={{0,16},{16,0},{1,17},{17,1},{2,18},{18,2},{3,19},{19,3},{4,20},{20... | collective-permute-start | bytes 2359304 | tf_op jit(solution)/shard_map/ppermute | solution.py:25
  25.7 0.7 copy-start.9
  66.5 3.1 %collective-permute-start.4 = (bf16[1,4,192,768]{3,2,1,0:T(8,128)(2,1)}, bf16[1,4,192,768]{3,2,1,0:T(8,128)(2,1)S(1)}, u32[]{:S(2)}, u32[]{:S(2)}) collective-permute-start(bf16[1,4,192,768]{3,2,1,0:T(8,128)(2,1)} %get-tuple-element.134), channel_id=1, source_target_pairs={{0,1},{1,0},{2,3},{3,2},{4,5},{5,4},{6,7},{7,6},{8,9},{9,8},{10,11... | collective-permute-start | bytes 3538952 | tf_op jit(solution)/shard_map/ppermute | solution.py:25
  66.5 29.2 %collective-permute-start.6 = (bf16[1,4,192,768]{3,2,1,0:T(8,128)(2,1)}, bf16[1,4,192,768]{3,2,1,0:T(8,128)(2,1)S(1)}, u32[]{:S(2)}, u32[]{:S(2)}) collective-permute-start(bf16[1,4,192,768]{3,2,1,0:T(8,128)(2,1)} %get-tuple-element.137), channel_id=1, source_target_pairs={{0,1},{1,0},{2,3},{3,2},{4,5},{5,4},{6,7},{7,6},{8,9},{9,8},{10,11... | collective-permute-start | bytes 3538952 | tf_op jit(solution)/shard_map/ppermute | solution.py:25
  69.6 3.3 %copy-start.7 = (bf16[8,64,768]{2,1,0:T(8,128)(2,1)S(1)}, bf16[8,64,768]{2,1,0:T(8,128)(2,1)}, u32[]{:S(2)}) copy-start(bf16[8,64,768]{2,1,0:T(8,128)(2,1)} %get-tuple-element.132) | copy-start | bytes 2359300
  71.2 28.1 %collective-permute-start.5 = (bf16[4,192,768]{2,1,0:T(8,128)(2,1)S(1)}, bf16[4,192,768]{2,1,0:T(8,128)(2,1)S(1)}, u32[]{:S(2)}, u32[]{:S(2)}) collective-permute-start(bf16[4,192,768]{2,1,0:T(8,128)(2,1)S(1)} %fusion.refs_8_), channel_id=1, source_target_pairs={{0,2},{1,3},{2,0},{3,1},{4,6},{5,7},{6,4},{7,5},{8,10},{9,11},{10,... | collective-permute-start | bytes 3538952 | tf_op jit(solution)/shard_map/ppermute | solution.py:25
  72.8 28.3 %collective-permute-start.3 = (bf16[8,64,768]{2,1,0:T(8,128)(2,1)S(1)}, bf16[8,64,768]{2,1,0:T(8,128)(2,1)S(1)}, u32[]{:S(2)}, u32[]{:S(2)}) collective-permute-start(bf16[8,64,768]{2,1,0:T(8,128)(2,1)S(1)} %copy-done.7), channel_id=1, source_target_pairs={{0,16},{16,0},{1,17},{17,1},{2,18},{18,2},{3,19},{19,3},{4,20},{20... | collective-permute-start | bytes 2359304 | tf_op jit(solution)/shard_map/ppermute | solution.py:25
  74.1 25.2 %copy-start = (bf16[2,4,192,768]{3,2,1,0:T(8,128)(2,1)S(1)}, bf16[2,4,192,768]{3,2,1,0:T(8,128)(2,1)}, u32[]{:S(2)}) copy-start(bf16[2,4,192,768]{3,2,1,0:T(8,128)(2,1)} %get-tuple-element.133) | copy-start | bytes 7077892
  95.7 6.0 %collective-permute-start.8 = (bf16[8,48,3072]{2,1,0:T(8,128)(2,1)}, bf16[8,48,3072]{2,1,0:T(8,128)(2,1)S(1)}, u32[]{:S(2)}, u32[]{:S(2)}) collective-permute-start(bf16[8,48,3072]{2,1,0:T(8,128)(2,1)} %get-tuple-element.154), channel_id=1, source_target_pairs={{0,1},{1,0},{2,3},{3,2},{4,5},{5,4},{6,7},{7,6},{8,9},{9,8},{10,11... | collective-permute-start | bytes 7077896 | tf_op jit(solution)/shard_map/ppermute | solution.py:25
  99.5 2.2 %copy-start.1 = (bf16[8,48,3072]{2,1,0:T(8,128)(2,1)S(1)}, bf16[8,48,3072]{2,1,0:T(8,128)(2,1)}, u32[]{:S(2)}) copy-start(bf16[8,48,3072]{2,1,0:T(8,128)(2,1)} %get-tuple-element.153) | copy-start | bytes 7077892
  99.6 18.0 %collective-permute-start.7 = (bf16[2,192,768]{2,1,0:T(8,128)(2,1)S(1)}, bf16[2,192,768]{2,1,0:T(8,128)(2,1)S(1)}, u32[]{:S(2)}, u32[]{:S(2)}) collective-permute-start(bf16[2,192,768]{2,1,0:T(8,128)(2,1)S(1)} %add_convert_fusion.3), channel_id=1, source_target_pairs={{0,4},{1,5},{2,6},{3,7},{4,0},{5,1},{6,2},{7,3},{8,12},{9,13},{10,... | collective-permute-start | bytes 1769480 | tf_op jit(solution)/shard_map/ppermute | solution.py:25
  102.2 38.3 %collective-permute-start.11 = (bf16[8,48,1536]{2,1,0:T(8,128)(2,1)S(1)}, bf16[8,48,1536]{2,1,0:T(8,128)(2,1)S(1)}, u32[]{:S(2)}, u32[]{:S(2)}) collective-permute-start(bf16[8,48,1536]{2,1,0:T(8,128)(2,1)S(1)} %add_convert_fusion.refs_6_), channel_id=1, source_target_pairs={{0,16},{16,0},{1,17},{17,1},{2,18},{18,2},{3,19},{19,3},{4,20},{20... | collective-permute-start | bytes 3538952 | tf_op jit(solution)/shard_map/ppermute | solution.py:25
  117.8 23.5 %collective-permute-start.16 = (bf16[1,192,768]{2,1,0:T(8,128)(2,1)S(1)}, bf16[1,192,768]{2,1,0:T(8,128)(2,1)S(1)}, u32[]{:S(2)}, u32[]{:S(2)}) collective-permute-start(bf16[1,192,768]{2,1,0:T(8,128)(2,1)S(1)} %add_convert_fusion.8.refs_2_), channel_id=1, source_target_pairs={{0,8},{1,9},{2,10},{3,11},{4,12},{5,13},{6,14},{7,15},{8,0},{9,1},... | collective-permute-start | bytes 884744 | tf_op jit(solution)/shard_map/ppermute | solution.py:25
  120.4 4.2 %collective-permute-start.9 = (bf16[4,48,2304]{2,1,0:T(8,128)(2,1)}, bf16[4,48,2304]{2,1,0:T(8,128)(2,1)S(1)}, u32[]{:S(2)}, u32[]{:S(2)}) collective-permute-start(bf16[4,48,2304]{2,1,0:T(8,128)(2,1)} %get-tuple-element.168), channel_id=1, source_target_pairs={{0,1},{1,0},{2,3},{3,2},{4,5},{5,4},{6,7},{7,6},{8,9},{9,8},{10,11... | collective-permute-start | bytes 2654216 | tf_op jit(solution)/shard_map/ppermute | solution.py:25
  120.4 22.1 %collective-permute-start.15 = (bf16[4,48,2304]{2,1,0:T(8,128)(2,1)}, bf16[4,48,2304]{2,1,0:T(8,128)(2,1)S(1)}, u32[]{:S(2)}, u32[]{:S(2)}) collective-permute-start(bf16[4,48,2304]{2,1,0:T(8,128)(2,1)} %get-tuple-element.177), channel_id=1, source_target_pairs={{0,1},{1,0},{2,3},{3,2},{4,5},{5,4},{6,7},{7,6},{8,9},{9,8},{10,11... | collective-permute-start | bytes 2654216 | tf_op jit(solution)/shard_map/ppermute | solution.py:25
  120.9 3.7 %copy-start.2 = (bf16[8,48,2304]{2,1,0:T(8,128)(2,1)S(1)}, bf16[8,48,2304]{2,1,0:T(8,128)(2,1)}, u32[]{:S(2)}) copy-start(bf16[8,48,2304]{2,1,0:T(8,128)(2,1)} %get-tuple-element.167) | copy-start | bytes 5308420
  124.9 22.6 %collective-permute-start.14 = (bf16[4,48,2304]{2,1,0:T(8,128)(2,1)S(1)}, bf16[4,48,2304]{2,1,0:T(8,128)(2,1)S(1)}, u32[]{:S(2)}, u32[]{:S(2)}) collective-permute-start(bf16[4,48,2304]{2,1,0:T(8,128)(2,1)S(1)} %add_convert_fusion.1.refs_11_), channel_id=1, source_target_pairs={{0,2},{1,3},{2,0},{3,1},{4,6},{5,7},{6,4},{7,5},{8,10},{9,11},{10,... | collective-permute-start | bytes 2654216 | tf_op jit(solution)/shard_map/ppermute | solution.py:25
  140.4 1.1 copy-start.6
  140.4 8.0 %collective-permute-start.13 = (bf16[4,48,896]{2,1,0:T(8,128)(2,1)}, bf16[4,48,896]{2,1,0:T(8,128)(2,1)S(1)}, u32[]{:S(2)}, u32[]{:S(2)}) collective-permute-start(bf16[4,48,896]{2,1,0:T(8,128)(2,1)} %get-tuple-element.176), channel_id=1, source_target_pairs={{0,1},{1,0},{2,3},{3,2},{4,5},{5,4},{6,7},{7,6},{8,9},{9,8},{10,11... | collective-permute-start | bytes 1032200 | tf_op jit(solution)/shard_map/ppermute | solution.py:25
  140.5 22.1 %collective-permute-start.20 = (bf16[4,48,896]{2,1,0:T(8,128)(2,1)}, bf16[4,48,896]{2,1,0:T(8,128)(2,1)S(1)}, u32[]{:S(2)}, u32[]{:S(2)}) collective-permute-start(bf16[4,48,896]{2,1,0:T(8,128)(2,1)} %get-tuple-element.189), channel_id=1, source_target_pairs={{0,1},{1,0},{2,3},{3,2},{4,5},{5,4},{6,7},{7,6},{8,9},{9,8},{10,11... | collective-permute-start | bytes 1032200 | tf_op jit(solution)/shard_map/ppermute | solution.py:25
  141.6 8.0 %copy-start.3 = (bf16[8,48,896]{2,1,0:T(8,128)(2,1)S(1)}, bf16[8,48,896]{2,1,0:T(8,128)(2,1)}, u32[]{:S(2)}) copy-start(bf16[8,48,896]{2,1,0:T(8,128)(2,1)} %get-tuple-element.186) | copy-start | bytes 2064388
  141.6 43.1 %collective-permute-start.10 = (bf16[8,64,768]{2,1,0:T(8,128)(2,1)S(1)}, bf16[8,64,768]{2,1,0:T(8,128)(2,1)S(1)}, u32[]{:S(2)}, u32[]{:S(2)}) collective-permute-start(bf16[8,64,768]{2,1,0:T(8,128)(2,1)S(1)} %copy-done.6), channel_id=1, source_target_pairs={{0,16},{16,0},{1,17},{17,1},{2,18},{18,2},{3,19},{19,3},{4,20},{20... | collective-permute-start | bytes 2359304 | tf_op jit(solution)/shard_map/ppermute | solution.py:25
  142.6 16.6 %collective-permute-start.12 = (bf16[4,48,1536]{2,1,0:T(8,128)(2,1)S(1)}, bf16[4,48,1536]{2,1,0:T(8,128)(2,1)S(1)}, u32[]{:S(2)}, u32[]{:S(2)}) collective-permute-start(bf16[4,48,1536]{2,1,0:T(8,128)(2,1)S(1)} %add_convert_fusion.2), channel_id=1, source_target_pairs={{0,2},{1,3},{2,0},{3,1},{4,6},{5,7},{6,4},{7,5},{8,10},{9,11},{10,... | collective-permute-start | bytes 1769480 | tf_op jit(solution)/shard_map/ppermute | solution.py:25
  147.5 23.5 %collective-permute-start.18 = (bf16[192,768]{1,0:T(8,128)(2,1)S(1)}, bf16[192,768]{1,0:T(8,128)(2,1)S(1)}, u32[]{:S(2)}, u32[]{:S(2)}) collective-permute-start(bf16[192,768]{1,0:T(8,128)(2,1)S(1)} %bitcast.42), channel_id=1, source_target_pairs={{0,16},{16,0},{1,17},{17,1},{2,18},{18,2},{3,19},{19,3},{4,20},{20... | collective-permute-start | bytes 884744 | tf_op jit(solution)/shard_map/ppermute | solution.py:25
  148.5 12.5 %collective-permute-start.21 = (bf16[2,48,2304]{2,1,0:T(8,128)(2,1)S(1)}, bf16[2,48,2304]{2,1,0:T(8,128)(2,1)S(1)}, u32[]{:S(2)}, u32[]{:S(2)}) collective-permute-start(bf16[2,48,2304]{2,1,0:T(8,128)(2,1)S(1)} %add_convert_fusion.4), channel_id=1, source_target_pairs={{0,4},{1,5},{2,6},{3,7},{4,0},{5,1},{6,2},{7,3},{8,12},{9,13},{10,... | collective-permute-start | bytes 1327112 | tf_op jit(solution)/shard_map/ppermute | solution.py:25
  159.3 11.7 %collective-permute-start.17 = (bf16[2,48,1536]{2,1,0:T(8,128)(2,1)S(1)}, bf16[2,48,1536]{2,1,0:T(8,128)(2,1)S(1)}, u32[]{:S(2)}, u32[]{:S(2)}) collective-permute-start(bf16[2,48,1536]{2,1,0:T(8,128)(2,1)S(1)} %add_convert_fusion.6.refs_0_), channel_id=1, source_target_pairs={{0,4},{1,5},{2,6},{3,7},{4,0},{5,1},{6,2},{7,3},{8,12},{9,13},{10,... | collective-permute-start | bytes 884744 | tf_op jit(solution)/shard_map/ppermute | solution.py:25
  161.0 8.9 %collective-permute-start.19 = (bf16[4,48,896]{2,1,0:T(8,128)(2,1)S(1)}, bf16[4,48,896]{2,1,0:T(8,128)(2,1)S(1)}, u32[]{:S(2)}, u32[]{:S(2)}) collective-permute-start(bf16[4,48,896]{2,1,0:T(8,128)(2,1)S(1)} %add_convert_fusion.5), channel_id=1, source_target_pairs={{0,2},{1,3},{2,0},{3,1},{4,6},{5,7},{6,4},{7,5},{8,10},{9,11},{10,... | collective-permute-start | bytes 1032200 | tf_op jit(solution)/shard_map/ppermute | solution.py:25
  162.7 14.4 %collective-permute-start.24 = (bf16[1,48,2304]{2,1,0:T(8,128)(2,1)S(1)}, bf16[1,48,2304]{2,1,0:T(8,128)(2,1)S(1)}, u32[]{:S(2)}, u32[]{:S(2)}) collective-permute-start(bf16[1,48,2304]{2,1,0:T(8,128)(2,1)S(1)} %add_convert_fusion.10), channel_id=1, source_target_pairs={{0,8},{1,9},{2,10},{3,11},{4,12},{5,13},{6,14},{7,15},{8,0},{9,1},... | collective-permute-start | bytes 663560 | tf_op jit(solution)/shard_map/ppermute | solution.py:25
  169.9 7.9 %collective-permute-start.23 = (bf16[2,48,896]{2,1,0:T(8,128)(2,1)S(1)}, bf16[2,48,896]{2,1,0:T(8,128)(2,1)S(1)}, u32[]{:S(2)}, u32[]{:S(2)}) collective-permute-start(bf16[2,48,896]{2,1,0:T(8,128)(2,1)S(1)} %add_convert_fusion.11), channel_id=1, source_target_pairs={{0,4},{1,5},{2,6},{3,7},{4,0},{5,1},{6,2},{7,3},{8,12},{9,13},{10,... | collective-permute-start | bytes 516104 | tf_op jit(solution)/shard_map/ppermute | solution.py:25
  171.1 11.4 %collective-permute-start.22 = (bf16[1,48,1536]{2,1,0:T(8,128)(2,1)S(1)}, bf16[1,48,1536]{2,1,0:T(8,128)(2,1)S(1)}, u32[]{:S(2)}, u32[]{:S(2)}) collective-permute-start(bf16[1,48,1536]{2,1,0:T(8,128)(2,1)S(1)} %add_convert_fusion.13.refs_0_), channel_id=1, source_target_pairs={{0,8},{1,9},{2,10},{3,11},{4,12},{5,13},{6,14},{7,15},{8,0},{9,1},... | collective-permute-start | bytes 442376 | tf_op jit(solution)/shard_map/ppermute | solution.py:25
  177.9 10.5 %collective-permute-start.27 = (bf16[1,48,896]{2,1,0:T(8,128)(2,1)S(1)}, bf16[1,48,896]{2,1,0:T(8,128)(2,1)S(1)}, u32[]{:S(2)}, u32[]{:S(2)}) collective-permute-start(bf16[1,48,896]{2,1,0:T(8,128)(2,1)S(1)} %add_convert_fusion.15), channel_id=1, source_target_pairs={{0,8},{1,9},{2,10},{3,11},{4,12},{5,13},{6,14},{7,15},{8,0},{9,1},... | collective-permute-start | bytes 258056 | tf_op jit(solution)/shard_map/ppermute | solution.py:25
  182.6 7.6 %collective-permute-start.25 = (bf16[48,1536]{1,0:T(8,128)(2,1)S(1)}, bf16[48,1536]{1,0:T(8,128)(2,1)S(1)}, u32[]{:S(2)}, u32[]{:S(2)}) collective-permute-start(bf16[48,1536]{1,0:T(8,128)(2,1)S(1)} %bitcast.27), channel_id=1, source_target_pairs={{0,16},{16,0},{1,17},{17,1},{2,18},{18,2},{3,19},{19,3},{4,20},{20... | collective-permute-start | bytes 442376 | tf_op jit(solution)/shard_map/ppermute | solution.py:25
  183.4 9.6 %collective-permute-start.26 = (bf16[48,2304]{1,0:T(8,128)(2,1)S(1)}, bf16[48,2304]{1,0:T(8,128)(2,1)S(1)}, u32[]{:S(2)}, u32[]{:S(2)}) collective-permute-start(bf16[48,2304]{1,0:T(8,128)(2,1)S(1)} %bitcast.25), channel_id=1, source_target_pairs={{0,16},{16,0},{1,17},{17,1},{2,18},{18,2},{3,19},{19,3},{4,20},{20... | collective-permute-start | bytes 663560 | tf_op jit(solution)/shard_map/ppermute | solution.py:25
  188.5 4.6 %collective-permute-start.28 = (bf16[48,896]{1,0:T(8,128)(2,1)S(1)}, bf16[48,896]{1,0:T(8,128)(2,1)S(1)}, u32[]{:S(2)}, u32[]{:S(2)}) collective-permute-start(bf16[48,896]{1,0:T(8,128)(2,1)S(1)} %bitcast.29), channel_id=1, source_target_pairs={{0,16},{16,0},{1,17},{17,1},{2,18},{18,2},{3,19},{19,3},{4,20},{20... | collective-permute-start | bytes 258056 | tf_op jit(solution)/shard_map/ppermute | solution.py:25

commit v4 on v3

--- a/solution.py
+++ b/solution.py
@@ -854,11 +854,11 @@
         b_qv[...] = small[0:2]
         gains[...] = small[2:4]
         biases[...] = small[4:8]
-        b_in[...] = small[8 : 8 + count]
+        b_in[...] = jnp.concatenate([small[8 + i : 9 + i] for i in range(count)], 1)
 
     operands = [each for piece in pieces for each in (piece.mine, piece.coming)]
     shapes = [(shard, inner_width), (shard, width), (shard, 3 * width)]
-    shapes += [(2, shard), (2, shard), (4, shard), (count, shard)]
+    shapes += [(2, shard), (2, shard), (4, shard), (1, count * shard)]
     return call(
         kernel,
         scalars,
@@ -996,11 +996,10 @@
         qkv_b.step()
         grad_back = back.result()
         inner.step()
-        pause(scalars)
+        grad_rows = scatter_home(scalars, d_kept, d_back, half).reshape(1, -1, width)
         qkv_a.step()
         qkv_b.step()
         inner.step()
-        grad_rows = scatter_home(scalars, d_kept, d_back, half).reshape(1, -1, width)
         qkv_b.step()
         grad_in, grad_out, grad_qkv, *small = finish(
             scalars, inner, qkv_a, qkv_b, width, inner_width, groups

time: 197 us -> 195 us (0.990)
    pallas_call x15 -> x14, Pallas kernels: 114 us -> 114 us  [call(): pl.pallas_call(wrapped, grid_spec=pltpu.PrefetchScalarGridSpec(num_scalar...]
  transfers between devices with their start and end apart: 29 -> 29, of which waited for: 10 -> 11; matrix products, arithmetic and copies ran while one was open for 3% -> 3% of each run, Pallas kernels for 43% -> 43%
where the time goes in v4:
time: 195 us
  Pallas kernels  114 us (58%)
  waiting for transfers between devices  43.9 us (23%)
  starting transfers between devices  28.5 us (15%)
  other arithmetic  5.83 us (3%)
    pallas_call x14, Pallas kernels, call(): pl.pallas_call(wrapped, grid_spec=pltpu.PrefetchScalarGridSpec(num_scalar...  114 us
    ppermute x29, waiting for transfers between devices, flipped(): return lax.ppermute(value, axis, pairs)  43.9 us
    ppermute x29, starting transfers between devices, flipped(): return lax.ppermute(value, axis, pairs)  28.5 us
    convert_element_type x17, other arithmetic, step(): total = total.astype(BF16)  4.19 us
  transfers between devices with their start and end apart: 29, of which 11 were waited for; matrix products, arithmetic and copies ran while one was open for 3% of the time, Pallas kernels for 43%

profile of v4, /device:TPU:0, one launch (start us, length us, event | category | flops | bytes accessed | tf_op | source)
XLA Modules:
  0.0 194.6 jit_solution(1860937583623978196)
XLA Ops:
  0.6 2.5 %gather_sent.3 = (bf16[4,64,768]{2,1,0:T(8,128)(2,1)}, f32[8,128]{1,0:T(8,128)}) custom-call(s32[16]{0:T(128)} %bitcast.49, bf16[16,64,768]{2,1,0:T(8,128)(2,1)} %bitcast.35), custom_call_target="tpu_custom_call" | custom-call | flops 10000000 | bytes 1048576 | tf_op jit(solution)/shard_map/gather_sent/pallas_call | solution.py:72
  3.1 3.0 %collective-permute-start = (bf16[4,64,768]{2,1,0:T(8,128)(2,1)}, bf16[4,64,768]{2,1,0:T(8,128)(2,1)S(1)}, u32[]{:S(2)}, u32[]{:S(2)}) collective-permute-start(bf16[4,64,768]{2,1,0:T(8,128)(2,1)} %get-tuple-element.114), channel_id=1, source_target_pairs={{0,16},{16,0},{1,17},{17,1},{2,18},{18,2},{3,19},{19,3},{4,20},{20... | collective-permute-start | bytes 1179656 | tf_op jit(solution)/shard_map/ppermute | solution.py:25
  6.2 2.6 %gather_sent.4 = (bf16[4,64,768]{2,1,0:T(8,128)(2,1)}, f32[8,128]{1,0:T(8,128)}) custom-call(s32[16]{0:T(128)} %bitcast.50, bf16[16,64,768]{2,1,0:T(8,128)(2,1)} %bitcast.36, f32[8,128]{1,0:T(8,128)} %get-tuple-element.115.refs_1_), custom_call_target="tpu_custom_call" | custom-call | flops 10000000 | bytes 1048576 | tf_op jit(solution)/shard_map/gather_sent/pallas_call | solution.py:72
  8.9 2.8 %gather_sent.5 = (bf16[8,64,768]{2,1,0:T(8,128)(2,1)}, f32[8,128]{1,0:T(8,128)}) custom-call(s32[16]{0:T(128)} %bitcast.51, bf16[16,64,768]{2,1,0:T(8,128)(2,1)} %bitcast.32, f32[8,128]{1,0:T(8,128)} %get-tuple-element.116.refs_1_), custom_call_target="tpu_custom_call" | custom-call | flops 10000000 | bytes 1048576 | tf_op jit(solution)/shard_map/gather_sent/pallas_call | solution.py:72
  11.7 4.6 %collective-permute-done.refs_2_ = bf16[4,64,768]{2,1,0:T(8,128)(2,1)S(1)} collective-permute-done((bf16[4,64,768]{2,1,0:T(8,128)(2,1)}, bf16[4,64,768]{2,1,0:T(8,128)(2,1)S(1)}, u32[]{:S(2)}, u32[]{:S(2)}) %collective-permute-start) | collective-permute-done | bytes 393248 | tf_op jit(solution)/shard_map/ppermute | solution.py:25
  16.6 2.1 %collective-permute-start.2 = (bf16[8,64,768]{2,1,0:T(8,128)(2,1)}, bf16[8,64,768]{2,1,0:T(8,128)(2,1)S(1)}, u32[]{:S(2)}, u32[]{:S(2)}) collective-permute-start(bf16[8,64,768]{2,1,0:T(8,128)(2,1)} %get-tuple-element.127), channel_id=1, source_target_pairs={{0,16},{16,0},{1,17},{17,1},{2,18},{18,2},{3,19},{19,3},{4,20},{20... | collective-permute-start | bytes 2359304 | tf_op jit(solution)/shard_map/ppermute | solution.py:25
  18.6 0.6 gather_fusion
  19.3 5.7 %fetch.1 = (bf16[768,2304]{1,0:T(8,128)(2,1)S(1)}, bf16[768,768]{1,0:T(8,128)(2,1)S(1)}, bf16[768,3072]{1,0:T(8,128)(2,1)S(1)}, bf16[3072,768]{1,0:T(8,128)(2,1)S(1)}, f32[8,128]{1,0:T(8,128)}) custom-call(s32[20]{0:T(128)S(1)} %concatenate.6.scalars_ref, bf16[768,2304]{1,0:T(8,128)(2,1)} %refs_0_.1, bf16[768,768]{1,0:T(8,128)(2,1)} %refs_1_.1, ...), custom_call_target="tpu_custom_call" | custom-call | flops 10000000 | bytes 1048576 | tf_op jit(solution)/shard_map/fetch/pallas_call | solution.py:72
  25.0 0.7 pad_add_fusion
  25.7 0.7 copy-done.9
  26.4 14.8 %attention_forward.1 = (bf16[1024,768]{1,0:T(8,128)(2,1)S(1)}, bf16[1024,2304]{1,0:T(8,128)(2,1)}, bf16[8,6,256,128]{3,2,1,0:T(8,128)(2,1)}, bf16[1024,768]{1,0:...) custom-call(s32[20]{0:T(128)S(1)} %concatenate.6.scalars_ref, ...), custom_call_target="tpu_custom_call" | custom-call | flops 40000000000 | bytes 1048576 | tf_op jit(solution)/shard_map/attention_forward/pallas_call | solution.py:72
  41.2 25.3 %feed_forward.1 = (bf16[1024,3072]{1,0:T(8,128)(2,1)S(1)}, bf16[1024,768]{1,0:T(8,128)(2,1)S(1)}, bf16[8,64,768]{2,1,0:T(8,128)(2,1)}, bf16[8,64,768]{2,1,0:T(8,...) custom-call(s32[20]{0:T(128)S(1)} %concatenate.6.scalars_ref, ...), custom_call_target="tpu_custom_call" | custom-call | flops 4000000000 | bytes 1048576 | tf_op jit(solution)/shard_map/feed_forward/pallas_call | solution.py:72
  67.0 2.5 %collective-permute-done.4 = bf16[1,4,192,768]{3,2,1,0:T(8,128)(2,1)S(1)} collective-permute-done((bf16[1,4,192,768]{3,2,1,0:T(8,128)(2,1)}, bf16[1,4,192,768]{3,2,1,0:T(8,128)(2,1)S(1)}, u32[]{:S(2)}, u32[]{:S(2)}) %collective-permute-start.4) | collective-permute-done | bytes 1179680 | tf_op jit(solution)/shard_map/ppermute | solution.py:25
  69.6 1.7 fusion.refs_8_
  71.2 1.6 collective-permute-start.5
  72.8 1.2 collective-permute-start.3
  74.1 21.7 %feed_backward.1 = (bf16[1024,768]{1,0:T(8,128)(2,1)S(1)}, f32[8,768]{1,0:T(8,128)}, f32[8,3072]{1,0:T(8,128)}, bf16[8,48,3072]{2,1,0:T(8,128)(2,1)}, bf16[8,48,3072]{2,1,0:T(8,128)(2,1)}, /*index=5*/f32[8,128]{1,0:T(8,128)}) custom-call(s32[20]{0:T(128)S(1)} %concatenate.6.scalars_ref, bf16[1024,768]{1,0:T(8,128)(2,1)S(1)} %get-tuple-element.138.refs_0_, ...), custom_call_target="tpu_custom_call" | custom-call | flops 4000000000 | bytes 1048576 | tf_op jit(solution)/shard_map/feed_backward/pallas_call | solution.py:72
  95.7 3.6 %collective-permute-done.5 = bf16[4,192,768]{2,1,0:T(8,128)(2,1)S(1)} collective-permute-done((bf16[4,192,768]{2,1,0:T(8,128)(2,1)S(1)}, bf16[4,192,768]{2,1,0:T(8,128)(2,1)S(1)}, u32[]{:S(2)}, u32[]{:S(2)}) %collective-permute-start.5) | collective-permute-done | bytes 1179680 | tf_op jit(solution)/shard_map/ppermute | solution.py:25
  99.6 1.6 collective-permute-start.7
  101.2 0.5 pause.2.refs_7_
  102.2 1.3 collective-permute-start.11
  103.5 14.1 %attention_backward.2 = (bf16[1024,1536]{1,0:T(8,128)(2,1)S(1)}, f32[8,512]{1,0:T(8,128)}, bf16[4,48,2304]{2,1,0:T(8,128)(2,1)}, bf16[4,48,2304]{2,1,0:T(8,128)(...) custom-call(s32[20]{0:T(128)S(1)} %concatenate.6.scalars_ref, bf16[1024,768]{1,0:T(8,128)(2,1)S(1)} %get-tuple-element.148.refs_0_, ...), custom_call_target="tpu_custom_call" | custom-call | flops 4000000000 | bytes 1048576 | tf_op jit(solution)/shard_map/attention_backward/pallas_call | solution.py:72
  117.8 2.7 %collective-permute-start.16 = (bf16[1,192,768]{2,1,0:T(8,128)(2,1)S(1)}, bf16[1,192,768]{2,1,0:T(8,128)(2,1)S(1)}, u32[]{:S(2)}, u32[]{:S(2)}) collective-permute-start(bf16[1,192,768]{2,1,0:T(8,128)(2,1)S(1)} %add_convert_fusion.8.refs_2_), channel_id=1, source_target_pairs={{0,8},{1,9},{2,10},{3,11},{4,12},{5,13},{6,14},{7,15},{8,0},{9,1},... | collective-permute-start | bytes 884744 | tf_op jit(solution)/shard_map/ppermute | solution.py:25
  121.0 3.7 %scatter_home.2 = (bf16[16,64,768]{2,1,0:T(8,128)(2,1)}, f32[8,128]{1,0:T(8,128)}) custom-call(s32[20]{0:T(128)S(1)} %concatenate.6.scalars_ref, bf16[8,64,768]{2,1,0:T(8,128)(2,1)} %get-tuple-element.131.refs_0_, bf16[8,64,768]{2,1,0:T(8,128)(2,1)S(1)} %collective-permute-done.3.refs_1_, bf16[1,192,768]{2,1,0:T(8,128)(2,1)S(1)} %add_convert_fusion.8.refs_2_, ...), custom_call_target="tpu_custom_call" | custom-call | flops 20000000000 | bytes 1048576 | tf_op jit(solution)/shard_map/scatter_home/pallas_call | solution.py:72
  124.9 1.6 collective-permute-start.14
  126.5 14.0 %attention_backward.3 = (bf16[8,64,768]{2,1,0:T(8,128)(2,1)}, bf16[8,64,768]{2,1,0:T(8,128)(2,1)}, f32[8,256]{1,0:T(8,128)}, bf16[4,48,896]{2,1,0:T(8,128)(2,1)}...) custom-call(s32[20]{0:T(128)S(1)} %concatenate.6.scalars_ref, ...), custom_call_target="tpu_custom_call" | custom-call | flops 4000000000 | bytes 1048576 | tf_op jit(solution)/shard_map/attention_backward/pallas_call | solution.py:72
  141.6 0.8 collective-permute-start.10
  142.6 0.6 collective-permute-start.12
  143.2 4.3 %collective-permute-done.14 = bf16[4,48,2304]{2,1,0:T(8,128)(2,1)S(1)} collective-permute-done((bf16[4,48,2304]{2,1,0:T(8,128)(2,1)S(1)}, bf16[4,48,2304]{2,1,0:T(8,128)(2,1)S(1)}, u32[]{:S(2)}, u32[]{:S(2)}) %collective-permute-start.14) | collective-permute-done | bytes 884768 | tf_op jit(solution)/shard_map/ppermute | solution.py:25
  147.5 0.8 collective-permute-start.18
  148.5 1.1 collective-permute-start.21
  149.6 9.5 %collective-permute-done.12 = bf16[4,48,1536]{2,1,0:T(8,128)(2,1)S(1)} collective-permute-done((bf16[4,48,1536]{2,1,0:T(8,128)(2,1)S(1)}, bf16[4,48,1536]{2,1,0:T(8,128)(2,1)S(1)}, u32[]{:S(2)}, u32[]{:S(2)}) %collective-permute-start.12) | collective-permute-done | bytes 589856 | tf_op jit(solution)/shard_map/ppermute | solution.py:25
  159.3 1.1 collective-permute-start.17
  161.0 1.6 collective-permute-start.19
  163.1 6.8 %collective-permute-done.19 = bf16[4,48,896]{2,1,0:T(8,128)(2,1)S(1)} collective-permute-done((bf16[4,48,896]{2,1,0:T(8,128)(2,1)S(1)}, bf16[4,48,896]{2,1,0:T(8,128)(2,1)S(1)}, u32[]{:S(2)}, u32[]{:S(2)}) %collective-permute-start.19) | collective-permute-done | bytes 344096 | tf_op jit(solution)/shard_map/ppermute | solution.py:25
  169.9 1.1 collective-permute-start.23
  171.1 1.1 collective-permute-start.22
  172.2 3.7 %scatter_home.3 = (bf16[16,64,768]{2,1,0:T(8,128)(2,1)}, f32[8,128]{1,0:T(8,128)}) custom-call(s32[20]{0:T(128)S(1)} %concatenate.6.scalars_ref, bf16[8,64,768]{2,1,0:T(8,128)(2,1)} %get-tuple-element.172.refs_0_, bf16[8,64,768]{2,1,0:T(8,128)(2,1)S(1)} %collective-permute-done.10.refs_1_, bf16[1,48,1536]{2,1,0:T(8,128)(2,1)S(1)} %add_convert_fusion.13.refs_2_, ...), custom_call_target="tpu_custom_call" | custom-call | flops 20000000000 | bytes 1048576 | tf_op jit(solution)/shard_map/scatter_home/pallas_call | solution.py:72
  176.0 1.1 collective-permute-done.24
  177.2 0.6 collective-permute-done.23
  178.1 4.3 %collective-permute-done.22 = bf16[1,48,1536]{2,1,0:T(8,128)(2,1)S(1)} collective-permute-done((bf16[1,48,1536]{2,1,0:T(8,128)(2,1)S(1)}, bf16[1,48,1536]{2,1,0:T(8,128)(2,1)S(1)}, u32[]{:S(2)}, u32[]{:S(2)}) %collective-permute-start.22) | collective-permute-done | bytes 147488 | tf_op jit(solution)/shard_map/ppermute | solution.py:25
  182.6 0.9 collective-permute-start.25
  183.4 1.2 collective-permute-start.26
  184.8 0.9 collective-permute-start.28
  185.6 0.9 convert_add_fusion.1
  186.5 3.0 %collective-permute-done.25.refs_1_ = bf16[48,1536]{1,0:T(8,128)(2,1)S(1)} collective-permute-done((bf16[48,1536]{1,0:T(8,128)(2,1)S(1)}, bf16[48,1536]{1,0:T(8,128)(2,1)S(1)}, u32[]{:S(2)}, u32[]{:S(2)}) %collective-permute-start.25) | collective-permute-done | bytes 147488 | tf_op jit(solution)/shard_map/ppermute | solution.py:25
  189.4 3.5 %collective-permute-done.28.refs_5_ = bf16[48,896]{1,0:T(8,128)(2,1)S(1)} collective-permute-done((bf16[48,896]{1,0:T(8,128)(2,1)S(1)}, bf16[48,896]{1,0:T(8,128)(2,1)S(1)}, u32[]{:S(2)}, u32[]{:S(2)}) %collective-permute-start.28) | collective-permute-done | bytes 86048 | tf_op jit(solution)/shard_map/ppermute | solution.py:25
  192.9 1.6 finish.1
  (71 shorter events, 6.1 us)
Async XLA Ops:
  3.1 13.2 %collective-permute-start = (bf16[4,64,768]{2,1,0:T(8,128)(2,1)}, bf16[4,64,768]{2,1,0:T(8,128)(2,1)S(1)}, u32[]{:S(2)}, u32[]{:S(2)}) collective-permute-start(bf16[4,64,768]{2,1,0:T(8,128)(2,1)} %get-tuple-element.114), channel_id=1, source_target_pairs={{0,16},{16,0},{1,17},{17,1},{2,18},{18,2},{3,19},{19,3},{4,20},{20... | collective-permute-start | bytes 1179656 | tf_op jit(solution)/shard_map/ppermute | solution.py:25
  6.1 10.2 %copy-start.5 = (s32[2,1024]{1,0:T(2,128)S(1)}, s32[2,1024]{1,0:T(2,128)}, u32[]{:S(2)}) copy-start(s32[2,1024]{1,0:T(2,128)} %param.14) | copy-start | bytes 24580
  6.1 10.2 %copy-start.4 = (s32[1,16]{1,0:T(1,128)S(1)}, s32[1,16]{1,0:T(1,128)}, u32[]{:S(2)}) copy-start(s32[1,16]{1,0:T(1,128)} %param.15) | copy-start | bytes 196
  8.8 16.9 %collective-permute-start.1 = (bf16[4,64,768]{2,1,0:T(8,128)(2,1)}, bf16[4,64,768]{2,1,0:T(8,128)(2,1)S(1)}, u32[]{:S(2)}, u32[]{:S(2)}) collective-permute-start(bf16[4,64,768]{2,1,0:T(8,128)(2,1)} %get-tuple-element.120), channel_id=1, source_target_pairs={{0,16},{16,0},{1,17},{17,1},{2,18},{18,2},{3,19},{19,3},{4,20},{20... | collective-permute-start | bytes 1179656 | tf_op jit(solution)/shard_map/ppermute | solution.py:25
  16.3 8.7 %copy-start.8 = (bf16[4,64,768]{2,1,0:T(8,128)(2,1)}, bf16[4,64,768]{2,1,0:T(8,128)(2,1)S(1)}, u32[]{:S(2)}) copy-start(bf16[4,64,768]{2,1,0:T(8,128)(2,1)S(1)} %collective-permute-done.refs_2_) | copy-start | bytes 1179652
  16.6 24.7 %collective-permute-start.2 = (bf16[8,64,768]{2,1,0:T(8,128)(2,1)}, bf16[8,64,768]{2,1,0:T(8,128)(2,1)S(1)}, u32[]{:S(2)}, u32[]{:S(2)}) collective-permute-start(bf16[8,64,768]{2,1,0:T(8,128)(2,1)} %get-tuple-element.127), channel_id=1, source_target_pairs={{0,16},{16,0},{1,17},{17,1},{2,18},{18,2},{3,19},{19,3},{4,20},{20... | collective-permute-start | bytes 2359304 | tf_op jit(solution)/shard_map/ppermute | solution.py:25
  25.7 0.7 copy-start.9
  66.5 3.1 %collective-permute-start.4 = (bf16[1,4,192,768]{3,2,1,0:T(8,128)(2,1)}, bf16[1,4,192,768]{3,2,1,0:T(8,128)(2,1)S(1)}, u32[]{:S(2)}, u32[]{:S(2)}) collective-permute-start(bf16[1,4,192,768]{3,2,1,0:T(8,128)(2,1)} %get-tuple-element.134), channel_id=1, source_target_pairs={{0,1},{1,0},{2,3},{3,2},{4,5},{5,4},{6,7},{7,6},{8,9},{9,8},{10,11... | collective-permute-start | bytes 3538952 | tf_op jit(solution)/shard_map/ppermute | solution.py:25
  66.5 29.2 %collective-permute-start.6 = (bf16[1,4,192,768]{3,2,1,0:T(8,128)(2,1)}, bf16[1,4,192,768]{3,2,1,0:T(8,128)(2,1)S(1)}, u32[]{:S(2)}, u32[]{:S(2)}) collective-permute-start(bf16[1,4,192,768]{3,2,1,0:T(8,128)(2,1)} %get-tuple-element.137), channel_id=1, source_target_pairs={{0,1},{1,0},{2,3},{3,2},{4,5},{5,4},{6,7},{7,6},{8,9},{9,8},{10,11... | collective-permute-start | bytes 3538952 | tf_op jit(solution)/shard_map/ppermute | solution.py:25
  69.6 3.3 %copy-start.7 = (bf16[8,64,768]{2,1,0:T(8,128)(2,1)S(1)}, bf16[8,64,768]{2,1,0:T(8,128)(2,1)}, u32[]{:S(2)}) copy-start(bf16[8,64,768]{2,1,0:T(8,128)(2,1)} %get-tuple-element.132) | copy-start | bytes 2359300
  71.2 28.1 %collective-permute-start.5 = (bf16[4,192,768]{2,1,0:T(8,128)(2,1)S(1)}, bf16[4,192,768]{2,1,0:T(8,128)(2,1)S(1)}, u32[]{:S(2)}, u32[]{:S(2)}) collective-permute-start(bf16[4,192,768]{2,1,0:T(8,128)(2,1)S(1)} %fusion.refs_8_), channel_id=1, source_target_pairs={{0,2},{1,3},{2,0},{3,1},{4,6},{5,7},{6,4},{7,5},{8,10},{9,11},{10,... | collective-permute-start | bytes 3538952 | tf_op jit(solution)/shard_map/ppermute | solution.py:25
  72.8 28.4 %collective-permute-start.3 = (bf16[8,64,768]{2,1,0:T(8,128)(2,1)S(1)}, bf16[8,64,768]{2,1,0:T(8,128)(2,1)S(1)}, u32[]{:S(2)}, u32[]{:S(2)}) collective-permute-start(bf16[8,64,768]{2,1,0:T(8,128)(2,1)S(1)} %copy-done.7), channel_id=1, source_target_pairs={{0,16},{16,0},{1,17},{17,1},{2,18},{18,2},{3,19},{19,3},{4,20},{20... | collective-permute-start | bytes 2359304 | tf_op jit(solution)/shard_map/ppermute | solution.py:25
  74.1 25.2 %copy-start.1 = (bf16[2,4,192,768]{3,2,1,0:T(8,128)(2,1)S(1)}, bf16[2,4,192,768]{3,2,1,0:T(8,128)(2,1)}, u32[]{:S(2)}) copy-start(bf16[2,4,192,768]{3,2,1,0:T(8,128)(2,1)} %get-tuple-element.133) | copy-start | bytes 7077892
  95.7 6.0 %collective-permute-start.8 = (bf16[8,48,3072]{2,1,0:T(8,128)(2,1)}, bf16[8,48,3072]{2,1,0:T(8,128)(2,1)S(1)}, u32[]{:S(2)}, u32[]{:S(2)}) collective-permute-start(bf16[8,48,3072]{2,1,0:T(8,128)(2,1)} %get-tuple-element.154), channel_id=1, source_target_pairs={{0,1},{1,0},{2,3},{3,2},{4,5},{5,4},{6,7},{7,6},{8,9},{9,8},{10,11... | collective-permute-start | bytes 7077896 | tf_op jit(solution)/shard_map/ppermute | solution.py:25
  99.6 2.2 %copy-start = (bf16[8,48,3072]{2,1,0:T(8,128)(2,1)S(1)}, bf16[8,48,3072]{2,1,0:T(8,128)(2,1)}, u32[]{:S(2)}) copy-start(bf16[8,48,3072]{2,1,0:T(8,128)(2,1)} %get-tuple-element.153) | copy-start | bytes 7077892
  99.6 18.0 %collective-permute-start.7 = (bf16[2,192,768]{2,1,0:T(8,128)(2,1)S(1)}, bf16[2,192,768]{2,1,0:T(8,128)(2,1)S(1)}, u32[]{:S(2)}, u32[]{:S(2)}) collective-permute-start(bf16[2,192,768]{2,1,0:T(8,128)(2,1)S(1)} %add_convert_fusion.3), channel_id=1, source_target_pairs={{0,4},{1,5},{2,6},{3,7},{4,0},{5,1},{6,2},{7,3},{8,12},{9,13},{10,... | collective-permute-start | bytes 1769480 | tf_op jit(solution)/shard_map/ppermute | solution.py:25
  102.2 38.4 %collective-permute-start.11 = (bf16[8,48,1536]{2,1,0:T(8,128)(2,1)S(1)}, bf16[8,48,1536]{2,1,0:T(8,128)(2,1)S(1)}, u32[]{:S(2)}, u32[]{:S(2)}) collective-permute-start(bf16[8,48,1536]{2,1,0:T(8,128)(2,1)S(1)} %add_convert_fusion.refs_6_), channel_id=1, source_target_pairs={{0,16},{16,0},{1,17},{17,1},{2,18},{18,2},{3,19},{19,3},{4,20},{20... | collective-permute-start | bytes 3538952 | tf_op jit(solution)/shard_map/ppermute | solution.py:25
  117.8 23.6 %collective-permute-start.16 = (bf16[1,192,768]{2,1,0:T(8,128)(2,1)S(1)}, bf16[1,192,768]{2,1,0:T(8,128)(2,1)S(1)}, u32[]{:S(2)}, u32[]{:S(2)}) collective-permute-start(bf16[1,192,768]{2,1,0:T(8,128)(2,1)S(1)} %add_convert_fusion.8.refs_2_), channel_id=1, source_target_pairs={{0,8},{1,9},{2,10},{3,11},{4,12},{5,13},{6,14},{7,15},{8,0},{9,1},... | collective-permute-start | bytes 884744 | tf_op jit(solution)/shard_map/ppermute | solution.py:25
  120.4 4.2 %collective-permute-start.9 = (bf16[4,48,2304]{2,1,0:T(8,128)(2,1)}, bf16[4,48,2304]{2,1,0:T(8,128)(2,1)S(1)}, u32[]{:S(2)}, u32[]{:S(2)}) collective-permute-start(bf16[4,48,2304]{2,1,0:T(8,128)(2,1)} %get-tuple-element.168), channel_id=1, source_target_pairs={{0,1},{1,0},{2,3},{3,2},{4,5},{5,4},{6,7},{7,6},{8,9},{9,8},{10,11... | collective-permute-start | bytes 2654216 | tf_op jit(solution)/shard_map/ppermute | solution.py:25
  120.4 22.1 %collective-permute-start.15 = (bf16[4,48,2304]{2,1,0:T(8,128)(2,1)}, bf16[4,48,2304]{2,1,0:T(8,128)(2,1)S(1)}, u32[]{:S(2)}, u32[]{:S(2)}) collective-permute-start(bf16[4,48,2304]{2,1,0:T(8,128)(2,1)} %get-tuple-element.177), channel_id=1, source_target_pairs={{0,1},{1,0},{2,3},{3,2},{4,5},{5,4},{6,7},{7,6},{8,9},{9,8},{10,11... | collective-permute-start | bytes 2654216 | tf_op jit(solution)/shard_map/ppermute | solution.py:25
  120.9 3.7 %copy-start.2 = (bf16[8,48,2304]{2,1,0:T(8,128)(2,1)S(1)}, bf16[8,48,2304]{2,1,0:T(8,128)(2,1)}, u32[]{:S(2)}) copy-start(bf16[8,48,2304]{2,1,0:T(8,128)(2,1)} %get-tuple-element.167) | copy-start | bytes 5308420
  124.9 22.6 %collective-permute-start.14 = (bf16[4,48,2304]{2,1,0:T(8,128)(2,1)S(1)}, bf16[4,48,2304]{2,1,0:T(8,128)(2,1)S(1)}, u32[]{:S(2)}, u32[]{:S(2)}) collective-permute-start(bf16[4,48,2304]{2,1,0:T(8,128)(2,1)S(1)} %add_convert_fusion.1.refs_11_), channel_id=1, source_target_pairs={{0,2},{1,3},{2,0},{3,1},{4,6},{5,7},{6,4},{7,5},{8,10},{9,11},{10,... | collective-permute-start | bytes 2654216 | tf_op jit(solution)/shard_map/ppermute | solution.py:25
  140.5 1.1 copy-start.6
  140.5 8.0 %collective-permute-start.13 = (bf16[4,48,896]{2,1,0:T(8,128)(2,1)}, bf16[4,48,896]{2,1,0:T(8,128)(2,1)S(1)}, u32[]{:S(2)}, u32[]{:S(2)}) collective-permute-start(bf16[4,48,896]{2,1,0:T(8,128)(2,1)} %get-tuple-element.176), channel_id=1, source_target_pairs={{0,1},{1,0},{2,3},{3,2},{4,5},{5,4},{6,7},{7,6},{8,9},{9,8},{10,11... | collective-permute-start | bytes 1032200 | tf_op jit(solution)/shard_map/ppermute | solution.py:25
  140.6 22.1 %collective-permute-start.20 = (bf16[4,48,896]{2,1,0:T(8,128)(2,1)}, bf16[4,48,896]{2,1,0:T(8,128)(2,1)S(1)}, u32[]{:S(2)}, u32[]{:S(2)}) collective-permute-start(bf16[4,48,896]{2,1,0:T(8,128)(2,1)} %get-tuple-element.189), channel_id=1, source_target_pairs={{0,1},{1,0},{2,3},{3,2},{4,5},{5,4},{6,7},{7,6},{8,9},{9,8},{10,11... | collective-permute-start | bytes 1032200 | tf_op jit(solution)/shard_map/ppermute | solution.py:25
  141.6 7.9 %copy-start.3 = (bf16[8,48,896]{2,1,0:T(8,128)(2,1)S(1)}, bf16[8,48,896]{2,1,0:T(8,128)(2,1)}, u32[]{:S(2)}) copy-start(bf16[8,48,896]{2,1,0:T(8,128)(2,1)} %get-tuple-element.186) | copy-start | bytes 2064388
  141.6 30.6 %collective-permute-start.10 = (bf16[8,64,768]{2,1,0:T(8,128)(2,1)S(1)}, bf16[8,64,768]{2,1,0:T(8,128)(2,1)S(1)}, u32[]{:S(2)}, u32[]{:S(2)}) collective-permute-start(bf16[8,64,768]{2,1,0:T(8,128)(2,1)S(1)} %copy-done.6), channel_id=1, source_target_pairs={{0,16},{16,0},{1,17},{17,1},{2,18},{18,2},{3,19},{19,3},{4,20},{20... | collective-permute-start | bytes 2359304 | tf_op jit(solution)/shard_map/ppermute | solution.py:25
  142.6 16.6 %collective-permute-start.12 = (bf16[4,48,1536]{2,1,0:T(8,128)(2,1)S(1)}, bf16[4,48,1536]{2,1,0:T(8,128)(2,1)S(1)}, u32[]{:S(2)}, u32[]{:S(2)}) collective-permute-start(bf16[4,48,1536]{2,1,0:T(8,128)(2,1)S(1)} %add_convert_fusion.2), channel_id=1, source_target_pairs={{0,2},{1,3},{2,0},{3,1},{4,6},{5,7},{6,4},{7,5},{8,10},{9,11},{10,... | collective-permute-start | bytes 1769480 | tf_op jit(solution)/shard_map/ppermute | solution.py:25
  147.5 23.5 %collective-permute-start.18 = (bf16[192,768]{1,0:T(8,128)(2,1)S(1)}, bf16[192,768]{1,0:T(8,128)(2,1)S(1)}, u32[]{:S(2)}, u32[]{:S(2)}) collective-permute-start(bf16[192,768]{1,0:T(8,128)(2,1)S(1)} %bitcast.43), channel_id=1, source_target_pairs={{0,16},{16,0},{1,17},{17,1},{2,18},{18,2},{3,19},{19,3},{4,20},{20... | collective-permute-start | bytes 884744 | tf_op jit(solution)/shard_map/ppermute | solution.py:25
  148.5 12.5 %collective-permute-start.21 = (bf16[2,48,2304]{2,1,0:T(8,128)(2,1)S(1)}, bf16[2,48,2304]{2,1,0:T(8,128)(2,1)S(1)}, u32[]{:S(2)}, u32[]{:S(2)}) collective-permute-start(bf16[2,48,2304]{2,1,0:T(8,128)(2,1)S(1)} %add_convert_fusion.4), channel_id=1, source_target_pairs={{0,4},{1,5},{2,6},{3,7},{4,0},{5,1},{6,2},{7,3},{8,12},{9,13},{10,... | collective-permute-start | bytes 1327112 | tf_op jit(solution)/shard_map/ppermute | solution.py:25
  159.3 11.7 %collective-permute-start.17 = (bf16[2,48,1536]{2,1,0:T(8,128)(2,1)S(1)}, bf16[2,48,1536]{2,1,0:T(8,128)(2,1)S(1)}, u32[]{:S(2)}, u32[]{:S(2)}) collective-permute-start(bf16[2,48,1536]{2,1,0:T(8,128)(2,1)S(1)} %add_convert_fusion.6.refs_0_), channel_id=1, source_target_pairs={{0,4},{1,5},{2,6},{3,7},{4,0},{5,1},{6,2},{7,3},{8,12},{9,13},{10,... | collective-permute-start | bytes 884744 | tf_op jit(solution)/shard_map/ppermute | solution.py:25
  161.0 8.9 %collective-permute-start.19 = (bf16[4,48,896]{2,1,0:T(8,128)(2,1)S(1)}, bf16[4,48,896]{2,1,0:T(8,128)(2,1)S(1)}, u32[]{:S(2)}, u32[]{:S(2)}) collective-permute-start(bf16[4,48,896]{2,1,0:T(8,128)(2,1)S(1)} %add_convert_fusion.5), channel_id=1, source_target_pairs={{0,2},{1,3},{2,0},{3,1},{4,6},{5,7},{6,4},{7,5},{8,10},{9,11},{10,... | collective-permute-start | bytes 1032200 | tf_op jit(solution)/shard_map/ppermute | solution.py:25
  162.7 14.4 %collective-permute-start.24 = (bf16[1,48,2304]{2,1,0:T(8,128)(2,1)S(1)}, bf16[1,48,2304]{2,1,0:T(8,128)(2,1)S(1)}, u32[]{:S(2)}, u32[]{:S(2)}) collective-permute-start(bf16[1,48,2304]{2,1,0:T(8,128)(2,1)S(1)} %add_convert_fusion.10), channel_id=1, source_target_pairs={{0,8},{1,9},{2,10},{3,11},{4,12},{5,13},{6,14},{7,15},{8,0},{9,1},... | collective-permute-start | bytes 663560 | tf_op jit(solution)/shard_map/ppermute | solution.py:25
  169.9 7.9 %collective-permute-start.23 = (bf16[2,48,896]{2,1,0:T(8,128)(2,1)S(1)}, bf16[2,48,896]{2,1,0:T(8,128)(2,1)S(1)}, u32[]{:S(2)}, u32[]{:S(2)}) collective-permute-start(bf16[2,48,896]{2,1,0:T(8,128)(2,1)S(1)} %add_convert_fusion.11), channel_id=1, source_target_pairs={{0,4},{1,5},{2,6},{3,7},{4,0},{5,1},{6,2},{7,3},{8,12},{9,13},{10,... | collective-permute-start | bytes 516104 | tf_op jit(solution)/shard_map/ppermute | solution.py:25
  171.1 11.3 %collective-permute-start.22 = (bf16[1,48,1536]{2,1,0:T(8,128)(2,1)S(1)}, bf16[1,48,1536]{2,1,0:T(8,128)(2,1)S(1)}, u32[]{:S(2)}, u32[]{:S(2)}) collective-permute-start(bf16[1,48,1536]{2,1,0:T(8,128)(2,1)S(1)} %add_convert_fusion.13.refs_2_), channel_id=1, source_target_pairs={{0,8},{1,9},{2,10},{3,11},{4,12},{5,13},{6,14},{7,15},{8,0},{9,1},... | collective-permute-start | bytes 442376 | tf_op jit(solution)/shard_map/ppermute | solution.py:25
  177.9 6.8 %collective-permute-start.27 = (bf16[1,48,896]{2,1,0:T(8,128)(2,1)S(1)}, bf16[1,48,896]{2,1,0:T(8,128)(2,1)S(1)}, u32[]{:S(2)}, u32[]{:S(2)}) collective-permute-start(bf16[1,48,896]{2,1,0:T(8,128)(2,1)S(1)} %add_convert_fusion.15), channel_id=1, source_target_pairs={{0,8},{1,9},{2,10},{3,11},{4,12},{5,13},{6,14},{7,15},{8,0},{9,1},... | collective-permute-start | bytes 258056 | tf_op jit(solution)/shard_map/ppermute | solution.py:25
  182.6 6.9 %collective-permute-start.25 = (bf16[48,1536]{1,0:T(8,128)(2,1)S(1)}, bf16[48,1536]{1,0:T(8,128)(2,1)S(1)}, u32[]{:S(2)}, u32[]{:S(2)}) collective-permute-start(bf16[48,1536]{1,0:T(8,128)(2,1)S(1)} %bitcast.28), channel_id=1, source_target_pairs={{0,16},{16,0},{1,17},{17,1},{2,18},{18,2},{3,19},{19,3},{4,20},{20... | collective-permute-start | bytes 442376 | tf_op jit(solution)/shard_map/ppermute | solution.py:25
  183.4 9.5 %collective-permute-start.26 = (bf16[48,2304]{1,0:T(8,128)(2,1)S(1)}, bf16[48,2304]{1,0:T(8,128)(2,1)S(1)}, u32[]{:S(2)}, u32[]{:S(2)}) collective-permute-start(bf16[48,2304]{1,0:T(8,128)(2,1)S(1)} %bitcast.26), channel_id=1, source_target_pairs={{0,16},{16,0},{1,17},{17,1},{2,18},{18,2},{3,19},{19,3},{4,20},{20... | collective-permute-start | bytes 663560 | tf_op jit(solution)/shard_map/ppermute | solution.py:25
  184.8 8.2 %collective-permute-start.28 = (bf16[48,896]{1,0:T(8,128)(2,1)S(1)}, bf16[48,896]{1,0:T(8,128)(2,1)S(1)}, u32[]{:S(2)}, u32[]{:S(2)}) collective-permute-start(bf16[48,896]{1,0:T(8,128)(2,1)S(1)} %bitcast.30), channel_id=1, source_target_pairs={{0,16},{16,0},{1,17},{17,1},{2,18},{18,2},{3,19},{19,3},{4,20},{20... | collective-permute-start | bytes 258056 | tf_op jit(solution)/shard_map/ppermute | solution.py:25

commit v5 on v4

--- a/solution.py
+++ b/solution.py
@@ -186,7 +186,7 @@
 
 
 def parts_of(blocks):
-    early = 2 * blocks // 3
+    early = blocks // 2
     return (0, early), (early, blocks - early)
 
 

time: 195 us -> 193 us (0.990)
  waiting for transfers between devices: 43.9 us -> 40.1 us
    ppermute x29, waiting for transfers between devices: 43.9 us -> 40.1 us  [flipped(): return lax.ppermute(value, axis, pairs)]
  transfers between devices with their start and end apart: 29 -> 29, of which waited for: 11 -> 8; matrix products, arithmetic and copies ran while one was open for 3% -> 3% of each run, Pallas kernels for 43% -> 44%
where the time goes in v5:
time: 193 us; the launch traced here: 192 us
  Pallas kernels  115 us (60%)
  waiting for transfers between devices  40.1 us (21%)
  starting transfers between devices  28.9 us (15%)
  other arithmetic  5.91 us (3%)
    pallas_call x14, Pallas kernels, call(): pl.pallas_call(wrapped, grid_spec=pltpu.PrefetchScalarGridSpec(num_scalar...  115 us
    ppermute x29, waiting for transfers between devices, flipped(): return lax.ppermute(value, axis, pairs)  40.1 us
    ppermute x29, starting transfers between devices, flipped(): return lax.ppermute(value, axis, pairs)  28.9 us
    convert_element_type x17, other arithmetic, step(): total = total.astype(BF16)  4.25 us
  transfers between devices with their start and end apart: 29, of which 8 were waited for; matrix products, arithmetic and copies ran while one was open for 3% of the time, Pallas kernels for 44%

profile of v5, /device:TPU:0, one launch (start us, length us, event | category | flops | bytes accessed | tf_op | source)
XLA Modules:
  0.0 192.5 jit_solution(10179818510209477734)
XLA Ops:
  0.6 2.5 %gather_sent.3 = (bf16[4,64,768]{2,1,0:T(8,128)(2,1)}, f32[8,128]{1,0:T(8,128)}) custom-call(s32[16]{0:T(128)} %bitcast.49, bf16[16,64,768]{2,1,0:T(8,128)(2,1)} %bitcast.35), custom_call_target="tpu_custom_call" | custom-call | flops 10000000 | bytes 1048576 | tf_op jit(solution)/shard_map/gather_sent/pallas_call | solution.py:72
  3.1 3.0 %collective-permute-start = (bf16[4,64,768]{2,1,0:T(8,128)(2,1)}, bf16[4,64,768]{2,1,0:T(8,128)(2,1)S(1)}, u32[]{:S(2)}, u32[]{:S(2)}) collective-permute-start(bf16[4,64,768]{2,1,0:T(8,128)(2,1)} %get-tuple-element.114), channel_id=1, source_target_pairs={{0,16},{16,0},{1,17},{17,1},{2,18},{18,2},{3,19},{19,3},{4,20},{20... | collective-permute-start | bytes 1179656 | tf_op jit(solution)/shard_map/ppermute | solution.py:25
  6.2 2.6 %gather_sent.4 = (bf16[4,64,768]{2,1,0:T(8,128)(2,1)}, f32[8,128]{1,0:T(8,128)}) custom-call(s32[16]{0:T(128)} %bitcast.50, bf16[16,64,768]{2,1,0:T(8,128)(2,1)} %bitcast.36, f32[8,128]{1,0:T(8,128)} %get-tuple-element.115.refs_1_), custom_call_target="tpu_custom_call" | custom-call | flops 10000000 | bytes 1048576 | tf_op jit(solution)/shard_map/gather_sent/pallas_call | solution.py:72
  8.9 2.8 %gather_sent.5 = (bf16[8,64,768]{2,1,0:T(8,128)(2,1)}, f32[8,128]{1,0:T(8,128)}) custom-call(s32[16]{0:T(128)} %bitcast.51, bf16[16,64,768]{2,1,0:T(8,128)(2,1)} %bitcast.32, f32[8,128]{1,0:T(8,128)} %get-tuple-element.116.refs_1_), custom_call_target="tpu_custom_call" | custom-call | flops 10000000 | bytes 1048576 | tf_op jit(solution)/shard_map/gather_sent/pallas_call | solution.py:72
  11.7 4.6 %collective-permute-done.refs_2_ = bf16[4,64,768]{2,1,0:T(8,128)(2,1)S(1)} collective-permute-done((bf16[4,64,768]{2,1,0:T(8,128)(2,1)}, bf16[4,64,768]{2,1,0:T(8,128)(2,1)S(1)}, u32[]{:S(2)}, u32[]{:S(2)}) %collective-permute-start) | collective-permute-done | bytes 393248 | tf_op jit(solution)/shard_map/ppermute | solution.py:25
  16.6 2.1 %collective-permute-start.2 = (bf16[8,64,768]{2,1,0:T(8,128)(2,1)}, bf16[8,64,768]{2,1,0:T(8,128)(2,1)S(1)}, u32[]{:S(2)}, u32[]{:S(2)}) collective-permute-start(bf16[8,64,768]{2,1,0:T(8,128)(2,1)} %get-tuple-element.127), channel_id=1, source_target_pairs={{0,16},{16,0},{1,17},{17,1},{2,18},{18,2},{3,19},{19,3},{4,20},{20... | collective-permute-start | bytes 2359304 | tf_op jit(solution)/shard_map/ppermute | solution.py:25
  18.6 0.6 gather_fusion
  19.3 5.7 %fetch.1 = (bf16[768,2304]{1,0:T(8,128)(2,1)S(1)}, bf16[768,768]{1,0:T(8,128)(2,1)S(1)}, bf16[768,3072]{1,0:T(8,128)(2,1)S(1)}, bf16[3072,768]{1,0:T(8,128)(2,1)S(1)}, f32[8,128]{1,0:T(8,128)}) custom-call(s32[20]{0:T(128)S(1)} %concatenate.6.scalars_ref, bf16[768,2304]{1,0:T(8,128)(2,1)} %refs_0_.1, bf16[768,768]{1,0:T(8,128)(2,1)} %refs_1_.1, ...), custom_call_target="tpu_custom_call" | custom-call | flops 10000000 | bytes 1048576 | tf_op jit(solution)/shard_map/fetch/pallas_call | solution.py:72
  25.0 0.7 pad_add_fusion
  25.7 0.7 copy-done.11
  26.4 14.8 %attention_forward.1 = (bf16[1024,768]{1,0:T(8,128)(2,1)S(1)}, bf16[1024,2304]{1,0:T(8,128)(2,1)}, bf16[8,6,256,128]{3,2,1,0:T(8,128)(2,1)}, bf16[1024,768]{1,0:...) custom-call(s32[20]{0:T(128)S(1)} %concatenate.6.scalars_ref, ...), custom_call_target="tpu_custom_call" | custom-call | flops 40000000000 | bytes 1048576 | tf_op jit(solution)/shard_map/attention_forward/pallas_call | solution.py:72
  41.3 25.3 %feed_forward.1 = (bf16[1024,3072]{1,0:T(8,128)(2,1)S(1)}, bf16[1024,768]{1,0:T(8,128)(2,1)S(1)}, bf16[8,64,768]{2,1,0:T(8,128)(2,1)}, bf16[8,64,768]{2,1,0:T(8,...) custom-call(s32[20]{0:T(128)S(1)} %concatenate.6.scalars_ref, ...), custom_call_target="tpu_custom_call" | custom-call | flops 4000000000 | bytes 1048576 | tf_op jit(solution)/shard_map/feed_forward/pallas_call | solution.py:72
  67.1 2.5 %collective-permute-done.4 = bf16[1,4,192,768]{3,2,1,0:T(8,128)(2,1)S(1)} collective-permute-done((bf16[1,4,192,768]{3,2,1,0:T(8,128)(2,1)}, bf16[1,4,192,768]{3,2,1,0:T(8,128)(2,1)S(1)}, u32[]{:S(2)}, u32[]{:S(2)}) %collective-permute-start.4) | collective-permute-done | bytes 1179680 | tf_op jit(solution)/shard_map/ppermute | solution.py:25
  69.6 1.7 fusion.refs_8_
  71.3 1.6 collective-permute-start.5
  72.9 1.2 collective-permute-start.3
  74.1 21.7 %feed_backward.1 = (bf16[1024,768]{1,0:T(8,128)(2,1)S(1)}, f32[8,768]{1,0:T(8,128)}, f32[8,3072]{1,0:T(8,128)}, bf16[8,48,3072]{2,1,0:T(8,128)(2,1)}, bf16[8,48,3072]{2,1,0:T(8,128)(2,1)}, /*index=5*/f32[8,128]{1,0:T(8,128)}) custom-call(s32[20]{0:T(128)S(1)} %concatenate.6.scalars_ref, bf16[1024,768]{1,0:T(8,128)(2,1)S(1)} %get-tuple-element.138.refs_0_, ...), custom_call_target="tpu_custom_call" | custom-call | flops 4000000000 | bytes 1048576 | tf_op jit(solution)/shard_map/feed_backward/pallas_call | solution.py:72
  95.8 3.6 %collective-permute-done.5 = bf16[4,192,768]{2,1,0:T(8,128)(2,1)S(1)} collective-permute-done((bf16[4,192,768]{2,1,0:T(8,128)(2,1)S(1)}, bf16[4,192,768]{2,1,0:T(8,128)(2,1)S(1)}, u32[]{:S(2)}, u32[]{:S(2)}) %collective-permute-start.5) | collective-permute-done | bytes 1179680 | tf_op jit(solution)/shard_map/ppermute | solution.py:25
  99.6 1.6 collective-permute-start.7
  101.3 0.5 pause.2.refs_7_
  102.3 1.3 collective-permute-start.11
  103.5 12.7 %attention_backward.2 = (bf16[1024,1152]{1,0:T(8,128)(2,1)S(1)}, f32[8,384]{1,0:T(8,128)}, bf16[4,48,1920]{2,1,0:T(8,128)(2,1)}, bf16[4,48,1920]{2,1,0:T(8,128)(...) custom-call(s32[20]{0:T(128)S(1)} %concatenate.6.scalars_ref, bf16[1024,768]{1,0:T(8,128)(2,1)S(1)} %get-tuple-element.148.refs_0_, ...), custom_call_target="tpu_custom_call" | custom-call | flops 4000000000 | bytes 1048576 | tf_op jit(solution)/shard_map/attention_backward/pallas_call | solution.py:72
  116.4 2.6 %collective-permute-start.16 = (bf16[1,192,768]{2,1,0:T(8,128)(2,1)S(1)}, bf16[1,192,768]{2,1,0:T(8,128)(2,1)S(1)}, u32[]{:S(2)}, u32[]{:S(2)}) collective-permute-start(bf16[1,192,768]{2,1,0:T(8,128)(2,1)S(1)} %add_convert_fusion.8.refs_2_), channel_id=1, source_target_pairs={{0,8},{1,9},{2,10},{3,11},{4,12},{5,13},{6,14},{7,15},{8,0},{9,1},... | collective-permute-start | bytes 884744 | tf_op jit(solution)/shard_map/ppermute | solution.py:25
  119.0 0.5 collective-permute-start.15
  119.5 3.7 %scatter_home.2 = (bf16[16,64,768]{2,1,0:T(8,128)(2,1)}, f32[8,128]{1,0:T(8,128)}) custom-call(s32[20]{0:T(128)S(1)} %concatenate.6.scalars_ref, bf16[8,64,768]{2,1,0:T(8,128)(2,1)} %get-tuple-element.131.refs_0_, bf16[8,64,768]{2,1,0:T(8,128)(2,1)S(1)} %collective-permute-done.3.refs_1_, bf16[1,192,768]{2,1,0:T(8,128)(2,1)S(1)} %add_convert_fusion.8.refs_2_, ...), custom_call_target="tpu_custom_call" | custom-call | flops 20000000000 | bytes 1048576 | tf_op jit(solution)/shard_map/scatter_home/pallas_call | solution.py:72
  123.5 1.6 collective-permute-start.14
  125.0 16.4 %attention_backward.3 = (bf16[8,64,768]{2,1,0:T(8,128)(2,1)}, bf16[8,64,768]{2,1,0:T(8,128)(2,1)}, f32[8,384]{1,0:T(8,128)}, bf16[4,48,1280]{2,1,0:T(8,128)(2,1)...) custom-call(s32[20]{0:T(128)S(1)} %concatenate.6.scalars_ref, ...), custom_call_target="tpu_custom_call" | custom-call | flops 4000000000 | bytes 1048576 | tf_op jit(solution)/shard_map/attention_backward/pallas_call | solution.py:72
  142.6 0.8 collective-permute-start.10
  143.6 0.6 collective-permute-start.12
  144.2 1.2 collective-permute-start.18
  145.6 1.1 collective-permute-start.21
  146.8 11.8 %collective-permute-done.12 = bf16[4,48,1536]{2,1,0:T(8,128)(2,1)S(1)} collective-permute-done((bf16[4,48,1536]{2,1,0:T(8,128)(2,1)S(1)}, bf16[4,48,1536]{2,1,0:T(8,128)(2,1)S(1)}, u32[]{:S(2)}, u32[]{:S(2)}) %collective-permute-start.12) | collective-permute-done | bytes 589856 | tf_op jit(solution)/shard_map/ppermute | solution.py:25
  158.5 0.5 collective-permute-start.19
  159.2 0.5 pause.3.refs_3_
  159.8 1.1 collective-permute-start.17
  161.0 1.0 collective-permute-start.24
  161.9 8.4 %collective-permute-done.19 = bf16[4,48,1280]{2,1,0:T(8,128)(2,1)S(1)} collective-permute-done((bf16[4,48,1280]{2,1,0:T(8,128)(2,1)S(1)}, bf16[4,48,1280]{2,1,0:T(8,128)(2,1)S(1)}, u32[]{:S(2)}, u32[]{:S(2)}) %collective-permute-start.19) | collective-permute-done | bytes 491552 | tf_op jit(solution)/shard_map/ppermute | solution.py:25
  170.5 1.1 collective-permute-start.23
  171.7 1.0 collective-permute-start.22
  172.7 3.7 %scatter_home.3 = (bf16[16,64,768]{2,1,0:T(8,128)(2,1)}, f32[8,128]{1,0:T(8,128)}) custom-call(s32[20]{0:T(128)S(1)} %concatenate.6.scalars_ref, bf16[8,64,768]{2,1,0:T(8,128)(2,1)} %get-tuple-element.172.refs_0_, bf16[8,64,768]{2,1,0:T(8,128)(2,1)S(1)} %collective-permute-done.10.refs_1_, bf16[1,48,1536]{2,1,0:T(8,128)(2,1)S(1)} %add_convert_fusion.13.refs_2_, ...), custom_call_target="tpu_custom_call" | custom-call | flops 20000000000 | bytes 1048576 | tf_op jit(solution)/shard_map/scatter_home/pallas_call | solution.py:72
  176.5 1.3 collective-permute-start.26
  177.8 1.7 collective-permute-done.23
  180.0 1.1 collective-permute-start.25
  181.1 4.7 %collective-permute-done.27 = bf16[1,48,1280]{2,1,0:T(8,128)(2,1)S(1)} collective-permute-done((bf16[1,48,1280]{2,1,0:T(8,128)(2,1)S(1)}, bf16[1,48,1280]{2,1,0:T(8,128)(2,1)S(1)}, u32[]{:S(2)}, u32[]{:S(2)}) %collective-permute-start.27) | collective-permute-done | bytes 122912 | tf_op jit(solution)/shard_map/ppermute | solution.py:25
  185.9 1.3 collective-permute-start.28
  187.1 0.9 convert_add_fusion.1
  188.0 2.8 %collective-permute-done.28.refs_5_ = bf16[48,1280]{1,0:T(8,128)(2,1)S(1)} collective-permute-done((bf16[48,1280]{1,0:T(8,128)(2,1)S(1)}, bf16[48,1280]{1,0:T(8,128)(2,1)S(1)}, u32[]{:S(2)}, u32[]{:S(2)}) %collective-permute-start.28) | collective-permute-done | bytes 122912 | tf_op jit(solution)/shard_map/ppermute | solution.py:25
  190.8 1.6 finish.1
  (75 shorter events, 4.8 us)
Async XLA Ops:
  3.1 13.2 %collective-permute-start = (bf16[4,64,768]{2,1,0:T(8,128)(2,1)}, bf16[4,64,768]{2,1,0:T(8,128)(2,1)S(1)}, u32[]{:S(2)}, u32[]{:S(2)}) collective-permute-start(bf16[4,64,768]{2,1,0:T(8,128)(2,1)} %get-tuple-element.114), channel_id=1, source_target_pairs={{0,16},{16,0},{1,17},{17,1},{2,18},{18,2},{3,19},{19,3},{4,20},{20... | collective-permute-start | bytes 1179656 | tf_op jit(solution)/shard_map/ppermute | solution.py:25
  6.1 10.2 %copy-start.5 = (s32[2,1024]{1,0:T(2,128)S(1)}, s32[2,1024]{1,0:T(2,128)}, u32[]{:S(2)}) copy-start(s32[2,1024]{1,0:T(2,128)} %param.14) | copy-start | bytes 24580
  6.1 10.2 %copy-start.4 = (s32[1,16]{1,0:T(1,128)S(1)}, s32[1,16]{1,0:T(1,128)}, u32[]{:S(2)}) copy-start(s32[1,16]{1,0:T(1,128)} %param.15) | copy-start | bytes 196
  8.8 16.9 %collective-permute-start.1 = (bf16[4,64,768]{2,1,0:T(8,128)(2,1)}, bf16[4,64,768]{2,1,0:T(8,128)(2,1)S(1)}, u32[]{:S(2)}, u32[]{:S(2)}) collective-permute-start(bf16[4,64,768]{2,1,0:T(8,128)(2,1)} %get-tuple-element.120), channel_id=1, source_target_pairs={{0,16},{16,0},{1,17},{17,1},{2,18},{18,2},{3,19},{19,3},{4,20},{20... | collective-permute-start | bytes 1179656 | tf_op jit(solution)/shard_map/ppermute | solution.py:25
  16.3 8.7 %copy-start.10 = (bf16[4,64,768]{2,1,0:T(8,128)(2,1)}, bf16[4,64,768]{2,1,0:T(8,128)(2,1)S(1)}, u32[]{:S(2)}) copy-start(bf16[4,64,768]{2,1,0:T(8,128)(2,1)S(1)} %collective-permute-done.refs_2_) | copy-start | bytes 1179652
  16.6 24.7 %collective-permute-start.2 = (bf16[8,64,768]{2,1,0:T(8,128)(2,1)}, bf16[8,64,768]{2,1,0:T(8,128)(2,1)S(1)}, u32[]{:S(2)}, u32[]{:S(2)}) collective-permute-start(bf16[8,64,768]{2,1,0:T(8,128)(2,1)} %get-tuple-element.127), channel_id=1, source_target_pairs={{0,16},{16,0},{1,17},{17,1},{2,18},{18,2},{3,19},{19,3},{4,20},{20... | collective-permute-start | bytes 2359304 | tf_op jit(solution)/shard_map/ppermute | solution.py:25
  25.7 0.7 copy-start.11
  66.6 3.1 %collective-permute-start.4 = (bf16[1,4,192,768]{3,2,1,0:T(8,128)(2,1)}, bf16[1,4,192,768]{3,2,1,0:T(8,128)(2,1)S(1)}, u32[]{:S(2)}, u32[]{:S(2)}) collective-permute-start(bf16[1,4,192,768]{3,2,1,0:T(8,128)(2,1)} %get-tuple-element.134), channel_id=1, source_target_pairs={{0,1},{1,0},{2,3},{3,2},{4,5},{5,4},{6,7},{7,6},{8,9},{9,8},{10,11... | collective-permute-start | bytes 3538952 | tf_op jit(solution)/shard_map/ppermute | solution.py:25
  66.6 29.2 %collective-permute-start.6 = (bf16[1,4,192,768]{3,2,1,0:T(8,128)(2,1)}, bf16[1,4,192,768]{3,2,1,0:T(8,128)(2,1)S(1)}, u32[]{:S(2)}, u32[]{:S(2)}) collective-permute-start(bf16[1,4,192,768]{3,2,1,0:T(8,128)(2,1)} %get-tuple-element.137), channel_id=1, source_target_pairs={{0,1},{1,0},{2,3},{3,2},{4,5},{5,4},{6,7},{7,6},{8,9},{9,8},{10,11... | collective-permute-start | bytes 3538952 | tf_op jit(solution)/shard_map/ppermute | solution.py:25
  69.6 3.2 %copy-start.7 = (bf16[8,64,768]{2,1,0:T(8,128)(2,1)S(1)}, bf16[8,64,768]{2,1,0:T(8,128)(2,1)}, u32[]{:S(2)}) copy-start(bf16[8,64,768]{2,1,0:T(8,128)(2,1)} %get-tuple-element.132) | copy-start | bytes 2359300
  71.3 28.1 %collective-permute-start.5 = (bf16[4,192,768]{2,1,0:T(8,128)(2,1)S(1)}, bf16[4,192,768]{2,1,0:T(8,128)(2,1)S(1)}, u32[]{:S(2)}, u32[]{:S(2)}) collective-permute-start(bf16[4,192,768]{2,1,0:T(8,128)(2,1)S(1)} %fusion.refs_8_), channel_id=1, source_target_pairs={{0,2},{1,3},{2,0},{3,1},{4,6},{5,7},{6,4},{7,5},{8,10},{9,11},{10,... | collective-permute-start | bytes 3538952 | tf_op jit(solution)/shard_map/ppermute | solution.py:25
  72.9 28.4 %collective-permute-start.3 = (bf16[8,64,768]{2,1,0:T(8,128)(2,1)S(1)}, bf16[8,64,768]{2,1,0:T(8,128)(2,1)S(1)}, u32[]{:S(2)}, u32[]{:S(2)}) collective-permute-start(bf16[8,64,768]{2,1,0:T(8,128)(2,1)S(1)} %copy-done.7), channel_id=1, source_target_pairs={{0,16},{16,0},{1,17},{17,1},{2,18},{18,2},{3,19},{19,3},{4,20},{20... | collective-permute-start | bytes 2359304 | tf_op jit(solution)/shard_map/ppermute | solution.py:25
  74.1 25.3 %copy-start.1 = (bf16[2,4,192,768]{3,2,1,0:T(8,128)(2,1)S(1)}, bf16[2,4,192,768]{3,2,1,0:T(8,128)(2,1)}, u32[]{:S(2)}) copy-start(bf16[2,4,192,768]{3,2,1,0:T(8,128)(2,1)} %get-tuple-element.133) | copy-start | bytes 7077892
  95.7 6.1 %collective-permute-start.8 = (bf16[8,48,3072]{2,1,0:T(8,128)(2,1)}, bf16[8,48,3072]{2,1,0:T(8,128)(2,1)S(1)}, u32[]{:S(2)}, u32[]{:S(2)}) collective-permute-start(bf16[8,48,3072]{2,1,0:T(8,128)(2,1)} %get-tuple-element.154), channel_id=1, source_target_pairs={{0,1},{1,0},{2,3},{3,2},{4,5},{5,4},{6,7},{7,6},{8,9},{9,8},{10,11... | collective-permute-start | bytes 7077896 | tf_op jit(solution)/shard_map/ppermute | solution.py:25
  99.6 2.2 %copy-start = (bf16[8,48,3072]{2,1,0:T(8,128)(2,1)S(1)}, bf16[8,48,3072]{2,1,0:T(8,128)(2,1)}, u32[]{:S(2)}) copy-start(bf16[8,48,3072]{2,1,0:T(8,128)(2,1)} %get-tuple-element.153) | copy-start | bytes 7077892
  99.6 16.6 %collective-permute-start.7 = (bf16[2,192,768]{2,1,0:T(8,128)(2,1)S(1)}, bf16[2,192,768]{2,1,0:T(8,128)(2,1)S(1)}, u32[]{:S(2)}, u32[]{:S(2)}) collective-permute-start(bf16[2,192,768]{2,1,0:T(8,128)(2,1)S(1)} %add_convert_fusion.3), channel_id=1, source_target_pairs={{0,4},{1,5},{2,6},{3,7},{4,0},{5,1},{6,2},{7,3},{8,12},{9,13},{10,... | collective-permute-start | bytes 1769480 | tf_op jit(solution)/shard_map/ppermute | solution.py:25
  102.3 39.3 %collective-permute-start.11 = (bf16[8,48,1536]{2,1,0:T(8,128)(2,1)S(1)}, bf16[8,48,1536]{2,1,0:T(8,128)(2,1)S(1)}, u32[]{:S(2)}, u32[]{:S(2)}) collective-permute-start(bf16[8,48,1536]{2,1,0:T(8,128)(2,1)S(1)} %add_convert_fusion.refs_6_), channel_id=1, source_target_pairs={{0,16},{16,0},{1,17},{17,1},{2,18},{18,2},{3,19},{19,3},{4,20},{20... | collective-permute-start | bytes 3538952 | tf_op jit(solution)/shard_map/ppermute | solution.py:25
  116.2 2.8 %copy-start.9 = (bf16[4,48,1920]{2,1,0:T(8,128)(2,1)S(1)}, bf16[4,48,1920]{2,1,0:T(8,128)(2,1)}, u32[]{:S(2)}) copy-start(bf16[4,48,1920]{2,1,0:T(8,128)(2,1)} %get-tuple-element.168) | copy-start | bytes 2211844
  116.2 2.8 %copy-start.8 = (bf16[4,48,1920]{2,1,0:T(8,128)(2,1)S(1)}, bf16[4,48,1920]{2,1,0:T(8,128)(2,1)}, u32[]{:S(2)}) copy-start(bf16[4,48,1920]{2,1,0:T(8,128)(2,1)} %get-tuple-element.177) | copy-start | bytes 2211844
  116.4 25.9 %collective-permute-start.16 = (bf16[1,192,768]{2,1,0:T(8,128)(2,1)S(1)}, bf16[1,192,768]{2,1,0:T(8,128)(2,1)S(1)}, u32[]{:S(2)}, u32[]{:S(2)}) collective-permute-start(bf16[1,192,768]{2,1,0:T(8,128)(2,1)S(1)} %add_convert_fusion.8.refs_2_), channel_id=1, source_target_pairs={{0,8},{1,9},{2,10},{3,11},{4,12},{5,13},{6,14},{7,15},{8,0},{9,1},... | collective-permute-start | bytes 884744 | tf_op jit(solution)/shard_map/ppermute | solution.py:25
  119.0 4.2 %collective-permute-start.9 = (bf16[4,48,1920]{2,1,0:T(8,128)(2,1)S(1)}, bf16[4,48,1920]{2,1,0:T(8,128)(2,1)S(1)}, u32[]{:S(2)}, u32[]{:S(2)}) collective-permute-start(bf16[4,48,1920]{2,1,0:T(8,128)(2,1)S(1)} %copy-done.9), channel_id=1, source_target_pairs={{0,1},{1,0},{2,3},{3,2},{4,5},{5,4},{6,7},{7,6},{8,9},{9,8},{10,11... | collective-permute-start | bytes 2211848 | tf_op jit(solution)/shard_map/ppermute | solution.py:25
  119.0 24.6 %collective-permute-start.15 = (bf16[4,48,1920]{2,1,0:T(8,128)(2,1)S(1)}, bf16[4,48,1920]{2,1,0:T(8,128)(2,1)S(1)}, u32[]{:S(2)}, u32[]{:S(2)}) collective-permute-start(bf16[4,48,1920]{2,1,0:T(8,128)(2,1)S(1)} %copy-done.8), channel_id=1, source_target_pairs={{0,1},{1,0},{2,3},{3,2},{4,5},{5,4},{6,7},{7,6},{8,9},{9,8},{10,11... | collective-permute-start | bytes 2211848 | tf_op jit(solution)/shard_map/ppermute | solution.py:25
  119.5 3.7 %copy-start.2 = (bf16[8,48,1920]{2,1,0:T(8,128)(2,1)S(1)}, bf16[8,48,1920]{2,1,0:T(8,128)(2,1)}, u32[]{:S(2)}) copy-start(bf16[8,48,1920]{2,1,0:T(8,128)(2,1)} %get-tuple-element.167) | copy-start | bytes 4423684
  123.5 20.7 %collective-permute-start.14 = (bf16[4,48,1920]{2,1,0:T(8,128)(2,1)S(1)}, bf16[4,48,1920]{2,1,0:T(8,128)(2,1)S(1)}, u32[]{:S(2)}, u32[]{:S(2)}) collective-permute-start(bf16[4,48,1920]{2,1,0:T(8,128)(2,1)S(1)} %add_convert_fusion.1.refs_11_), channel_id=1, source_target_pairs={{0,2},{1,3},{2,0},{3,1},{4,6},{5,7},{6,4},{7,5},{8,10},{9,11},{10,... | collective-permute-start | bytes 2211848 | tf_op jit(solution)/shard_map/ppermute | solution.py:25
  141.4 1.1 copy-start.6
  141.5 4.1 %collective-permute-start.13 = (bf16[4,48,1280]{2,1,0:T(8,128)(2,1)}, bf16[4,48,1280]{2,1,0:T(8,128)(2,1)S(1)}, u32[]{:S(2)}, u32[]{:S(2)}) collective-permute-start(bf16[4,48,1280]{2,1,0:T(8,128)(2,1)} %get-tuple-element.176), channel_id=1, source_target_pairs={{0,1},{1,0},{2,3},{3,2},{4,5},{5,4},{6,7},{7,6},{8,9},{9,8},{10,11... | collective-permute-start | bytes 1474568 | tf_op jit(solution)/shard_map/ppermute | solution.py:25
  141.5 19.4 %collective-permute-start.20 = (bf16[4,48,1280]{2,1,0:T(8,128)(2,1)}, bf16[4,48,1280]{2,1,0:T(8,128)(2,1)S(1)}, u32[]{:S(2)}, u32[]{:S(2)}) collective-permute-start(bf16[4,48,1280]{2,1,0:T(8,128)(2,1)} %get-tuple-element.189), channel_id=1, source_target_pairs={{0,1},{1,0},{2,3},{3,2},{4,5},{5,4},{6,7},{7,6},{8,9},{9,8},{10,11... | collective-permute-start | bytes 1474568 | tf_op jit(solution)/shard_map/ppermute | solution.py:25
  142.6 4.1 %copy-start.3 = (bf16[8,48,1280]{2,1,0:T(8,128)(2,1)S(1)}, bf16[8,48,1280]{2,1,0:T(8,128)(2,1)}, u32[]{:S(2)}) copy-start(bf16[8,48,1280]{2,1,0:T(8,128)(2,1)} %get-tuple-element.186) | copy-start | bytes 2949124
  142.6 30.1 %collective-permute-start.10 = (bf16[8,64,768]{2,1,0:T(8,128)(2,1)S(1)}, bf16[8,64,768]{2,1,0:T(8,128)(2,1)S(1)}, u32[]{:S(2)}, u32[]{:S(2)}) collective-permute-start(bf16[8,64,768]{2,1,0:T(8,128)(2,1)S(1)} %copy-done.6), channel_id=1, source_target_pairs={{0,16},{16,0},{1,17},{17,1},{2,18},{18,2},{3,19},{19,3},{4,20},{20... | collective-permute-start | bytes 2359304 | tf_op jit(solution)/shard_map/ppermute | solution.py:25
  143.6 14.9 %collective-permute-start.12 = (bf16[4,48,1536]{2,1,0:T(8,128)(2,1)S(1)}, bf16[4,48,1536]{2,1,0:T(8,128)(2,1)S(1)}, u32[]{:S(2)}, u32[]{:S(2)}) collective-permute-start(bf16[4,48,1536]{2,1,0:T(8,128)(2,1)S(1)} %add_convert_fusion.2), channel_id=1, source_target_pairs={{0,2},{1,3},{2,0},{3,1},{4,6},{5,7},{6,4},{7,5},{8,10},{9,11},{10,... | collective-permute-start | bytes 1769480 | tf_op jit(solution)/shard_map/ppermute | solution.py:25
  144.2 27.4 %collective-permute-start.18 = (bf16[192,768]{1,0:T(8,128)(2,1)S(1)}, bf16[192,768]{1,0:T(8,128)(2,1)S(1)}, u32[]{:S(2)}, u32[]{:S(2)}) collective-permute-start(bf16[192,768]{1,0:T(8,128)(2,1)S(1)} %bitcast.43), channel_id=1, source_target_pairs={{0,16},{16,0},{1,17},{17,1},{2,18},{18,2},{3,19},{19,3},{4,20},{20... | collective-permute-start | bytes 884744 | tf_op jit(solution)/shard_map/ppermute | solution.py:25
  145.6 14.2 %collective-permute-start.21 = (bf16[2,48,1920]{2,1,0:T(8,128)(2,1)S(1)}, bf16[2,48,1920]{2,1,0:T(8,128)(2,1)S(1)}, u32[]{:S(2)}, u32[]{:S(2)}) collective-permute-start(bf16[2,48,1920]{2,1,0:T(8,128)(2,1)S(1)} %add_convert_fusion.5), channel_id=1, source_target_pairs={{0,4},{1,5},{2,6},{3,7},{4,0},{5,1},{6,2},{7,3},{8,12},{9,13},{10,... | collective-permute-start | bytes 1105928 | tf_op jit(solution)/shard_map/ppermute | solution.py:25
  158.5 11.8 %collective-permute-start.19 = (bf16[4,48,1280]{2,1,0:T(8,128)(2,1)S(1)}, bf16[4,48,1280]{2,1,0:T(8,128)(2,1)S(1)}, u32[]{:S(2)}, u32[]{:S(2)}) collective-permute-start(bf16[4,48,1280]{2,1,0:T(8,128)(2,1)S(1)} %add_convert_fusion.4), channel_id=1, source_target_pairs={{0,2},{1,3},{2,0},{3,1},{4,6},{5,7},{6,4},{7,5},{8,10},{9,11},{10,... | collective-permute-start | bytes 1474568 | tf_op jit(solution)/shard_map/ppermute | solution.py:25
  159.8 11.8 %collective-permute-start.17 = (bf16[2,48,1536]{2,1,0:T(8,128)(2,1)S(1)}, bf16[2,48,1536]{2,1,0:T(8,128)(2,1)S(1)}, u32[]{:S(2)}, u32[]{:S(2)}) collective-permute-start(bf16[2,48,1536]{2,1,0:T(8,128)(2,1)S(1)} %add_convert_fusion.6.refs_0_), channel_id=1, source_target_pairs={{0,4},{1,5},{2,6},{3,7},{4,0},{5,1},{6,2},{7,3},{8,12},{9,13},{10,... | collective-permute-start | bytes 884744 | tf_op jit(solution)/shard_map/ppermute | solution.py:25
  161.0 15.4 %collective-permute-start.24 = (bf16[1,48,1920]{2,1,0:T(8,128)(2,1)S(1)}, bf16[1,48,1920]{2,1,0:T(8,128)(2,1)S(1)}, u32[]{:S(2)}, u32[]{:S(2)}) collective-permute-start(bf16[1,48,1920]{2,1,0:T(8,128)(2,1)S(1)} %add_convert_fusion.11), channel_id=1, source_target_pairs={{0,8},{1,9},{2,10},{3,11},{4,12},{5,13},{6,14},{7,15},{8,0},{9,1},... | collective-permute-start | bytes 552968 | tf_op jit(solution)/shard_map/ppermute | solution.py:25
  170.5 9.1 %collective-permute-start.23 = (bf16[2,48,1280]{2,1,0:T(8,128)(2,1)S(1)}, bf16[2,48,1280]{2,1,0:T(8,128)(2,1)S(1)}, u32[]{:S(2)}, u32[]{:S(2)}) collective-permute-start(bf16[2,48,1280]{2,1,0:T(8,128)(2,1)S(1)} %add_convert_fusion.9), channel_id=1, source_target_pairs={{0,4},{1,5},{2,6},{3,7},{4,0},{5,1},{6,2},{7,3},{8,12},{9,13},{10,... | collective-permute-start | bytes 737288 | tf_op jit(solution)/shard_map/ppermute | solution.py:25
  171.7 8.3 %collective-permute-start.22 = (bf16[1,48,1536]{2,1,0:T(8,128)(2,1)S(1)}, bf16[1,48,1536]{2,1,0:T(8,128)(2,1)S(1)}, u32[]{:S(2)}, u32[]{:S(2)}) collective-permute-start(bf16[1,48,1536]{2,1,0:T(8,128)(2,1)S(1)} %add_convert_fusion.13.refs_2_), channel_id=1, source_target_pairs={{0,8},{1,9},{2,10},{3,11},{4,12},{5,13},{6,14},{7,15},{8,0},{9,1},... | collective-permute-start | bytes 442376 | tf_op jit(solution)/shard_map/ppermute | solution.py:25
  176.5 11.5 %collective-permute-start.26 = (bf16[48,1920]{1,0:T(8,128)(2,1)S(1)}, bf16[48,1920]{1,0:T(8,128)(2,1)S(1)}, u32[]{:S(2)}, u32[]{:S(2)}) collective-permute-start(bf16[48,1920]{1,0:T(8,128)(2,1)S(1)} %bitcast.26), channel_id=1, source_target_pairs={{0,16},{16,0},{1,17},{17,1},{2,18},{18,2},{3,19},{19,3},{4,20},{20... | collective-permute-start | bytes 552968 | tf_op jit(solution)/shard_map/ppermute | solution.py:25
  179.6 6.1 %collective-permute-start.27 = (bf16[1,48,1280]{2,1,0:T(8,128)(2,1)S(1)}, bf16[1,48,1280]{2,1,0:T(8,128)(2,1)S(1)}, u32[]{:S(2)}, u32[]{:S(2)}) collective-permute-start(bf16[1,48,1280]{2,1,0:T(8,128)(2,1)S(1)} %add_convert_fusion.15), channel_id=1, source_target_pairs={{0,8},{1,9},{2,10},{3,11},{4,12},{5,13},{6,14},{7,15},{8,0},{9,1},... | collective-permute-start | bytes 368648 | tf_op jit(solution)/shard_map/ppermute | solution.py:25
  180.0 8.0 %collective-permute-start.25 = (bf16[48,1536]{1,0:T(8,128)(2,1)S(1)}, bf16[48,1536]{1,0:T(8,128)(2,1)S(1)}, u32[]{:S(2)}, u32[]{:S(2)}) collective-permute-start(bf16[48,1536]{1,0:T(8,128)(2,1)S(1)} %bitcast.28), channel_id=1, source_target_pairs={{0,16},{16,0},{1,17},{17,1},{2,18},{18,2},{3,19},{19,3},{4,20},{20... | collective-permute-start | bytes 442376 | tf_op jit(solution)/shard_map/ppermute | solution.py:25
  185.9 4.9 %collective-permute-start.28 = (bf16[48,1280]{1,0:T(8,128)(2,1)S(1)}, bf16[48,1280]{1,0:T(8,128)(2,1)S(1)}, u32[]{:S(2)}, u32[]{:S(2)}) collective-permute-start(bf16[48,1280]{1,0:T(8,128)(2,1)S(1)} %bitcast.30), channel_id=1, source_target_pairs={{0,16},{16,0},{1,17},{17,1},{2,18},{18,2},{3,19},{19,3},{4,20},{20... | collective-permute-start | bytes 368648 | tf_op jit(solution)/shard_map/ppermute | solution.py:25

commit v6 on v5

--- a/solution.py
+++ b/solution.py
@@ -509,7 +509,7 @@
     )
 
 
-def feed_backward(scalars, branch, slope, normed, root, weights, shards, base, order):
+def feed_backward(scalars, branch, slope, normed, root, context, weights, shards, base, order):
     w_in, w_back, norm_gains, bias_rows = weights
     total, width = branch.shape
     inner_width = slope.shape[1]
@@ -525,11 +525,13 @@
         slope_ref,
         normed_ref,
         root_ref,
+        context_ref,
         w_in_ref,
         w_back_ref,
         gains_ref,
         biases_ref,
         low_attn_out,
+        outer_out,
         sums_out,
         inner_sum_out,
         send,
@@ -573,6 +575,7 @@
                 for j, term in enumerate((d_hidden * scaled, d_hidden, d_one)):
                     sums[j] = sums[j] + row_sum(term)
             sums_out[...] = jnp.concatenate(sums + [jnp.zeros((5, width), F32)], 0)
+            outer_out[...] = dot(context_ref[...], low_attn_out[...], 0, 0).astype(BF16)
     grads = pl.BlockSpec(
         (places, shard, chunk), lambda i, s: (0, 0, i ^ (s[base + 3] * (steps // 2)))
     )
@@ -580,18 +583,14 @@
     return call(
         kernel,
         scalars,
-        [branch, slope, normed, root, w_in, w_back, norm_gains, bias_rows],
+        [branch, slope, normed, root, context, w_in, w_back, norm_gains, bias_rows],
         [
-            RESIDENT,
-            RESIDENT,
-            RESIDENT,
-            RESIDENT,
-            RESIDENT,
-            RESIDENT,
+            *[RESIDENT] * 7,
             whole(norm_gains),
             whole(bias_rows),
         ],
         [
+            RESIDENT,
             RESIDENT,
             pl.BlockSpec((8, width), lambda i, s: (0, 0)),
             pl.BlockSpec((8, chunk), lambda i, s: (0, i)),
@@ -600,6 +599,7 @@
         ],
         [
             jax.ShapeDtypeStruct((total, width), BF16),
+            jax.ShapeDtypeStruct((width, width), BF16),
             jax.ShapeDtypeStruct((8, width), F32),
             jax.ShapeDtypeStruct((8, inner_width), F32),
             shape,
@@ -607,7 +607,7 @@
         ],
         (steps,),
         "feed_backward",
-        limit=21 * 2**20,
+        limit=20 * 2**20,
         scratch=[
             pltpu.VMEM((total, width), F32),
             pltpu.VMEM((total, width), BF16),
@@ -617,7 +617,7 @@
 
 
 def attention_backward(scalars, kept, weights, part, shards, base, order, earlier=(), sums=()):
-    low_attn, mixed, probs, joined, context = kept
+    low_attn, mixed, probs, joined, outer = kept
     w_out, w_qkv = weights
     total, width = low_attn.shape
     pairs, blocks, _, length = probs.shape
@@ -645,7 +645,7 @@
             w_qkv_ref, earlier_ref, one, two, inner, sums_ref = refs[:6]
             kept_out, far_out, sums_out, near, away, keep, held, grad = refs[6:]
         else:
-            context_ref, held, sums_out, near, away, keep, grad = refs
+            outer_ref, held, sums_out, near, away, keep, grad = refs
         step = pl.program_id(0)
 
         @pl.when(step == 0)
@@ -723,8 +723,7 @@
                 small.append(jnp.zeros((120 - count, width), F32))
                 grad[:, 3 * span_cols :] = jnp.concatenate(small, 0).T.astype(BF16)
             else:
-                outer = dot(context_ref[...], low_attn_ref[...], 0, 0)
-                grad[:, 3 * span_cols :] = outer.astype(BF16)
+                grad[:, 3 * span_cols :] = outer_ref[...]
             spread(grad, ((near, away), keep), scalars_ref, base, shard, order)
 
     two_slots = pl.BlockSpec((2, slot_rows, width), lambda i, s: (i, 0, 0))
@@ -750,7 +749,7 @@
         out_specs = [two_slots, two_slots] + out_specs
         out_shape = [jax.ShapeDtypeStruct((pairs, slot_rows, width), BF16)] * 2 + out_shape
     else:
-        operands.append(context)
+        operands.append(outer)
         in_specs.append(RESIDENT)
         out_specs = [RESIDENT] + out_specs
         out_shape = [jax.ShapeDtypeStruct((total, 3 * span_cols), BF16)] + out_shape
@@ -763,7 +762,7 @@
         out_shape,
         (steps,),
         "attention_backward",
-        limit=16 * 2**20,
+        limit=13 * 2**20,
         scratch=[pltpu.VMEM((total, 3 * span_cols), BF16)] * last
         + [pltpu.VMEM((width, columns), BF16)],
     )
@@ -955,8 +954,8 @@
     if aligned:
         back = Shards(*back, order=path)
         back.step()
-    low_attn, sums_one, inner_sum, *inner = feed_backward(
-        scalars, branch, slope, normed, root, back_weights, layout, groups, path
+    low_attn, outer, sums_one, inner_sum, *inner = feed_backward(
+        scalars, branch, slope, normed, root, context, back_weights, layout, groups, path
     )
     shard = width // shards
     count = inner_width // width
@@ -966,7 +965,7 @@
         pause(scalars)
         inner = Shards(*inner, order=("mod", 0, 1, 2))
         inner.step()
-    attn_kept = (low_attn, mixed, probs, joined, context)
+    attn_kept = (low_attn, mixed, probs, joined, outer)
     d_mixed, sums_qv, *qkv_a = attention_backward(
         scalars, attn_kept, attn_weights, 0, layout, groups, path
     )

time: 193 us -> 192 us (level)
  no operation moved by 1% of the time
where the time goes in v6:
time: 192 us
  Pallas kernels  115 us (60%)
  waiting for transfers between devices  38.7 us (20%)
  starting transfers between devices  29.6 us (15%)
  other arithmetic  5.82 us (3%)
    pallas_call x14, Pallas kernels, call(): pl.pallas_call(wrapped, grid_spec=pltpu.PrefetchScalarGridSpec(num_scalar...  115 us
    ppermute x29, waiting for transfers between devices, flipped(): return lax.ppermute(value, axis, pairs)  38.7 us
    ppermute x29, starting transfers between devices, flipped(): return lax.ppermute(value, axis, pairs)  29.6 us
    convert_element_type x17, other arithmetic, step(): total = total.astype(BF16)  4.18 us
  transfers between devices with their start and end apart: 29, of which 8 were waited for; matrix products, arithmetic and copies ran while one was open for 3% of the time, Pallas kernels for 44%

profile of v6, /device:TPU:0, one launch (start us, length us, event | category | flops | bytes accessed | tf_op | source)
XLA Modules:
  0.0 191.6 jit_solution(5095931403693587383)
XLA Ops:
  0.6 2.5 %gather_sent.3 = (bf16[4,64,768]{2,1,0:T(8,128)(2,1)}, f32[8,128]{1,0:T(8,128)}) custom-call(s32[16]{0:T(128)} %bitcast.49, bf16[16,64,768]{2,1,0:T(8,128)(2,1)} %bitcast.35), custom_call_target="tpu_custom_call" | custom-call | flops 10000000 | bytes 1048576 | tf_op jit(solution)/shard_map/gather_sent/pallas_call | solution.py:72
  3.1 3.0 %collective-permute-start = (bf16[4,64,768]{2,1,0:T(8,128)(2,1)}, bf16[4,64,768]{2,1,0:T(8,128)(2,1)S(1)}, u32[]{:S(2)}, u32[]{:S(2)}) collective-permute-start(bf16[4,64,768]{2,1,0:T(8,128)(2,1)} %get-tuple-element.115), channel_id=1, source_target_pairs={{0,16},{16,0},{1,17},{17,1},{2,18},{18,2},{3,19},{19,3},{4,20},{20... | collective-permute-start | bytes 1179656 | tf_op jit(solution)/shard_map/ppermute | solution.py:25
  6.2 2.6 %gather_sent.4 = (bf16[4,64,768]{2,1,0:T(8,128)(2,1)}, f32[8,128]{1,0:T(8,128)}) custom-call(s32[16]{0:T(128)} %bitcast.50, bf16[16,64,768]{2,1,0:T(8,128)(2,1)} %bitcast.36, f32[8,128]{1,0:T(8,128)} %get-tuple-element.116.refs_1_), custom_call_target="tpu_custom_call" | custom-call | flops 10000000 | bytes 1048576 | tf_op jit(solution)/shard_map/gather_sent/pallas_call | solution.py:72
  8.9 2.8 %gather_sent.5 = (bf16[8,64,768]{2,1,0:T(8,128)(2,1)}, f32[8,128]{1,0:T(8,128)}) custom-call(s32[16]{0:T(128)} %bitcast.51, bf16[16,64,768]{2,1,0:T(8,128)(2,1)} %bitcast.32, f32[8,128]{1,0:T(8,128)} %get-tuple-element.117.refs_1_), custom_call_target="tpu_custom_call" | custom-call | flops 10000000 | bytes 1048576 | tf_op jit(solution)/shard_map/gather_sent/pallas_call | solution.py:72
  11.7 4.6 %collective-permute-done.refs_2_ = bf16[4,64,768]{2,1,0:T(8,128)(2,1)S(1)} collective-permute-done((bf16[4,64,768]{2,1,0:T(8,128)(2,1)}, bf16[4,64,768]{2,1,0:T(8,128)(2,1)S(1)}, u32[]{:S(2)}, u32[]{:S(2)}) %collective-permute-start) | collective-permute-done | bytes 393248 | tf_op jit(solution)/shard_map/ppermute | solution.py:25
  16.6 2.1 %collective-permute-start.2 = (bf16[8,64,768]{2,1,0:T(8,128)(2,1)}, bf16[8,64,768]{2,1,0:T(8,128)(2,1)S(1)}, u32[]{:S(2)}, u32[]{:S(2)}) collective-permute-start(bf16[8,64,768]{2,1,0:T(8,128)(2,1)} %get-tuple-element.128), channel_id=1, source_target_pairs={{0,16},{16,0},{1,17},{17,1},{2,18},{18,2},{3,19},{19,3},{4,20},{20... | collective-permute-start | bytes 2359304 | tf_op jit(solution)/shard_map/ppermute | solution.py:25
  18.6 0.6 gather_fusion
  19.3 5.7 %fetch.1 = (bf16[768,2304]{1,0:T(8,128)(2,1)S(1)}, bf16[768,768]{1,0:T(8,128)(2,1)S(1)}, bf16[768,3072]{1,0:T(8,128)(2,1)S(1)}, bf16[3072,768]{1,0:T(8,128)(2,1)S(1)}, f32[8,128]{1,0:T(8,128)}) custom-call(s32[20]{0:T(128)S(1)} %concatenate.6.scalars_ref, bf16[768,2304]{1,0:T(8,128)(2,1)} %refs_0_.1, bf16[768,768]{1,0:T(8,128)(2,1)} %refs_1_.1, ...), custom_call_target="tpu_custom_call" | custom-call | flops 10000000 | bytes 1048576 | tf_op jit(solution)/shard_map/fetch/pallas_call | solution.py:72
  25.0 0.7 pad_add_fusion
  25.7 0.7 copy-done.15
  26.4 14.8 %attention_forward.1 = (bf16[1024,768]{1,0:T(8,128)(2,1)S(1)}, bf16[1024,2304]{1,0:T(8,128)(2,1)}, bf16[8,6,256,128]{3,2,1,0:T(8,128)(2,1)}, bf16[1024,768]{1,0:...) custom-call(s32[20]{0:T(128)S(1)} %concatenate.6.scalars_ref, ...), custom_call_target="tpu_custom_call" | custom-call | flops 40000000000 | bytes 1048576 | tf_op jit(solution)/shard_map/attention_forward/pallas_call | solution.py:72
  41.2 25.3 %feed_forward.1 = (bf16[1024,3072]{1,0:T(8,128)(2,1)S(1)}, bf16[1024,768]{1,0:T(8,128)(2,1)S(1)}, bf16[8,64,768]{2,1,0:T(8,128)(2,1)}, bf16[8,64,768]{2,1,0:T(8,...) custom-call(s32[20]{0:T(128)S(1)} %concatenate.6.scalars_ref, ...), custom_call_target="tpu_custom_call" | custom-call | flops 4000000000 | bytes 1048576 | tf_op jit(solution)/shard_map/feed_forward/pallas_call | solution.py:72
  67.0 2.5 %collective-permute-done.4 = bf16[1,4,192,768]{3,2,1,0:T(8,128)(2,1)S(1)} collective-permute-done((bf16[1,4,192,768]{3,2,1,0:T(8,128)(2,1)}, bf16[1,4,192,768]{3,2,1,0:T(8,128)(2,1)S(1)}, u32[]{:S(2)}, u32[]{:S(2)}) %collective-permute-start.4) | collective-permute-done | bytes 1179680 | tf_op jit(solution)/shard_map/ppermute | solution.py:25
  69.6 1.7 fusion.refs_9_
  71.2 1.6 collective-permute-start.5
  72.8 1.2 collective-permute-start.3
  74.0 23.0 %feed_backward.1 = (bf16[1024,768]{1,0:T(8,128)(2,1)S(1)}, bf16[768,768]{1,0:T(8,128)(2,1)S(1)}, f32[8,768]{1,0:T(8,128)}, f32[8,3072]{1,0:T(8,128)}, bf16[8,48,...) custom-call(s32[20]{0:T(128)S(1)} %concatenate.6.scalars_ref, ...), custom_call_target="tpu_custom_call" | custom-call | flops 4000000000 | bytes 1048576 | tf_op jit(solution)/shard_map/feed_backward/pallas_call | solution.py:72
  97.1 2.2 %collective-permute-done.5 = bf16[4,192,768]{2,1,0:T(8,128)(2,1)S(1)} collective-permute-done((bf16[4,192,768]{2,1,0:T(8,128)(2,1)S(1)}, bf16[4,192,768]{2,1,0:T(8,128)(2,1)S(1)}, u32[]{:S(2)}, u32[]{:S(2)}) %collective-permute-start.5) | collective-permute-done | bytes 1179680 | tf_op jit(solution)/shard_map/ppermute | solution.py:25
  99.6 1.7 collective-permute-start.7
  101.2 0.5 pause.2.refs_7_
  102.3 1.3 collective-permute-start.11
  103.5 11.6 %attention_backward.2 = (bf16[1024,1152]{1,0:T(8,128)(2,1)S(1)}, f32[8,384]{1,0:T(8,128)}, bf16[4,48,1920]{2,1,0:T(8,128)(2,1)}, bf16[4,48,1920]{2,1,0:T(8,128)(...) custom-call(s32[20]{0:T(128)S(1)} %concatenate.6.scalars_ref, bf16[1024,768]{1,0:T(8,128)(2,1)S(1)} %get-tuple-element.150.refs_0_, ...), custom_call_target="tpu_custom_call" | custom-call | flops 4000000000 | bytes 1048576 | tf_op jit(solution)/shard_map/attention_backward/pallas_call | solution.py:72
  115.3 2.7 %collective-permute-start.16 = (bf16[1,192,768]{2,1,0:T(8,128)(2,1)S(1)}, bf16[1,192,768]{2,1,0:T(8,128)(2,1)S(1)}, u32[]{:S(2)}, u32[]{:S(2)}) collective-permute-start(bf16[1,192,768]{2,1,0:T(8,128)(2,1)S(1)} %add_convert_fusion.8.refs_2_), channel_id=1, source_target_pairs={{0,8},{1,9},{2,10},{3,11},{4,12},{5,13},{6,14},{7,15},{8,0},{9,1},... | collective-permute-start | bytes 884744 | tf_op jit(solution)/shard_map/ppermute | solution.py:25
  118.0 0.5 collective-permute-start.15
  118.5 3.7 %scatter_home.2 = (bf16[16,64,768]{2,1,0:T(8,128)(2,1)}, f32[8,128]{1,0:T(8,128)}) custom-call(s32[20]{0:T(128)S(1)} %concatenate.6.scalars_ref, bf16[8,64,768]{2,1,0:T(8,128)(2,1)} %get-tuple-element.132.refs_0_, bf16[8,64,768]{2,1,0:T(8,128)(2,1)S(1)} %collective-permute-done.3.refs_1_, bf16[1,192,768]{2,1,0:T(8,128)(2,1)S(1)} %add_convert_fusion.8.refs_2_, ...), custom_call_target="tpu_custom_call" | custom-call | flops 20000000000 | bytes 1048576 | tf_op jit(solution)/shard_map/scatter_home/pallas_call | solution.py:72
  122.4 1.6 collective-permute-start.14
  124.0 16.2 %attention_backward.3 = (bf16[8,64,768]{2,1,0:T(8,128)(2,1)}, bf16[8,64,768]{2,1,0:T(8,128)(2,1)}, f32[8,384]{1,0:T(8,128)}, bf16[4,48,1280]{2,1,0:T(8,128)(2,1)...) custom-call(s32[20]{0:T(128)S(1)} %concatenate.6.scalars_ref, ...), custom_call_target="tpu_custom_call" | custom-call | flops 4000000000 | bytes 1048576 | tf_op jit(solution)/shard_map/attention_backward/pallas_call | solution.py:72
  141.3 0.8 collective-permute-start.10
  142.3 0.6 collective-permute-start.12
  142.9 1.2 collective-permute-start.18
  144.3 1.3 collective-permute-start.21
  145.7 11.6 %collective-permute-done.12 = bf16[4,48,1536]{2,1,0:T(8,128)(2,1)S(1)} collective-permute-done((bf16[4,48,1536]{2,1,0:T(8,128)(2,1)S(1)}, bf16[4,48,1536]{2,1,0:T(8,128)(2,1)S(1)}, u32[]{:S(2)}, u32[]{:S(2)}) %collective-permute-start.12) | collective-permute-done | bytes 589856 | tf_op jit(solution)/shard_map/ppermute | solution.py:25
  157.2 0.5 collective-permute-start.19
  157.9 0.5 pause.3.refs_3_
  158.5 1.6 collective-permute-start.17
  160.3 1.0 collective-permute-start.24
  161.2 7.8 %collective-permute-done.19 = bf16[4,48,1280]{2,1,0:T(8,128)(2,1)S(1)} collective-permute-done((bf16[4,48,1280]{2,1,0:T(8,128)(2,1)S(1)}, bf16[4,48,1280]{2,1,0:T(8,128)(2,1)S(1)}, u32[]{:S(2)}, u32[]{:S(2)}) %collective-permute-start.19) | collective-permute-done | bytes 491552 | tf_op jit(solution)/shard_map/ppermute | solution.py:25
  169.2 1.3 collective-permute-start.23
  170.5 1.0 collective-permute-start.22
  171.6 3.7 %scatter_home.3 = (bf16[16,64,768]{2,1,0:T(8,128)(2,1)}, f32[8,128]{1,0:T(8,128)}) custom-call(s32[20]{0:T(128)S(1)} %concatenate.6.scalars_ref, bf16[8,64,768]{2,1,0:T(8,128)(2,1)} %get-tuple-element.174.refs_0_, bf16[8,64,768]{2,1,0:T(8,128)(2,1)S(1)} %collective-permute-done.10.refs_1_, bf16[1,48,1536]{2,1,0:T(8,128)(2,1)S(1)} %add_convert_fusion.13.refs_2_, ...), custom_call_target="tpu_custom_call" | custom-call | flops 20000000000 | bytes 1048576 | tf_op jit(solution)/shard_map/scatter_home/pallas_call | solution.py:72
  175.4 1.3 collective-permute-start.26
  176.7 1.6 collective-permute-done.23
  179.0 0.9 collective-permute-start.25
  179.8 5.1 %collective-permute-done.27 = bf16[1,48,1280]{2,1,0:T(8,128)(2,1)S(1)} collective-permute-done((bf16[1,48,1280]{2,1,0:T(8,128)(2,1)S(1)}, bf16[1,48,1280]{2,1,0:T(8,128)(2,1)S(1)}, u32[]{:S(2)}, u32[]{:S(2)}) %collective-permute-start.27) | collective-permute-done | bytes 122912 | tf_op jit(solution)/shard_map/ppermute | solution.py:25
  185.0 0.9 collective-permute-start.28
  185.9 0.9 convert_add_fusion.1
  186.8 3.2 %collective-permute-done.28.refs_5_ = bf16[48,1280]{1,0:T(8,128)(2,1)S(1)} collective-permute-done((bf16[48,1280]{1,0:T(8,128)(2,1)S(1)}, bf16[48,1280]{1,0:T(8,128)(2,1)S(1)}, u32[]{:S(2)}, u32[]{:S(2)}) %collective-permute-start.28) | collective-permute-done | bytes 122912 | tf_op jit(solution)/shard_map/ppermute | solution.py:25
  190.0 1.6 finish.1
  (83 shorter events, 4.9 us)
Async XLA Ops:
  3.1 13.2 %collective-permute-start = (bf16[4,64,768]{2,1,0:T(8,128)(2,1)}, bf16[4,64,768]{2,1,0:T(8,128)(2,1)S(1)}, u32[]{:S(2)}, u32[]{:S(2)}) collective-permute-start(bf16[4,64,768]{2,1,0:T(8,128)(2,1)} %get-tuple-element.115), channel_id=1, source_target_pairs={{0,16},{16,0},{1,17},{17,1},{2,18},{18,2},{3,19},{19,3},{4,20},{20... | collective-permute-start | bytes 1179656 | tf_op jit(solution)/shard_map/ppermute | solution.py:25
  6.1 10.2 %copy-start.9 = (s32[2,1024]{1,0:T(2,128)S(1)}, s32[2,1024]{1,0:T(2,128)}, u32[]{:S(2)}) copy-start(s32[2,1024]{1,0:T(2,128)} %param.14) | copy-start | bytes 24580
  6.1 10.2 %copy-start.8 = (s32[1,16]{1,0:T(1,128)S(1)}, s32[1,16]{1,0:T(1,128)}, u32[]{:S(2)}) copy-start(s32[1,16]{1,0:T(1,128)} %param.15) | copy-start | bytes 196
  8.8 16.9 %collective-permute-start.1 = (bf16[4,64,768]{2,1,0:T(8,128)(2,1)}, bf16[4,64,768]{2,1,0:T(8,128)(2,1)S(1)}, u32[]{:S(2)}, u32[]{:S(2)}) collective-permute-start(bf16[4,64,768]{2,1,0:T(8,128)(2,1)} %get-tuple-element.121), channel_id=1, source_target_pairs={{0,16},{16,0},{1,17},{17,1},{2,18},{18,2},{3,19},{19,3},{4,20},{20... | collective-permute-start | bytes 1179656 | tf_op jit(solution)/shard_map/ppermute | solution.py:25
  16.3 8.7 %copy-start.14 = (bf16[4,64,768]{2,1,0:T(8,128)(2,1)}, bf16[4,64,768]{2,1,0:T(8,128)(2,1)S(1)}, u32[]{:S(2)}) copy-start(bf16[4,64,768]{2,1,0:T(8,128)(2,1)S(1)} %collective-permute-done.refs_2_) | copy-start | bytes 1179652
  16.6 24.7 %collective-permute-start.2 = (bf16[8,64,768]{2,1,0:T(8,128)(2,1)}, bf16[8,64,768]{2,1,0:T(8,128)(2,1)S(1)}, u32[]{:S(2)}, u32[]{:S(2)}) collective-permute-start(bf16[8,64,768]{2,1,0:T(8,128)(2,1)} %get-tuple-element.128), channel_id=1, source_target_pairs={{0,16},{16,0},{1,17},{17,1},{2,18},{18,2},{3,19},{19,3},{4,20},{20... | collective-permute-start | bytes 2359304 | tf_op jit(solution)/shard_map/ppermute | solution.py:25
  25.7 0.7 copy-start.15
  66.5 3.1 %collective-permute-start.4 = (bf16[1,4,192,768]{3,2,1,0:T(8,128)(2,1)}, bf16[1,4,192,768]{3,2,1,0:T(8,128)(2,1)S(1)}, u32[]{:S(2)}, u32[]{:S(2)}) collective-permute-start(bf16[1,4,192,768]{3,2,1,0:T(8,128)(2,1)} %get-tuple-element.135), channel_id=1, source_target_pairs={{0,1},{1,0},{2,3},{3,2},{4,5},{5,4},{6,7},{7,6},{8,9},{9,8},{10,11... | collective-permute-start | bytes 3538952 | tf_op jit(solution)/shard_map/ppermute | solution.py:25
  66.5 30.6 %collective-permute-start.6 = (bf16[1,4,192,768]{3,2,1,0:T(8,128)(2,1)}, bf16[1,4,192,768]{3,2,1,0:T(8,128)(2,1)S(1)}, u32[]{:S(2)}, u32[]{:S(2)}) collective-permute-start(bf16[1,4,192,768]{3,2,1,0:T(8,128)(2,1)} %get-tuple-element.138), channel_id=1, source_target_pairs={{0,1},{1,0},{2,3},{3,2},{4,5},{5,4},{6,7},{7,6},{8,9},{9,8},{10,11... | collective-permute-start | bytes 3538952 | tf_op jit(solution)/shard_map/ppermute | solution.py:25
  69.6 3.2 %copy-start.11 = (bf16[8,64,768]{2,1,0:T(8,128)(2,1)S(1)}, bf16[8,64,768]{2,1,0:T(8,128)(2,1)}, u32[]{:S(2)}) copy-start(bf16[8,64,768]{2,1,0:T(8,128)(2,1)} %get-tuple-element.133) | copy-start | bytes 2359300
  71.2 28.1 %collective-permute-start.5 = (bf16[4,192,768]{2,1,0:T(8,128)(2,1)S(1)}, bf16[4,192,768]{2,1,0:T(8,128)(2,1)S(1)}, u32[]{:S(2)}, u32[]{:S(2)}) collective-permute-start(bf16[4,192,768]{2,1,0:T(8,128)(2,1)S(1)} %fusion.refs_9_), channel_id=1, source_target_pairs={{0,2},{1,3},{2,0},{3,1},{4,6},{5,7},{6,4},{7,5},{8,10},{9,11},{10,... | collective-permute-start | bytes 3538952 | tf_op jit(solution)/shard_map/ppermute | solution.py:25
  72.8 28.4 %collective-permute-start.3 = (bf16[8,64,768]{2,1,0:T(8,128)(2,1)S(1)}, bf16[8,64,768]{2,1,0:T(8,128)(2,1)S(1)}, u32[]{:S(2)}, u32[]{:S(2)}) collective-permute-start(bf16[8,64,768]{2,1,0:T(8,128)(2,1)S(1)} %copy-done.11), channel_id=1, source_target_pairs={{0,16},{16,0},{1,17},{17,1},{2,18},{18,2},{3,19},{19,3},{4,20},{20... | collective-permute-start | bytes 2359304 | tf_op jit(solution)/shard_map/ppermute | solution.py:25
  74.0 25.3 %copy-start.1 = (bf16[2,4,192,768]{3,2,1,0:T(8,128)(2,1)S(1)}, bf16[2,4,192,768]{3,2,1,0:T(8,128)(2,1)}, u32[]{:S(2)}) copy-start(bf16[2,4,192,768]{3,2,1,0:T(8,128)(2,1)} %get-tuple-element.134) | copy-start | bytes 7077892
  97.1 4.7 %collective-permute-start.8 = (bf16[8,48,3072]{2,1,0:T(8,128)(2,1)}, bf16[8,48,3072]{2,1,0:T(8,128)(2,1)S(1)}, u32[]{:S(2)}, u32[]{:S(2)}) collective-permute-start(bf16[8,48,3072]{2,1,0:T(8,128)(2,1)} %get-tuple-element.156), channel_id=1, source_target_pairs={{0,1},{1,0},{2,3},{3,2},{4,5},{5,4},{6,7},{7,6},{8,9},{9,8},{10,11... | collective-permute-start | bytes 7077896 | tf_op jit(solution)/shard_map/ppermute | solution.py:25
  97.1 2.5 %copy-start.3 = (bf16[1,4,192,768]{3,2,1,0:T(8,128)(2,1)}, bf16[1,4,192,768]{3,2,1,0:T(8,128)(2,1)S(1)}, u32[]{:S(2)}) copy-start(bf16[1,4,192,768]{3,2,1,0:T(8,128)(2,1)S(1)} %collective-permute-done.6) | copy-start | bytes 3538948
  99.3 1.9 copy-start.5
  99.5 2.3 %copy-start = (bf16[8,48,3072]{2,1,0:T(8,128)(2,1)S(1)}, bf16[8,48,3072]{2,1,0:T(8,128)(2,1)}, u32[]{:S(2)}) copy-start(bf16[8,48,3072]{2,1,0:T(8,128)(2,1)} %get-tuple-element.155) | copy-start | bytes 7077892
  99.6 15.6 %collective-permute-start.7 = (bf16[2,192,768]{2,1,0:T(8,128)(2,1)S(1)}, bf16[2,192,768]{2,1,0:T(8,128)(2,1)S(1)}, u32[]{:S(2)}, u32[]{:S(2)}) collective-permute-start(bf16[2,192,768]{2,1,0:T(8,128)(2,1)S(1)} %add_convert_fusion.3), channel_id=1, source_target_pairs={{0,4},{1,5},{2,6},{3,7},{4,0},{5,1},{6,2},{7,3},{8,12},{9,13},{10,... | collective-permute-start | bytes 1769480 | tf_op jit(solution)/shard_map/ppermute | solution.py:25
  102.3 38.0 %collective-permute-start.11 = (bf16[8,48,1536]{2,1,0:T(8,128)(2,1)S(1)}, bf16[8,48,1536]{2,1,0:T(8,128)(2,1)S(1)}, u32[]{:S(2)}, u32[]{:S(2)}) collective-permute-start(bf16[8,48,1536]{2,1,0:T(8,128)(2,1)S(1)} %add_convert_fusion.refs_6_), channel_id=1, source_target_pairs={{0,16},{16,0},{1,17},{17,1},{2,18},{18,2},{3,19},{19,3},{4,20},{20... | collective-permute-start | bytes 3538952 | tf_op jit(solution)/shard_map/ppermute | solution.py:25
  103.5 11.6 %copy-start.4 = (bf16[1,4,192,768]{3,2,1,0:T(8,128)(2,1)S(1)}, bf16[1,4,192,768]{3,2,1,0:T(8,128)(2,1)}, u32[]{:S(2)}) copy-start(bf16[1,4,192,768]{3,2,1,0:T(8,128)(2,1)} %copy-done.3) | copy-start | bytes 3538948
  103.5 11.6 %copy-start.6 = (bf16[4,192,768]{2,1,0:T(8,128)(2,1)S(1)}, bf16[4,192,768]{2,1,0:T(8,128)(2,1)}, u32[]{:S(2)}) copy-start(bf16[4,192,768]{2,1,0:T(8,128)(2,1)} %copy-done.5) | copy-start | bytes 3538948
  115.1 2.9 %copy-start.13 = (bf16[4,48,1920]{2,1,0:T(8,128)(2,1)S(1)}, bf16[4,48,1920]{2,1,0:T(8,128)(2,1)}, u32[]{:S(2)}) copy-start(bf16[4,48,1920]{2,1,0:T(8,128)(2,1)} %get-tuple-element.170) | copy-start | bytes 2211844
  115.1 2.9 %copy-start.12 = (bf16[4,48,1920]{2,1,0:T(8,128)(2,1)S(1)}, bf16[4,48,1920]{2,1,0:T(8,128)(2,1)}, u32[]{:S(2)}) copy-start(bf16[4,48,1920]{2,1,0:T(8,128)(2,1)} %get-tuple-element.179) | copy-start | bytes 2211844
  115.3 25.7 %collective-permute-start.16 = (bf16[1,192,768]{2,1,0:T(8,128)(2,1)S(1)}, bf16[1,192,768]{2,1,0:T(8,128)(2,1)S(1)}, u32[]{:S(2)}, u32[]{:S(2)}) collective-permute-start(bf16[1,192,768]{2,1,0:T(8,128)(2,1)S(1)} %add_convert_fusion.8.refs_2_), channel_id=1, source_target_pairs={{0,8},{1,9},{2,10},{3,11},{4,12},{5,13},{6,14},{7,15},{8,0},{9,1},... | collective-permute-start | bytes 884744 | tf_op jit(solution)/shard_map/ppermute | solution.py:25
  118.0 4.2 %collective-permute-start.9 = (bf16[4,48,1920]{2,1,0:T(8,128)(2,1)S(1)}, bf16[4,48,1920]{2,1,0:T(8,128)(2,1)S(1)}, u32[]{:S(2)}, u32[]{:S(2)}) collective-permute-start(bf16[4,48,1920]{2,1,0:T(8,128)(2,1)S(1)} %copy-done.13), channel_id=1, source_target_pairs={{0,1},{1,0},{2,3},{3,2},{4,5},{5,4},{6,7},{7,6},{8,9},{9,8},{10,11... | collective-permute-start | bytes 2211848 | tf_op jit(solution)/shard_map/ppermute | solution.py:25
  118.0 24.3 %collective-permute-start.15 = (bf16[4,48,1920]{2,1,0:T(8,128)(2,1)S(1)}, bf16[4,48,1920]{2,1,0:T(8,128)(2,1)S(1)}, u32[]{:S(2)}, u32[]{:S(2)}) collective-permute-start(bf16[4,48,1920]{2,1,0:T(8,128)(2,1)S(1)} %copy-done.12), channel_id=1, source_target_pairs={{0,1},{1,0},{2,3},{3,2},{4,5},{5,4},{6,7},{7,6},{8,9},{9,8},{10,11... | collective-permute-start | bytes 2211848 | tf_op jit(solution)/shard_map/ppermute | solution.py:25
  118.5 3.7 %copy-start.2 = (bf16[8,48,1920]{2,1,0:T(8,128)(2,1)S(1)}, bf16[8,48,1920]{2,1,0:T(8,128)(2,1)}, u32[]{:S(2)}) copy-start(bf16[8,48,1920]{2,1,0:T(8,128)(2,1)} %get-tuple-element.169) | copy-start | bytes 4423684
  122.4 20.5 %collective-permute-start.14 = (bf16[4,48,1920]{2,1,0:T(8,128)(2,1)S(1)}, bf16[4,48,1920]{2,1,0:T(8,128)(2,1)S(1)}, u32[]{:S(2)}, u32[]{:S(2)}) collective-permute-start(bf16[4,48,1920]{2,1,0:T(8,128)(2,1)S(1)} %add_convert_fusion.1.refs_11_), channel_id=1, source_target_pairs={{0,2},{1,3},{2,0},{3,1},{4,6},{5,7},{6,4},{7,5},{8,10},{9,11},{10,... | collective-permute-start | bytes 2211848 | tf_op jit(solution)/shard_map/ppermute | solution.py:25
  140.2 1.1 copy-start.10
  140.2 4.1 %collective-permute-start.13 = (bf16[4,48,1280]{2,1,0:T(8,128)(2,1)}, bf16[4,48,1280]{2,1,0:T(8,128)(2,1)S(1)}, u32[]{:S(2)}, u32[]{:S(2)}) collective-permute-start(bf16[4,48,1280]{2,1,0:T(8,128)(2,1)} %get-tuple-element.178), channel_id=1, source_target_pairs={{0,1},{1,0},{2,3},{3,2},{4,5},{5,4},{6,7},{7,6},{8,9},{9,8},{10,11... | collective-permute-start | bytes 1474568 | tf_op jit(solution)/shard_map/ppermute | solution.py:25
  140.3 20.0 %collective-permute-start.20 = (bf16[4,48,1280]{2,1,0:T(8,128)(2,1)}, bf16[4,48,1280]{2,1,0:T(8,128)(2,1)S(1)}, u32[]{:S(2)}, u32[]{:S(2)}) collective-permute-start(bf16[4,48,1280]{2,1,0:T(8,128)(2,1)} %get-tuple-element.191), channel_id=1, source_target_pairs={{0,1},{1,0},{2,3},{3,2},{4,5},{5,4},{6,7},{7,6},{8,9},{9,8},{10,11... | collective-permute-start | bytes 1474568 | tf_op jit(solution)/shard_map/ppermute | solution.py:25
  141.3 4.2 %copy-start.7 = (bf16[8,48,1280]{2,1,0:T(8,128)(2,1)S(1)}, bf16[8,48,1280]{2,1,0:T(8,128)(2,1)}, u32[]{:S(2)}) copy-start(bf16[8,48,1280]{2,1,0:T(8,128)(2,1)} %get-tuple-element.188) | copy-start | bytes 2949124
  141.3 30.2 %collective-permute-start.10 = (bf16[8,64,768]{2,1,0:T(8,128)(2,1)S(1)}, bf16[8,64,768]{2,1,0:T(8,128)(2,1)S(1)}, u32[]{:S(2)}, u32[]{:S(2)}) collective-permute-start(bf16[8,64,768]{2,1,0:T(8,128)(2,1)S(1)} %copy-done.10), channel_id=1, source_target_pairs={{0,16},{16,0},{1,17},{17,1},{2,18},{18,2},{3,19},{19,3},{4,20},{20... | collective-permute-start | bytes 2359304 | tf_op jit(solution)/shard_map/ppermute | solution.py:25
  142.3 14.9 %collective-permute-start.12 = (bf16[4,48,1536]{2,1,0:T(8,128)(2,1)S(1)}, bf16[4,48,1536]{2,1,0:T(8,128)(2,1)S(1)}, u32[]{:S(2)}, u32[]{:S(2)}) collective-permute-start(bf16[4,48,1536]{2,1,0:T(8,128)(2,1)S(1)} %add_convert_fusion.2), channel_id=1, source_target_pairs={{0,2},{1,3},{2,0},{3,1},{4,6},{5,7},{6,4},{7,5},{8,10},{9,11},{10,... | collective-permute-start | bytes 1769480 | tf_op jit(solution)/shard_map/ppermute | solution.py:25
  142.9 27.5 %collective-permute-start.18 = (bf16[192,768]{1,0:T(8,128)(2,1)S(1)}, bf16[192,768]{1,0:T(8,128)(2,1)S(1)}, u32[]{:S(2)}, u32[]{:S(2)}) collective-permute-start(bf16[192,768]{1,0:T(8,128)(2,1)S(1)} %bitcast.43), channel_id=1, source_target_pairs={{0,16},{16,0},{1,17},{17,1},{2,18},{18,2},{3,19},{19,3},{4,20},{20... | collective-permute-start | bytes 884744 | tf_op jit(solution)/shard_map/ppermute | solution.py:25
  144.3 14.2 %collective-permute-start.21 = (bf16[2,48,1920]{2,1,0:T(8,128)(2,1)S(1)}, bf16[2,48,1920]{2,1,0:T(8,128)(2,1)S(1)}, u32[]{:S(2)}, u32[]{:S(2)}) collective-permute-start(bf16[2,48,1920]{2,1,0:T(8,128)(2,1)S(1)} %add_convert_fusion.5), channel_id=1, source_target_pairs={{0,4},{1,5},{2,6},{3,7},{4,0},{5,1},{6,2},{7,3},{8,12},{9,13},{10,... | collective-permute-start | bytes 1105928 | tf_op jit(solution)/shard_map/ppermute | solution.py:25
  157.2 11.8 %collective-permute-start.19 = (bf16[4,48,1280]{2,1,0:T(8,128)(2,1)S(1)}, bf16[4,48,1280]{2,1,0:T(8,128)(2,1)S(1)}, u32[]{:S(2)}, u32[]{:S(2)}) collective-permute-start(bf16[4,48,1280]{2,1,0:T(8,128)(2,1)S(1)} %add_convert_fusion.4), channel_id=1, source_target_pairs={{0,2},{1,3},{2,0},{3,1},{4,6},{5,7},{6,4},{7,5},{8,10},{9,11},{10,... | collective-permute-start | bytes 1474568 | tf_op jit(solution)/shard_map/ppermute | solution.py:25
  158.5 11.9 %collective-permute-start.17 = (bf16[2,48,1536]{2,1,0:T(8,128)(2,1)S(1)}, bf16[2,48,1536]{2,1,0:T(8,128)(2,1)S(1)}, u32[]{:S(2)}, u32[]{:S(2)}) collective-permute-start(bf16[2,48,1536]{2,1,0:T(8,128)(2,1)S(1)} %add_convert_fusion.6.refs_0_), channel_id=1, source_target_pairs={{0,4},{1,5},{2,6},{3,7},{4,0},{5,1},{6,2},{7,3},{8,12},{9,13},{10,... | collective-permute-start | bytes 884744 | tf_op jit(solution)/shard_map/ppermute | solution.py:25
  160.3 15.0 %collective-permute-start.24 = (bf16[1,48,1920]{2,1,0:T(8,128)(2,1)S(1)}, bf16[1,48,1920]{2,1,0:T(8,128)(2,1)S(1)}, u32[]{:S(2)}, u32[]{:S(2)}) collective-permute-start(bf16[1,48,1920]{2,1,0:T(8,128)(2,1)S(1)} %add_convert_fusion.11), channel_id=1, source_target_pairs={{0,8},{1,9},{2,10},{3,11},{4,12},{5,13},{6,14},{7,15},{8,0},{9,1},... | collective-permute-start | bytes 552968 | tf_op jit(solution)/shard_map/ppermute | solution.py:25
  169.2 9.1 %collective-permute-start.23 = (bf16[2,48,1280]{2,1,0:T(8,128)(2,1)S(1)}, bf16[2,48,1280]{2,1,0:T(8,128)(2,1)S(1)}, u32[]{:S(2)}, u32[]{:S(2)}) collective-permute-start(bf16[2,48,1280]{2,1,0:T(8,128)(2,1)S(1)} %add_convert_fusion.9), channel_id=1, source_target_pairs={{0,4},{1,5},{2,6},{3,7},{4,0},{5,1},{6,2},{7,3},{8,12},{9,13},{10,... | collective-permute-start | bytes 737288 | tf_op jit(solution)/shard_map/ppermute | solution.py:25
  170.5 8.3 %collective-permute-start.22 = (bf16[1,48,1536]{2,1,0:T(8,128)(2,1)S(1)}, bf16[1,48,1536]{2,1,0:T(8,128)(2,1)S(1)}, u32[]{:S(2)}, u32[]{:S(2)}) collective-permute-start(bf16[1,48,1536]{2,1,0:T(8,128)(2,1)S(1)} %add_convert_fusion.13.refs_2_), channel_id=1, source_target_pairs={{0,8},{1,9},{2,10},{3,11},{4,12},{5,13},{6,14},{7,15},{8,0},{9,1},... | collective-permute-start | bytes 442376 | tf_op jit(solution)/shard_map/ppermute | solution.py:25
  175.4 11.4 %collective-permute-start.26 = (bf16[48,1920]{1,0:T(8,128)(2,1)S(1)}, bf16[48,1920]{1,0:T(8,128)(2,1)S(1)}, u32[]{:S(2)}, u32[]{:S(2)}) collective-permute-start(bf16[48,1920]{1,0:T(8,128)(2,1)S(1)} %bitcast.26), channel_id=1, source_target_pairs={{0,16},{16,0},{1,17},{17,1},{2,18},{18,2},{3,19},{19,3},{4,20},{20... | collective-permute-start | bytes 552968 | tf_op jit(solution)/shard_map/ppermute | solution.py:25
  178.4 6.6 %collective-permute-start.27 = (bf16[1,48,1280]{2,1,0:T(8,128)(2,1)S(1)}, bf16[1,48,1280]{2,1,0:T(8,128)(2,1)S(1)}, u32[]{:S(2)}, u32[]{:S(2)}) collective-permute-start(bf16[1,48,1280]{2,1,0:T(8,128)(2,1)S(1)} %add_convert_fusion.15), channel_id=1, source_target_pairs={{0,8},{1,9},{2,10},{3,11},{4,12},{5,13},{6,14},{7,15},{8,0},{9,1},... | collective-permute-start | bytes 368648 | tf_op jit(solution)/shard_map/ppermute | solution.py:25
  179.0 7.9 %collective-permute-start.25 = (bf16[48,1536]{1,0:T(8,128)(2,1)S(1)}, bf16[48,1536]{1,0:T(8,128)(2,1)S(1)}, u32[]{:S(2)}, u32[]{:S(2)}) collective-permute-start(bf16[48,1536]{1,0:T(8,128)(2,1)S(1)} %bitcast.28), channel_id=1, source_target_pairs={{0,16},{16,0},{1,17},{17,1},{2,18},{18,2},{3,19},{19,3},{4,20},{20... | collective-permute-start | bytes 442376 | tf_op jit(solution)/shard_map/ppermute | solution.py:25
  185.0 4.9 %collective-permute-start.28 = (bf16[48,1280]{1,0:T(8,128)(2,1)S(1)}, bf16[48,1280]{1,0:T(8,128)(2,1)S(1)}, u32[]{:S(2)}, u32[]{:S(2)}) collective-permute-start(bf16[48,1280]{1,0:T(8,128)(2,1)S(1)} %bitcast.30), channel_id=1, source_target_pairs={{0,16},{16,0},{1,17},{17,1},{2,18},{18,2},{3,19},{19,3},{4,20},{20... | collective-permute-start | bytes 368648 | tf_op jit(solution)/shard_map/ppermute | solution.py:25
